TPU v7x, 128 devices: a whole 4x4x4 slice. The times are simulated.
128 devices in a mesh: dp: 32 (over z, x, core), tp: 4 (over y).
Axes of the slice: x: 4, y: 4, z: 4, core: 2. Of those that a mesh axis runs over, the one named last changes fastest.
Arguments:
- activations: bfloat16 [16384, 8192], P(('dp', 'tp')), may hold values from -6 to 6
- value_grad: bfloat16 [16384, 1024], P('dp', 'tp'), may hold values from -6 to 6
- value_weight: bfloat16 [8192, 1024], P(None, 'tp'), may hold values from -0.1875 to 0.1875
- error_prev: float32 [32, 8192, 1024], P('dp', None, 'tp'), may hold values from -96 to 96
- right_prev: float32 [1024, 32], P('tp'), may hold values from -6 to 6
Outputs:
- grad_input: bfloat16 [16384, 8192], P(('dp', 'tp'))
- error_next: float32 [32, 8192, 1024], P('dp', None, 'tp')
- left_factor: float32 [8192, 32], replicated
- right_factor: float32 [1024, 32], P('tp')
All inputs are finite; a program needn't handle non-finite values.
Results may differ from a plain program's by a relative error of at most 0.019.
Values may be sent and summed in bfloat16 or wider, within the bound.
A program may use at most 128 MiB of HBM per device.

v0:
```python
import math

import jax
import jax.numpy as jnp
from jax import lax
from jax.sharding import PartitionSpec as P


def orthonormal(factor):
    highest = lax.Precision.HIGHEST
    columns = []
    for number in range(factor.shape[1]):
        vector = factor[:, number]
        if columns:
            spanned = jnp.stack(columns, axis=1)
            for sweep in range(2):
                weights = jnp.dot(vector, spanned, precision=highest)
                vector = vector - jnp.dot(spanned, weights, precision=highest)
        vector = vector / jnp.sqrt(jnp.sum(vector * vector) + 1e-12)
        columns.append(vector)
    return jnp.stack(columns, axis=1)


def body(activations, value_grad, value_weight, error_prev, right_prev):
    highest = lax.Precision.HIGHEST
    cotangent = value_grad
    grad = lax.dot_general(
        lax.all_gather(activations, "tp", axis=0, tiled=True),
        cotangent,
        (((0,), (0,)), ((), ())),
        preferred_element_type=jnp.float32,
    )
    merged = grad + error_prev[0]
    local_left = jnp.dot(merged, right_prev, precision=highest)
    left_sum = lax.psum(local_left, ("dp", "tp"))
    cotangent = value_grad
    grad_input = lax.psum_scatter(
        lax.dot_general(
            cotangent, value_weight, (((1,), (1,)), ((), ())), preferred_element_type=jnp.float32
        ).astype(jnp.bfloat16),
        "tp",
        scatter_dimension=0,
        tiled=True,
    )
    ortho = orthonormal(left_sum)
    local_right = lax.dot_general(merged, ortho, (((0,), (0,)), ((), ())), precision=highest)
    right_factor = lax.psum(local_right.astype(jnp.bfloat16), "dp").astype(jnp.float32) / float(
        lax.axis_size("dp")
    )
    error_next = merged - jnp.dot(ortho, right_factor.T, precision=highest)
    left_factor = ortho * math.sqrt(float(ortho.shape[0]))
    return (grad_input, error_next[None], left_factor, right_factor)


def solution(mesh):
    return jax.shard_map(
        body,
        mesh=mesh,
        in_specs=(
            P(("dp", "tp"), None),
            P("dp", "tp"),
            P(None, "tp"),
            P("dp", None, "tp"),
            P("tp", None),
        ),
        out_specs=(P(("dp", "tp"), None), P("dp", None, "tp"), P(), P("tp", None)),
        check_vma=False,
    )
```

profile of v0, /device:TPU:1, one launch (start us, length us, event | category | flops | bytes accessed | tf_op | source)
XLA Modules:
  0.0 575.5 jit_solution(5367285072795056821)
XLA Ops:
  8.0 88.1 %all-gather.2.cloned.1.call-done = bf16[512,8192]{1,0:T(8,128)(2,1)} async-done(((bf16[128,8192]{1,0:T(8,128)(2,1)}), bf16[512,8192]{1,0:T(8,128)(2,1)}) %all-gather.2.cloned.1.call-update) | async-done | bytes 8388624 | tf_op jit(solution)/shard_map/all_gather | solution.py:28
  96.0 8.1 %convolution_add_fusion = f32[8192,256]{1,0:T(8,128)S(1)} fusion(bf16[512,8192]{1,0:T(8,128)(2,1)} %all-gather.2.cloned.1.call-done, bf16[512,256]{1,0:T(8,128)(2,1)S(1)} %copy-done, f32[1,8192,256]{2,1,0:T(8,128)} %param.8), kind=kOutput, calls=%fused_computation.3 | convolution fusion | flops 2149580800 | bytes 25427968 | tf_op jit(solution)/shard_map/dot_general | solution.py:27
  104.2 3.4 copy-done.2
  107.6 8.7 %fusion.34 = f32[8192,32]{0,1:T(8,128)} fusion(f32[8192,256]{1,0:T(8,128)S(1)} %convolution_add_fusion, f32[256,32]{0,1:T(8,128)S(1)} %copy-done.5), kind=kOutput, calls=%fused_computation.171 | convolution fusion | flops 805306368 | bytes 9469952 | tf_op jit(solution)/shard_map/dot_general | solution.py:34
  116.9 7.8 %convolution_convert_fusion = bf16[512,8192]{1,0:T(8,128)(2,1)} fusion(bf16[512,256]{1,0:T(8,128)(2,1)S(1)} %copy-done, bf16[8192,256]{1,0:T(8,128)(2,1)} %param.7), kind=kOutput, calls=%fused_computation | convolution fusion | flops 2151677952 | bytes 12845056 | tf_op jit(solution)/shard_map/dot_general | solution.py:38
  124.7 140.1 %all-reduce.2.cloned.1.call-done = f32[8192,32]{0,1:T(8,128)} async-done(((f32[8192,32]{0,1:T(8,128)}), f32[8192,32]{0,1:T(8,128)}) %all-reduce.2.cloned.1.call-update) | async-done | bytes 1048592 | tf_op jit(solution)/shard_map/psum | solution.py:35
  264.8 3.8 fusion.33
  269.3 3.8 fusion.32
  273.7 1.3 multiply_reduce_fusion
  275.0 2.0 multiply_reduce_fusion.32
  277.6 1.3 broadcast_divide_fusion.30
  282.5 1.6 convolution_bitcast_fusion.57
  287.1 1.6 convolution_bitcast_fusion.55
  291.7 1.6 convolution_bitcast_fusion.53
  321.9 0.9 convolution_bitcast_fusion.38
  343.5 1.0 fusion.63
  352.3 0.9 stack.159
  357.3 1.0 stack.161
  362.4 1.2 stack.163
  367.7 1.1 stack.165
  372.9 1.1 stack.167
  378.1 1.2 stack.169
  383.6 1.2 stack.171
  384.8 0.9 convolution_bitcast_fusion.13
  386.4 0.9 convolution_bitcast_fusion.12
  389.4 1.3 stack.173
  390.7 0.9 convolution_bitcast_fusion.11
  392.3 0.9 convolution_bitcast_fusion.10
  395.3 1.3 stack.175
  396.6 1.3 convolution_bitcast_fusion.9
  398.7 0.9 convolution_bitcast_fusion.8
  401.6 1.4 stack.177
  403.0 0.9 convolution_bitcast_fusion.7
  404.7 0.9 convolution_bitcast_fusion.6
  407.6 1.4 stack.179
  409.0 0.9 convolution_bitcast_fusion.5
  410.7 0.9 convolution_bitcast_fusion.4
  413.7 1.6 stack.181
  415.3 0.9 convolution_bitcast_fusion.3
  417.0 0.9 convolution_bitcast_fusion.2
  419.9 1.5 stack.183
  421.4 0.9 convolution_bitcast_fusion.1
  423.1 0.9 convolution_bitcast_fusion
  426.0 1.5 stack.185
  427.6 7.0 %convolution_convert_fusion.1 = bf16[256,32]{0,1:T(8,128)(2,1)S(1)} fusion(f32[8192,256]{1,0:T(8,128)} %copy-done.2, f32[8192,32]{0,1:T(8,128)S(1)} %stack.185), kind=kOutput, calls=%fused_computation.4 | convolution fusion | flops 805314560 | bytes 9453568 | tf_op jit(solution)/shard_map/dot_general | solution.py:46
  434.6 121.9 %psum.15 = bf16[256,32]{0,1:T(8,128)(2,1)S(1)} all-reduce(bf16[256,32]{0,1:T(8,128)(2,1)S(1)} %convolution_convert_fusion.1), channel_id=1, replica_groups=mesh['dp'=32,'tp'=4] {'dp'}, use_global_device_ids=true, to_apply=%region_34.0 | all-reduce | flops 8192 | bytes 32768 | tf_op jit(solution)/shard_map/psum | solution.py:47
  556.5 11.2 %fusion = f32[1,8192,256]{2,1,0:T(8,128)} fusion(f32[8192,256]{1,0:T(8,128)} %copy-done.2, f32[8192,32]{0,1:T(8,128)S(1)} %stack.185, f32[256,32]{0,1:T(8,128)S(1)} %convert_multiply_fusion), kind=kOutput, calls=%fused_computation.2 | convolution fusion | flops 807403520 | bytes 17858560 | tf_op jit(solution)/shard_map/dot_general | solution.py:50
  567.7 1.1 broadcast_multiply_fusion
  (227 shorter events, 91.2 us)
Async XLA Ops:
  7.2 88.9 %copy-start = (bf16[512,256]{1,0:T(8,128)(2,1)S(1)}, bf16[512,256]{1,0:T(8,128)(2,1)}, u32[]{:S(2)}) copy-start(bf16[512,256]{1,0:T(8,128)(2,1)} %param.6) | copy-start | bytes 786436
  7.2 88.9 %all-gather.2.cloned.1.call-start = ((), (), s32[]{:S(2)}) async-start(), calls=%async_computation.2 | async-start | bytes 10485760 | tf_op jit(solution)/shard_map/all_gather | solution.py:28
  7.9 99.7 %copy-start.5 = (f32[256,32]{0,1:T(8,128)S(1)}, f32[256,32]{0,1:T(8,128)}, u32[]{:S(2)}) copy-start(f32[256,32]{0,1:T(8,128)} %param.9) | copy-start | bytes 98308
  7.9 256.9 %all-reduce.2.cloned.1.call-start = ((), (), s32[]{:S(2)}) async-start(), calls=%async_computation.3 | async-start | bytes 2097152 | tf_op jit(solution)/shard_map/psum | solution.py:35
  104.2 3.4 copy-start.2
  116.4 452.4 %reduce-scatter.2.cloned.1.call-start = ((), (), s32[]{:S(2)}) async-start(), calls=%async_computation.1 | async-start | bytes 10485760 | tf_op jit(solution)/shard_map/reduce_scatter | solution.py:37
  264.8 31.6 %copy-start.3 = (f32[8192,32]{0,1:T(8,128)S(1)}, f32[8192,32]{0,1:T(8,128)}, u32[]{:S(2)}) copy-start(f32[8192,32]{0,1:T(8,128)} %all-reduce.2.cloned.1.call-done) | copy-start | bytes 3145732
  556.5 12.3 %copy-start.1 = (bf16[512,256]{1,0:T(8,128)(2,1)S(1)}, bf16[512,256]{1,0:T(8,128)(2,1)}, u32[]{:S(2)}) copy-start(bf16[512,256]{1,0:T(8,128)(2,1)} %param.6) | copy-start | bytes 786436
  556.5 11.2 %copy-start.4 = (f32[256,32]{0,1:T(8,128)}, f32[256,32]{0,1:T(8,128)S(1)}, u32[]{:S(2)}) copy-start(f32[256,32]{0,1:T(8,128)S(1)} %convert_multiply_fusion) | copy-start | bytes 98308
Sparse Core Ops, SparseCore 0:
  9.7 86.3 all-gather.1
  116.5 148.2 all-reduce.1
  268.0 79.1 reduce-scatter.1
where the time goes:
time: 587 us; the launch traced here: 576 us
  waiting for transfers between devices  229 us (39%)
  matrix products  125 us (21%)
  blocking collectives  122 us (21%)
  between operations  37.4 us (6%)
  other arithmetic  32.6 us (6%)
  local copies, waits for them, and re-layouts  29 us (5%)
    psum x1, waiting for transfers between devices, body(): left_sum = lax.psum(local_left, ('dp', 'tp'))  140 us
    psum x1, blocking collectives, body(): lax.psum(local_right.astype(jnp.bfloat16), 'dp').astype(jnp.float32)  122 us
    all_gather x1, waiting for transfers between devices, body(): lax.all_gather(activations, 'tp', axis=0, tiled=True)  88.1 us
    dot_general x60, matrix products, orthonormal(): weights = jnp.dot(vector, spanned, precision=highest)  50 us
    dot_general x60, matrix products, orthonormal(): vector = vector - jnp.dot(spanned, weights, precision=highest)  32.3 us
    another operation x27, local copies, waits for them, and re-layouts, orthonormal(): spanned = jnp.stack(columns, axis=1)  24 us
    reduce_sum x31, other arithmetic, orthonormal(): vector = vector / jnp.sqrt(jnp.sum(vector * vector) + 1e-12)  20.2 us
  transfers between devices with their start and end apart: 3, of which 2 were waited for; matrix products, arithmetic and copies ran while one was open for 29% of the time, Pallas kernels for 0%

commit v1 on v0

v1 whole, which is shorter than its diff:
```python
import functools
import math

import jax
import jax.numpy as jnp
from jax import lax
from jax.experimental import pallas as pl
from jax.experimental.pallas import tpu as pltpu
from jax.sharding import PartitionSpec as P

MESH = pl.DeviceIdType.MESH
HIGHEST = lax.Precision.HIGHEST
F32 = jnp.float32
BF16 = jnp.bfloat16
BLK = 256
EPS = 1e-12
NN = (((1,), (0,)), ((), ()))
NT = (((1,), (1,)), ((), ()))
TN = (((0,), (0,)), ((), ()))
CHUNKS = 4


def mm(a, b, dims=NN, precision=None):
    return lax.dot_general(a, b, dims, precision=precision, preferred_element_type=F32)


def split2(a):
    hi = a.astype(BF16)
    lo = (a - hi.astype(F32)).astype(BF16)
    return hi, lo


def split3(a):
    hi = a.astype(BF16)
    rest = a - hi.astype(F32)
    mid = rest.astype(BF16)
    lo = (rest - mid.astype(F32)).astype(BF16)
    return hi, mid, lo


def rows3(a):
    return jnp.concatenate(split3(a), axis=0)


def fold3(a):
    n = a.shape[0] // 3
    return (a[2 * n :] + a[n : 2 * n]) + a[:n]


def gram_schmidt(gram):
    n = gram.shape[0]
    row_id = lax.broadcasted_iota(jnp.int32, (n, 1), 0)
    eye = (lax.broadcasted_iota(jnp.int32, (n, n), 0) == lax.broadcasted_iota(jnp.int32, (n, n), 1)).astype(F32)
    left, weights = gram, eye
    for j in range(n):
        s = jnp.maximum(left[j : j + 1, j : j + 1], 0.0)
        inverse = 1.0 / (s + EPS)
        c = (2.0 - s * inverse) * inverse
        f = jnp.where(row_id > j, left[:, j : j + 1] * c, 0.0)
        new_weights = weights - f * weights[j : j + 1, :]
        left = left - (f * (2.0 - c * s)) * left[j : j + 1, :]
        weights = new_weights
    s = jnp.maximum(jnp.sum(left * eye, axis=1, keepdims=True), 0.0)
    return weights / jnp.sqrt(s + EPS), eye * (s / (s + EPS))


def comm_kernel(
    geom, act, vg, w, err, rt, actfull, q_out, r_out, gi,
    act_v, vg_v, err_v, rtf, vgx, wbuf, outs, lacc, lf, rc, rx, rz, ry, q1, ptf, rs0, rs1, rr_c, rr_x, rr_z,
    local_sem, send_sem, recv_sem,
):
    nz, nx, nc, ny = geom
    nb = nc * nx * nz
    tok, d = act_v.shape
    r = rt.shape[0]
    rq = r // ny
    dp, y = lax.axis_index("dp"), lax.axis_index("tp")
    c = lax.rem(dp, nc)
    x = lax.rem(lax.div(dp, nc), nx)
    z = lax.div(dp, nc * nx)
    k = c * nx + x

    def shifted(i, by, n):
        return lax.rem(i + by, n)

    def device(zz, xx, cc, yy):
        return ((zz * nx + xx) * nc + cc, yy)

    y_peers = [(dy, shifted(y, dy, ny)) for dy in range(1, ny)]
    z_peers = [(dz, shifted(z, dz, nz)) for dz in range(1, nz)]
    x_peers = [(dx, shifted(x, dx, nx)) for dx in range(1, nx)]
    group = [
        (shifted(x, dx, nx), shifted(c, dc, nc)) for dc in range(nc) for dx in range(nx) if (dc, dx) != (0, 0)
    ]

    sent = []
    counter = [0, 0]

    def send(src, dst, to):
        i = counter[0]
        counter[0] += 1
        copy = pltpu.make_async_remote_copy(
            src_ref=src, dst_ref=dst, send_sem=send_sem.at[i], recv_sem=recv_sem.at[i], device_id=to, device_id_type=MESH
        )
        copy.start()
        sent.append(copy)
        return copy

    def fetch(src, dst):
        i = counter[1]
        counter[1] += 1
        copy = pltpu.make_async_copy(src, dst, local_sem.at[i])
        copy.start()
        return copy

    def wait_all(copies):
        for copy in copies:
            copy.wait_recv()

    load_vgx = fetch(vg.at[pl.ds(pl.multiple_of(y * tok, tok), tok)], vgx.at[k, y])
    quarter = d // nc
    load_err = [fetch(err.at[pl.ds(i * quarter, quarter)], err_v.at[pl.ds(i * quarter, quarter)]) for i in range(nc)]
    load_act = fetch(act, act_v)
    load_vg = fetch(vg, vg_v)
    load_w = [
        fetch(w.at[pl.ds(pl.multiple_of((k * nz + zz) * BLK, BLK), BLK)], wbuf.at[zz, y]) for zz in range(nz)
    ]
    keep_act = fetch(act, actfull.at[y])

    barrier = pltpu.get_barrier_semaphore()
    everyone = (
        [device(z, xx, cc, y) for xx, cc in group]
        + [device(zz, x, c, y) for _, zz in z_peers]
        + [device(z, x, c, yy) for _, yy in y_peers]
    )
    for peer in everyone:
        pl.semaphore_signal(barrier, inc=1, device_id=peer, device_id_type=MESH)
    pl.semaphore_wait(barrier, len(everyone))

    recv_rt = [send(rt, rtf.at[y], device(z, x, c, yy)) for _, yy in y_peers]
    recv_vg = [
        send(vg.at[pl.ds(pl.multiple_of(yy * tok, tok), tok)], vgx.at[k, y], device(z, x, c, yy)) for _, yy in y_peers
    ]
    recv_w = [
        send(w.at[pl.ds(pl.multiple_of((k * nz + z) * BLK, BLK), BLK)], wbuf.at[z, y], device(z, x, c, yy))
        for _, yy in y_peers
    ]
    up, down = shifted(y, 1, ny), shifted(y, ny - 1, ny)
    part = tok // CHUNKS
    half = CHUNKS // 2

    def rows(i):
        return pl.ds(i * part, part)

    from_down, from_up = {}, {}
    for i in range(CHUNKS):
        j = (i + half) % CHUNKS
        from_down[i] = send(act.at[rows(i)], actfull.at[y, rows(i)], device(z, x, c, up))
        from_up[j] = send(act.at[rows(j)], actfull.at[y, rows(j)], device(z, x, c, down))

    passed = []

    def forward(i):
        from_down[i].wait_recv()
        passed.append(send(actfull.at[down, rows(i)], actfull.at[down, rows(i)], device(z, x, c, up)))
        j = i + half
        from_up[j].wait_recv()
        passed.append(send(actfull.at[up, rows(j)], actfull.at[up, rows(j)], device(z, x, c, down)))

    rtf[y] = rt[...]
    rt3 = rows3(rt[...])
    per = nx * nz

    def columns(b):
        return pl.ds(pl.multiple_of(b * BLK, BLK), BLK)

    for cc in range(nc):
        load_err[cc].wait()

        def err_left(j, carry, cc=cc):
            hi, lo = split2(err_v[columns(cc * per + j), :])
            lacc[cc, j] = fold3(mm(rt3, lo, NT)) + fold3(mm(rt3, hi, NT))
            return carry

        lax.fori_loop(0, per, err_left, 0)

    wait_all(recv_rt)
    load_vgx.wait()
    wait_all(recv_vg)
    recv_vgx = [send(vgx.at[k], vgx.at[k], device(z, xx, cc, y)) for xx, cc in group]
    ut = jnp.zeros((r, tok), F32)
    for yy in range(ny):
        ut = ut + fold3(mm(rows3(rtf[yy]), vgx[k, yy], NT))
    ut3 = rows3(ut)
    load_act.wait()

    def act_left(cc):
        def step(j, carry):
            lacc[cc, j] += fold3(mm(ut3, act_v[:, columns(cc * per + j)]))
            return carry

        lax.fori_loop(0, per, step, 0)

    recv_c = []
    for dc in range(1, nc):
        cc = shifted(c, dc, nc)
        act_left(cc)
        recv_c.append(send(lacc.at[cc], rc, device(z, x, cc, y)))
    act_left(c)

    for copy in load_w:
        copy.wait()
    recv_wz = []
    for copy, (dy, _) in zip(recv_w, y_peers):
        copy.wait_recv()
        source = shifted(y, ny - dy, ny)
        for _, zz in z_peers:
            recv_wz.append(send(wbuf.at[z, source], wbuf.at[z, source], device(zz, x, c, y)))

    wait_all(recv_c)
    lacc[c] += rc[...]
    recv = [
        send(lacc.at[c, pl.ds(xx * nz, nz)], rx.at[dx - 1], device(z, xx, c, y)) for dx, xx in x_peers
    ]
    wait_all(recv)
    own_x = pl.ds(x * nz, nz)
    total = lacc[c, own_x]
    for dx in range(nx - 1):
        total = total + rx[dx]
    lacc[c, own_x] = total
    mine = x * nz + z
    recv = [send(lacc.at[c, x * nz + zz], rz.at[dz - 1], device(zz, x, c, y)) for dz, zz in z_peers]
    wait_all(recv)
    total = lacc[c, mine]
    for dz in range(nz - 1):
        total = total + rz[dz]
    lacc[c, mine] = total

    def strip(yy):
        return pl.ds(pl.multiple_of(yy * rq, rq), rq)

    recv = [send(lacc.at[c, mine, strip(yy)], ry.at[dy - 1], device(z, x, c, yy)) for dy, yy in y_peers]

    sent_out, kept_out = [], []

    def input_grad(i):
        xx, cc = ([(x, c)] + group)[i]
        slot = cc * nx + xx
        for zz in range(nz):
            total = None
            for yy in range(ny):
                piece = mm(vgx[slot, yy], wbuf[zz, yy], NT).astype(BF16).astype(F32)
                total = piece if total is None else total + piece
            outs[i, :, zz * BLK : (zz + 1) * BLK] = total.astype(BF16)
        place = gi.at[:, pl.ds(pl.multiple_of(k * nz * BLK, BLK), nz * BLK)]
        if i == 0:
            kept_out.append(fetch(outs.at[i], place))
        else:
            sent_out.append(send(outs.at[i], place, device(z, xx, cc, y)))

    wait_all(recv_wz)
    wait_all(recv_vgx)
    jobs = list(range(nc * nx))

    def some_jobs(n):
        for _ in range(min(n, len(jobs))):
            input_grad(jobs.pop())

    some_jobs(2)
    wait_all(recv)
    total = lacc[c, mine, strip(y)]
    for dy in range(ny - 1):
        total = total + ry[dy]
    lf[c, mine, strip(y)] = total

    own = lf.at[c, mine, strip(y)]
    recv = [send(own, own, device(z, x, c, yy)) for _, yy in y_peers]
    some_jobs(2)
    forward(0)
    wait_all(recv)
    own = lf.at[c, mine]
    recv = [send(own, own, device(zz, x, c, y)) for _, zz in z_peers]
    some_jobs(2)
    wait_all(recv)
    own = lf.at[c, own_x]
    recv = [send(own, own, device(z, xx, c, y)) for _, xx in x_peers]
    some_jobs(2)
    wait_all(recv)
    own = lf.at[c]
    recv = [send(own, own, device(z, x, shifted(c, dc, nc), y)) for dc in range(1, nc)]
    some_jobs(len(jobs))
    for i in range(1, half):
        forward(i)
    wait_all(recv)

    def gram_of(ref_of):
        def step(b, total):
            block = ref_of(b)
            return total + mm(block, block, NT, HIGHEST)

        return lax.fori_loop(0, nb, step, jnp.zeros((r, r), F32))

    def left_block(b):
        return lf[lax.div(b, per), lax.rem(b, per)]

    weights, norms = gram_schmidt(gram_of(left_block))

    def apply_first(b, total):
        block = mm(weights, left_block(b), NN, HIGHEST)
        q1[b] = block
        return total + mm(block, block, NT, HIGHEST)

    off = lax.fori_loop(0, nb, apply_first, jnp.zeros((r, r), F32)) - norms
    row_id = lax.broadcasted_iota(jnp.int32, (r, r), 0)
    col_id = lax.broadcasted_iota(jnp.int32, (r, r), 1)
    again = jnp.where(col_id < row_id, off, jnp.where(col_id == row_id, 0.5 * off, 0.0))

    def apply_second(b, total):
        block = q1[b]
        block = block - mm(again, block, NN, HIGHEST)
        q_out[b] = block
        return total + fold3(mm(rows3(block), act_v[:, columns(b)], NT))

    pt = lax.fori_loop(0, nb, apply_second, jnp.zeros((r, tok), F32))
    ptf[y] = pt
    own = ptf.at[y]
    recv = [send(own, own, device(z, x, c, yy)) for _, yy in y_peers]

    def err_right(b, total):
        hi, lo = split2(err_v[columns(b), :])
        block = rows3(q_out[b])
        return total + (mm(block, lo) + mm(block, hi))

    right = fold3(lax.fori_loop(0, nb, err_right, jnp.zeros((3 * r, err_v.shape[1]), F32)))
    load_vg.wait()
    wait_all(recv)
    for yy in range(ny):
        right = right + fold3(mm(rows3(ptf[yy]), vg_v[yy * tok : (yy + 1) * tok, :]))
    rs0[...] = right
    recv = [send(rs0, rr_c.at[dc - 1], device(z, x, shifted(c, dc, nc), y)) for dc in range(1, nc)]
    wait_all(recv)
    for dc in range(nc - 1):
        right = right + rr_c[dc]
    rs1[0] = right
    recv = [send(rs1.at[0], rr_x.at[dx - 1], device(z, xx, c, y)) for dx, xx in x_peers]
    wait_all(recv)
    for dx in range(nx - 1):
        right = right + rr_x[dx]
    rs1[1] = right
    recv = [send(rs1.at[1], rr_z.at[dz - 1], device(zz, x, c, y)) for dz, zz in z_peers]
    wait_all(recv)
    for dz in range(nz - 1):
        right = right + rr_z[dz]
    r_out[...] = right / float(nz * nx * nc)

    for i in range(half, CHUNKS):
        from_down[i].wait_recv()
    for j in range(half):
        from_up[j].wait_recv()
    wait_all(passed)
    wait_all(sent_out)
    for copy in kept_out + [keep_act]:
        copy.wait()
    for copy in sent:
        copy.wait_send()


def error_kernel(act, vg, err, q, right, out):
    ny, tok, width = act.shape
    cotangent = vg[...]
    hi, lo = split2(right[...])
    right3 = jnp.concatenate([hi, hi, lo], axis=0)
    for j in range(width // BLK):
        cols = slice(j * BLK, (j + 1) * BLK)
        tokens = act[:, :, cols].reshape(ny * tok, BLK)
        hi, lo = split2(q[j])
        approx = mm(jnp.concatenate([hi, lo, hi], axis=0), right3, TN)
        out[cols, :] = (mm(tokens, cotangent, TN) + err[cols, :]) - approx


def build(geom):
    nz, nx, nc, ny = geom

    def body(act, vg, w, err, right_prev):
        tok, d = act.shape
        kv = vg.shape[1]
        r = right_prev.shape[1]
        nb = nc * nx * nz
        assert d == nb * BLK and kv == BLK
        err = err[0]
        anywhere = pl.BlockSpec(memory_space=pl.ANY)
        vmem = pl.BlockSpec(memory_space=pltpu.VMEM)
        xc = nx * nc
        sends = 6 * (ny - 1) + 2 * CHUNKS + CHUNKS + (xc - 1) * 2 + (ny - 1) * (nz - 1) + 3 * (nc + nx + nz - 3)
        actfull, q, right, grad_input = pl.pallas_call(
            functools.partial(comm_kernel, geom),
            out_shape=(
                jax.ShapeDtypeStruct((ny, tok, d), BF16),
                jax.ShapeDtypeStruct((nb, r, BLK), F32),
                jax.ShapeDtypeStruct((r, kv), F32),
                jax.ShapeDtypeStruct((tok, d), BF16),
            ),
            in_specs=[anywhere, anywhere, anywhere, anywhere, vmem],
            out_specs=(anywhere, vmem, vmem, anywhere),
            scratch_shapes=[
                pltpu.VMEM((tok, d), BF16),
                pltpu.VMEM(vg.shape, BF16),
                pltpu.VMEM((d, kv), F32),
                pltpu.VMEM((ny, r, kv), F32),
                pltpu.VMEM((xc, ny, tok, kv), BF16),
                pltpu.VMEM((nz, ny, BLK, kv), BF16),
                pltpu.VMEM((xc, tok, nz * BLK), BF16),
                pltpu.VMEM((nc, nx * nz, r, BLK), F32),
                pltpu.VMEM((nc, nx * nz, r, BLK), F32),
                pltpu.VMEM((nx * nz, r, BLK), F32),
                pltpu.VMEM((max(nx - 1, 1), nz, r, BLK), F32),
                pltpu.VMEM((max(nz - 1, 1), r, BLK), F32),
                pltpu.VMEM((ny - 1, r // ny, BLK), F32),
                pltpu.VMEM((nb, r, BLK), F32),
                pltpu.VMEM((ny, r, tok), F32),
                pltpu.VMEM((r, kv), F32),
                pltpu.VMEM((2, r, kv), F32),
                pltpu.VMEM((max(nc - 1, 1), r, kv), F32),
                pltpu.VMEM((max(nx - 1, 1), r, kv), F32),
                pltpu.VMEM((max(nz - 1, 1), r, kv), F32),
                pltpu.SemaphoreType.DMA((8 + nz + nc,)),
                pltpu.SemaphoreType.DMA((sends,)),
                pltpu.SemaphoreType.DMA((sends,)),
            ],
            compiler_params=pltpu.CompilerParams(
                collective_id=0, has_side_effects=True, vmem_limit_bytes=48 * 1024 * 1024
            ),
        )(act, vg, w, err, right_prev.T)

        width = 2 * BLK
        error_next = pl.pallas_call(
            error_kernel,
            grid=(d // width,),
            out_shape=jax.ShapeDtypeStruct((d, kv), F32),
            in_specs=[
                pl.BlockSpec((ny, tok, width), lambda i: (0, 0, i)),
                pl.BlockSpec(vg.shape, lambda i: (0, 0)),
                pl.BlockSpec((width, kv), lambda i: (i, 0)),
                pl.BlockSpec((2, r, BLK), lambda i: (i, 0, 0)),
                pl.BlockSpec((r, kv), lambda i: (0, 0)),
            ],
            out_specs=pl.BlockSpec((width, kv), lambda i: (i, 0)),
            compiler_params=pltpu.CompilerParams(vmem_limit_bytes=32 * 1024 * 1024),
        )(actfull, vg, err, q, right)
        left_factor = (q * math.sqrt(float(d))).transpose(0, 2, 1).reshape(d, r)
        return (grad_input, error_next[None], left_factor, right.T)

    return body


def solution(mesh):
    return jax.shard_map(
        build((4, 4, 2, 4)),
        mesh=mesh,
        in_specs=(
            P(("dp", "tp"), None),
            P("dp", "tp"),
            P(None, "tp"),
            P("dp", None, "tp"),
            P("tp", None),
        ),
        out_specs=(P(("dp", "tp"), None), P("dp", None, "tp"), P(), P("tp", None)),
        check_vma=False,
    )
```

time: 587 us -> 155 us (0.26); the launches traced: 576 us -> 154 us
  waiting for transfers between devices: 229 us -> 0 us
  Pallas kernels: 0 us -> 143 us
  matrix products: 125 us -> 0 us
  blocking collectives: 122 us -> 0 us
  between operations: 37.4 us -> 0.68 us
  other arithmetic: 32.6 us -> 0.14 us
  local copies, waits for them, and re-layouts: 29 us -> 9.67 us
    pallas_call x0 -> x2, Pallas kernels: none -> 143 us  [the longest x1 133 us: body(): pl.pallas_call(functools.partial(comm_kernel, geom), out_shape=(jax.Shape...]
    psum x1 -> x0, waiting for transfers between devices: 140 us -> none  [body(): left_sum = lax.psum(local_left, ('dp', 'tp'))]
    dot_general x125 -> x0, matrix products: 125 us -> none  [the longest x60 50 us: orthonormal(): weights = jnp.dot(vector, spanned, precision=highest)]
    psum x1 -> x0, blocking collectives: 122 us -> none  [body(): lax.psum(local_right.astype(jnp.bfloat16), 'dp').astype(jnp.float32)]
    all_gather x1 -> x0, waiting for transfers between devices: 88.1 us -> none  [body(): lax.all_gather(activations, 'tp', axis=0, tiled=True)]
    another operation x28 -> x0, local copies, waits for them, and re-layouts: 25.5 us -> none  [the longest x27 24 us: orthonormal(): spanned = jnp.stack(columns, axis=1)]
    reduce_sum x31 -> x0, other arithmetic: 20.2 us -> none  [orthonormal(): vector = vector / jnp.sqrt(jnp.sum(vector * vector) + 1e-12)]
    slice x2 -> x0, other arithmetic: 7.57 us -> none  [orthonormal(): vector = factor[:, number]]
  transfers between devices with their start and end apart: 3 -> 0, of which waited for: 2 -> 0; matrix products, arithmetic and copies ran while one was open for 29% -> 0% of each run, Pallas kernels for 0% -> 0%
where the time goes in v1:
time: 155 us; the launch traced here: 154 us
  Pallas kernels  143 us (92%)
  local copies, waits for them, and re-layouts  9.67 us (6%)
    pallas_call x1, Pallas kernels, body(): pl.pallas_call(functools.partial(comm_kernel, geom), out_shape=(jax.Shape...  133 us
    pallas_call x1, Pallas kernels, body(): pl.pallas_call(error_kernel, grid=(d // width,), out_shape=jax.ShapeDtype...  10.4 us
    unnamed x12, local copies, waits for them, and re-layouts  8.6 us

profile of v1, /device:TPU:1, one launch (start us, length us, event | category | flops | bytes accessed | tf_op | source)
XLA Modules:
  0.0 153.7 jit_solution(17248707429527958804)
XLA Ops:
  0.6 0.0 copy-start.2
  0.6 1.6 %copy-done.2 = bf16[128,8192]{1,0:T(8,128)(2,1)S(1)} copy-done((bf16[128,8192]{1,0:T(8,128)(2,1)S(1)}, bf16[128,8192]{1,0:T(8,128)(2,1)}, u32[]{:S(2)}) %copy-start.2) | copy-done | bytes 2097176
  2.2 0.0 copy-start.3
  2.2 0.9 copy-done.3
  3.2 0.0 copy-start.4
  3.2 0.8 copy-done.4
  3.9 0.0 copy-start
  3.9 132.8 %shard_map.84 = (bf16[4,128,8192]{2,1,0:T(8,128)(2,1)}, f32[32,32,256]{2,1,0:T(8,128)S(1)}, f32[32,256]{1,0:T(8,128)S(1)}, bf16[128,8192]{1,0:T(8,128)(2,1)S(1)}) custom-call(bf16[128,8192]{1,0:T(8,128)(2,1)S(1)} %copy-done.2, bf16[512,256]{1,0:T(8,128)(2,1)S(1)} %copy-done.3, bf16[8192,256]{1,0:T(8,128)(2,1)} %w.1, f32[8192,256]{1,0:T(8,128)} %bitcast.8, ...), custom_call_target="tpu_custom_call" | custom-call | tf_op jit(solution)/shard_map/pallas_call | solution.py:395
  136.8 0.0 copy-done
  136.8 0.0 copy-start.1
  136.8 3.4 %copy-done.1 = bf16[4,128,8192]{2,1,0:T(8,128)(2,1)S(1)} copy-done((bf16[4,128,8192]{2,1,0:T(8,128)(2,1)S(1)}, bf16[4,128,8192]{2,1,0:T(8,128)(2,1)}, u32[]{:S(2)}) %copy-start.1) | copy-done | bytes 8388632
  140.2 10.4 %shard_map.85 = f32[8192,256]{1,0:T(8,128)} custom-call(bf16[4,128,8192]{2,1,0:T(8,128)(2,1)S(1)} %copy-done.1, bf16[512,256]{1,0:T(8,128)(2,1)S(1)} %copy-done.3, f32[8192,256]{1,0:T(8,128)S(1)} %bitcast.9, f32[32,32,256]{2,1,0:T(8,128)S(1)} %get-tuple-element.10.q, f32[32,256]{1,0:T(8,128)S(1)} %get-tuple-element.11.right), custom_call_target="tpu_custom_call" | custom-call | tf_op jit(solution)/shard_map/pallas_call | solution.py:436
  150.5 0.1 multiply_bitcast_fusion
  150.7 1.1 copy.10
  151.8 1.3 copy.13
  153.1 0.6 copy.14
Async XLA Ops:
  0.6 1.6 %copy-start.2 = (bf16[128,8192]{1,0:T(8,128)(2,1)S(1)}, bf16[128,8192]{1,0:T(8,128)(2,1)}, u32[]{:S(2)}) copy-start(bf16[128,8192]{1,0:T(8,128)(2,1)} %act.1) | copy-start | bytes 6291460
  2.2 0.9 copy-start.3
  3.2 0.8 copy-start.4
  3.9 132.8 %copy-start = (f32[1,8192,256]{2,1,0:T(8,128)S(1)}, f32[1,8192,256]{2,1,0:T(8,128)}, u32[]{:S(2)}) copy-start(f32[1,8192,256]{2,1,0:T(8,128)} %param.8) | copy-start | bytes 25165828
  136.8 3.4 %copy-start.1 = (bf16[4,128,8192]{2,1,0:T(8,128)(2,1)S(1)}, bf16[4,128,8192]{2,1,0:T(8,128)(2,1)}, u32[]{:S(2)}) copy-start(bf16[4,128,8192]{2,1,0:T(8,128)(2,1)} %get-tuple-element.9.act) | copy-start | bytes 25165828

commit v2 on v1

--- a/solution.py
+++ b/solution.py
@@ -13,11 +13,12 @@
 F32 = jnp.float32
 BF16 = jnp.bfloat16
 BLK = 256
+D = 8192
 EPS = 1e-12
+VMEM = 62 * 1024 * 1024
 NN = (((1,), (0,)), ((), ()))
 NT = (((1,), (1,)), ((), ()))
 TN = (((0,), (0,)), ((), ()))
-CHUNKS = 4
 
 
 def mm(a, b, dims=NN, precision=None):
@@ -65,8 +66,8 @@
 
 
 def comm_kernel(
-    geom, act, vg, w, err, rt, actfull, q_out, r_out, gi,
-    act_v, vg_v, err_v, rtf, vgx, wbuf, outs, lacc, lf, rc, rx, rz, ry, q1, ptf, rs0, rs1, rr_c, rr_x, rr_z,
+    geom, act, vg, w, err, rt_in, q_out, r_out, gi,
+    rt, act_v, vg_v, err_v, rtf, vgx, wbuf, outs, lacc, lf, rc, rx, rz, ry, q1, ptf, rs0, rs1, rr_c, rr_x, rr_z,
     local_sem, send_sem, recv_sem,
 ):
     nz, nx, nc, ny = geom
@@ -117,6 +118,7 @@
         for copy in copies:
             copy.wait_recv()
 
+    load_rt = fetch(rt_in, rt)
     load_vgx = fetch(vg.at[pl.ds(pl.multiple_of(y * tok, tok), tok)], vgx.at[k, y])
     quarter = d // nc
     load_err = [fetch(err.at[pl.ds(i * quarter, quarter)], err_v.at[pl.ds(i * quarter, quarter)]) for i in range(nc)]
@@ -125,7 +127,6 @@
     load_w = [
         fetch(w.at[pl.ds(pl.multiple_of((k * nz + zz) * BLK, BLK), BLK)], wbuf.at[zz, y]) for zz in range(nz)
     ]
-    keep_act = fetch(act, actfull.at[y])
 
     barrier = pltpu.get_barrier_semaphore()
     everyone = (
@@ -137,7 +138,7 @@
         pl.semaphore_signal(barrier, inc=1, device_id=peer, device_id_type=MESH)
     pl.semaphore_wait(barrier, len(everyone))
 
-    recv_rt = [send(rt, rtf.at[y], device(z, x, c, yy)) for _, yy in y_peers]
+    recv_rt = [send(rt_in, rtf.at[y], device(z, x, c, yy)) for _, yy in y_peers]
     recv_vg = [
         send(vg.at[pl.ds(pl.multiple_of(yy * tok, tok), tok)], vgx.at[k, y], device(z, x, c, yy)) for _, yy in y_peers
     ]
@@ -145,28 +146,7 @@
         send(w.at[pl.ds(pl.multiple_of((k * nz + z) * BLK, BLK), BLK)], wbuf.at[z, y], device(z, x, c, yy))
         for _, yy in y_peers
     ]
-    up, down = shifted(y, 1, ny), shifted(y, ny - 1, ny)
-    part = tok // CHUNKS
-    half = CHUNKS // 2
-
-    def rows(i):
-        return pl.ds(i * part, part)
-
-    from_down, from_up = {}, {}
-    for i in range(CHUNKS):
-        j = (i + half) % CHUNKS
-        from_down[i] = send(act.at[rows(i)], actfull.at[y, rows(i)], device(z, x, c, up))
-        from_up[j] = send(act.at[rows(j)], actfull.at[y, rows(j)], device(z, x, c, down))
-
-    passed = []
-
-    def forward(i):
-        from_down[i].wait_recv()
-        passed.append(send(actfull.at[down, rows(i)], actfull.at[down, rows(i)], device(z, x, c, up)))
-        j = i + half
-        from_up[j].wait_recv()
-        passed.append(send(actfull.at[up, rows(j)], actfull.at[up, rows(j)], device(z, x, c, down)))
-
+    load_rt.wait()
     rtf[y] = rt[...]
     rt3 = rows3(rt[...])
     per = nx * nz
@@ -276,7 +256,6 @@
     own = lf.at[c, mine, strip(y)]
     recv = [send(own, own, device(z, x, c, yy)) for _, yy in y_peers]
     some_jobs(2)
-    forward(0)
     wait_all(recv)
     own = lf.at[c, mine]
     recv = [send(own, own, device(zz, x, c, y)) for _, zz in z_peers]
@@ -289,8 +268,6 @@
     own = lf.at[c]
     recv = [send(own, own, device(z, x, shifted(c, dc, nc), y)) for dc in range(1, nc)]
     some_jobs(len(jobs))
-    for i in range(1, half):
-        forward(i)
     wait_all(recv)
 
     def gram_of(ref_of):
@@ -353,26 +330,25 @@
         right = right + rr_z[dz]
     r_out[...] = right / float(nz * nx * nc)
 
-    for i in range(half, CHUNKS):
-        from_down[i].wait_recv()
-    for j in range(half):
-        from_up[j].wait_recv()
-    wait_all(passed)
     wait_all(sent_out)
-    for copy in kept_out + [keep_act]:
+    for copy in kept_out:
         copy.wait()
     for copy in sent:
         copy.wait_send()
 
 
-def error_kernel(act, vg, err, q, right, out):
+def error_kernel(act, vg, err, q, right, gi_in, out, left_out, right_out, gi_out):
     ny, tok, width = act.shape
+    gi_out[...] = gi_in[...]
+    right_out[...] = right[...]
+    scale = math.sqrt(float(D))
     cotangent = vg[...]
     hi, lo = split2(right[...])
     right3 = jnp.concatenate([hi, hi, lo], axis=0)
     for j in range(width // BLK):
         cols = slice(j * BLK, (j + 1) * BLK)
         tokens = act[:, :, cols].reshape(ny * tok, BLK)
+        left_out[:, cols] = q[j] * scale
         hi, lo = split2(q[j])
         approx = mm(jnp.concatenate([hi, lo, hi], axis=0), right3, TN)
         out[cols, :] = (mm(tokens, cotangent, TN) + err[cols, :]) - approx
@@ -388,21 +364,22 @@
         nb = nc * nx * nz
         assert d == nb * BLK and kv == BLK
         err = err[0]
-        anywhere = pl.BlockSpec(memory_space=pl.ANY)
+        hbm = pl.BlockSpec(memory_space=pltpu.HBM)
         vmem = pl.BlockSpec(memory_space=pltpu.VMEM)
         xc = nx * nc
-        sends = 6 * (ny - 1) + 2 * CHUNKS + CHUNKS + (xc - 1) * 2 + (ny - 1) * (nz - 1) + 3 * (nc + nx + nz - 3)
-        actfull, q, right, grad_input = pl.pallas_call(
+        sends = 6 * (ny - 1) + (xc - 1) * 2 + (ny - 1) * (nz - 1) + 3 * (nc + nx + nz - 3)
+        actfull = lax.all_gather(act, "tp", axis=0, tiled=False)
+        q, right, grad_input = pl.pallas_call(
             functools.partial(comm_kernel, geom),
             out_shape=(
-                jax.ShapeDtypeStruct((ny, tok, d), BF16),
                 jax.ShapeDtypeStruct((nb, r, BLK), F32),
                 jax.ShapeDtypeStruct((r, kv), F32),
                 jax.ShapeDtypeStruct((tok, d), BF16),
             ),
-            in_specs=[anywhere, anywhere, anywhere, anywhere, vmem],
-            out_specs=(anywhere, vmem, vmem, anywhere),
+            in_specs=[hbm] * 5,
+            out_specs=(vmem, vmem, hbm),
             scratch_shapes=[
+                pltpu.VMEM((r, kv), F32),
                 pltpu.VMEM((tok, d), BF16),
                 pltpu.VMEM(vg.shape, BF16),
                 pltpu.VMEM((d, kv), F32),
@@ -428,27 +405,37 @@
                 pltpu.SemaphoreType.DMA((sends,)),
             ],
             compiler_params=pltpu.CompilerParams(
-                collective_id=0, has_side_effects=True, vmem_limit_bytes=48 * 1024 * 1024
+                collective_id=0, has_side_effects=True, vmem_limit_bytes=VMEM
             ),
         )(act, vg, w, err, right_prev.T)
 
         width = 2 * BLK
-        error_next = pl.pallas_call(
+        error_next, left, right, grad_input = pl.pallas_call(
             error_kernel,
             grid=(d // width,),
-            out_shape=jax.ShapeDtypeStruct((d, kv), F32),
+            out_shape=(
+                jax.ShapeDtypeStruct((d, kv), F32),
+                jax.ShapeDtypeStruct((r, d), F32),
+                jax.ShapeDtypeStruct((r, kv), F32),
+                jax.ShapeDtypeStruct((tok, d), BF16),
+            ),
             in_specs=[
                 pl.BlockSpec((ny, tok, width), lambda i: (0, 0, i)),
                 pl.BlockSpec(vg.shape, lambda i: (0, 0)),
                 pl.BlockSpec((width, kv), lambda i: (i, 0)),
                 pl.BlockSpec((2, r, BLK), lambda i: (i, 0, 0)),
                 pl.BlockSpec((r, kv), lambda i: (0, 0)),
+                pl.BlockSpec((tok, width), lambda i: (0, i)),
             ],
-            out_specs=pl.BlockSpec((width, kv), lambda i: (i, 0)),
-            compiler_params=pltpu.CompilerParams(vmem_limit_bytes=32 * 1024 * 1024),
-        )(actfull, vg, err, q, right)
-        left_factor = (q * math.sqrt(float(d))).transpose(0, 2, 1).reshape(d, r)
-        return (grad_input, error_next[None], left_factor, right.T)
+            out_specs=(
+                pl.BlockSpec((width, kv), lambda i: (i, 0)),
+                pl.BlockSpec((r, width), lambda i: (0, i)),
+                pl.BlockSpec((r, kv), lambda i: (0, 0)),
+                pl.BlockSpec((tok, width), lambda i: (0, i)),
+            ),
+            compiler_params=pltpu.CompilerParams(vmem_limit_bytes=VMEM),
+        )(actfull, vg, err, q, right, grad_input)
+        return (grad_input, error_next[None], left.T, right.T)
 
     return body
 

time: 155 us -> 161 us (1.039)
  between operations: 0.68 us -> 14.1 us
  local copies, waits for them, and re-layouts: 9.67 us -> 0 us
    unnamed x12 -> x0, local copies, waits for them, and re-layouts: 8.6 us -> none
    pallas_call x1, Pallas kernels: 10.4 us -> 18 us  [body(): pl.pallas_call(error_kernel, grid=(d // width,), out_shape=(jax.ShapeDtyp...]
    pallas_call x1, Pallas kernels: 133 us -> 126 us  [body(): pl.pallas_call(functools.partial(comm_kernel, geom), out_shape=(jax.Shape...]
  transfers between devices with their start and end apart: 0 -> 1, of which waited for: 0 -> 0; matrix products, arithmetic and copies ran while one was open for 0% -> 0% of each run, Pallas kernels for 0% -> 79%
where the time goes in v2:
time: 161 us; the launch traced here: 159 us
  Pallas kernels  144 us (89%)
  between operations  14.1 us (9%)
    pallas_call x1, Pallas kernels, body(): pl.pallas_call(functools.partial(comm_kernel, geom), out_shape=(jax.Shape...  126 us
    pallas_call x1, Pallas kernels, body(): pl.pallas_call(error_kernel, grid=(d // width,), out_shape=(jax.ShapeDtyp...  18 us
  transfers between devices with their start and end apart: 1, of which 0 were waited for; matrix products, arithmetic and copies ran while one was open for 0% of the time, Pallas kernels for 79%

profile of v2, /device:TPU:1, one launch (start us, length us, event | category | flops | bytes accessed | tf_op | source)
XLA Modules:
  0.0 158.8 jit_solution(7005808955297423000)
XLA Ops:
  7.2 0.0 all-gather.3.cloned.1.call-start
  7.2 0.7 all-gather.3.cloned.1.call-update
  7.9 126.0 %shard_map.84 = (f32[32,32,256]{2,1,0:T(8,128)}, f32[32,256]{1,0:T(8,128)}, bf16[128,8192]{1,0:T(8,128)(2,1)}) custom-call(bf16[128,8192]{1,0:T(8,128)(2,1)} %act.1, bf16[512,256]{1,0:T(8,128)(2,1)} %vg.3, bf16[8192,256]{1,0:T(8,128)(2,1)} %w.1, f32[8192,256]{1,0:T(8,128)} %bitcast.6, f32[32,256]{1,0:T(8,128)} %bitcast.9), custom_call_target="tpu_custom_call" | custom-call | tf_op jit(solution)/shard_map/pallas_call | solution.py:372
  133.9 0.0 all-gather.3.cloned.1.call-done
  133.9 18.0 %shard_map.85 = (f32[8192,256]{1,0:T(8,128)}, f32[32,8192]{1,0:T(8,128)}, f32[32,256]{1,0:T(8,128)}, bf16[128,8192]{1,0:T(8,128)(2,1)}) custom-call(bf16[4,128,8192]{2,1,0:T(8,128)(2,1)} %bitcast.8, bf16[512,256]{1,0:T(8,128)(2,1)} %vg.3, f32[8192,256]{1,0:T(8,128)} %bitcast.7, f32[32,32,256]{2,1,0:T(8,128)} %get-tuple-element.11.q, ...), custom_call_target="tpu_custom_call" | custom-call | tf_op jit(solution)/shard_map/pallas_call | solution.py:413
Async XLA Ops:
  7.2 126.8 %all-gather.3.cloned.1.call-start = ((), (), s32[]{:S(2)}) async-start(), calls=%async_computation | async-start | bytes 10485760 | tf_op jit(solution)/shard_map/all_gather | solution.py:371
Sparse Core Ops, SparseCore 0:
  9.7 87.1 all-gather.2

commit v3 on v2

v3 whole, which is shorter than its diff:
```python
import functools
import math

import jax
import jax.numpy as jnp
from jax import lax
from jax.experimental import pallas as pl
from jax.experimental.pallas import tpu as pltpu
from jax.sharding import PartitionSpec as P

MESH = pl.DeviceIdType.MESH
HIGHEST = lax.Precision.HIGHEST
F32 = jnp.float32
BF16 = jnp.bfloat16
BLK = 256
D = 8192
EPS = 1e-12
MIB = 1024 * 1024
WIDE = 8 * BLK
CHUNKS = 8
NN = (((1,), (0,)), ((), ()))
NT = (((1,), (1,)), ((), ()))
TN = (((0,), (0,)), ((), ()))


def mm(a, b, dims=NN, precision=None):
    return lax.dot_general(a, b, dims, precision=precision, preferred_element_type=F32)


def split2(a):
    hi = a.astype(BF16)
    lo = (a - hi.astype(F32)).astype(BF16)
    return hi, lo


def split3(a):
    hi = a.astype(BF16)
    rest = a - hi.astype(F32)
    mid = rest.astype(BF16)
    lo = (rest - mid.astype(F32)).astype(BF16)
    return hi, mid, lo


def rows3(a):
    return jnp.concatenate(split3(a), axis=0)


def fold3(a):
    n = a.shape[0] // 3
    return (a[2 * n :] + a[n : 2 * n]) + a[:n]


def self_products(total, r):
    total = fold3(total)
    return (total[:, 2 * r :] + total[:, r : 2 * r]) + total[:, :r]


def times(a, b):
    a_hi, a_mid, a_lo = (v.astype(F32) for v in split3(a))
    b_hi, b_mid, b_lo = split3(b)
    left = jnp.concatenate([a_lo, a_mid, a_hi, a_mid, a_hi, a_hi], axis=1).astype(BF16)
    return mm(left, jnp.concatenate([b_hi, b_mid, b_lo, b_hi, b_mid, b_hi], axis=0))


def gram_schmidt(gram):
    n = gram.shape[0]
    row_id = lax.broadcasted_iota(jnp.int32, (n, 1), 0)
    eye = (lax.broadcasted_iota(jnp.int32, (n, n), 0) == lax.broadcasted_iota(jnp.int32, (n, n), 1)).astype(F32)
    left, weights = gram, eye
    for j in range(n):
        column = jnp.broadcast_to(left[:, j : j + 1], (n, n))
        s = jnp.maximum(column[j : j + 1, :], 0.0)
        inverse = 1.0 / (s + EPS)
        c = (2.0 - s * inverse) * inverse
        f = jnp.where(row_id > j, column * c, 0.0)
        new_weights = weights - f * weights[j : j + 1, :]
        left = left - (f * (2.0 - c * s)) * left[j : j + 1, :]
        weights = new_weights
    s = jnp.maximum(jnp.sum(left * eye, axis=1, keepdims=True), 0.0)
    return weights / jnp.sqrt(s + EPS), eye * (s / (s + EPS))


def comm_kernel(
    geom, act, vg, w, err, rt_in, merged, q_out, r_out, gi,
    rt, actr, vg_v, err_v, rtf, vgx, wbuf, outs, lacc, lf, rc, rx, rz, ry, q1, q3, ptf, rs0, rs1, rr_c, rr_x, rr_z,
    local_sem, send_sem, recv_sem,
):
    nz, nx, nc, ny = geom
    nb = nc * nx * nz
    per = nx * nz
    _, tok, d = actr.shape
    r = rt.shape[0]
    rq = r // ny
    wide = min(WIDE, per * BLK)
    wb = wide // BLK
    pieces = d // wide
    dp, y = lax.axis_index("dp"), lax.axis_index("tp")
    c = lax.rem(dp, nc)
    x = lax.rem(lax.div(dp, nc), nx)
    z = lax.div(dp, nc * nx)
    k = c * nx + x

    def shifted(i, by, n):
        return lax.rem(i + by, n)

    def device(zz, xx, cc, yy):
        return ((zz * nx + xx) * nc + cc, yy)

    y_peers = [(dy, shifted(y, dy, ny)) for dy in range(1, ny)]
    z_peers = [(dz, shifted(z, dz, nz)) for dz in range(1, nz)]
    x_peers = [(dx, shifted(x, dx, nx)) for dx in range(1, nx)]
    group = [
        (shifted(x, dx, nx), shifted(c, dc, nc)) for dc in range(nc) for dx in range(nx) if (dc, dx) != (0, 0)
    ]
    up, down, across = shifted(y, 1, ny), shifted(y, ny - 1, ny), shifted(y, 2, ny)

    sent = []
    counter = [0, 0]

    def send(src, dst, to):
        i = counter[0]
        counter[0] += 1
        copy = pltpu.make_async_remote_copy(
            src_ref=src, dst_ref=dst, send_sem=send_sem.at[i], recv_sem=recv_sem.at[i], device_id=to, device_id_type=MESH
        )
        copy.start()
        sent.append(copy)
        return copy

    def fetch(src, dst):
        i = counter[1]
        counter[1] += 1
        copy = pltpu.make_async_copy(src, dst, local_sem.at[i])
        copy.start()
        return copy

    def wait_all(copies):
        for copy in copies:
            copy.wait_recv()

    def tokens(yy):
        return pl.ds(pl.multiple_of(yy * tok, tok), tok)

    load_rt = fetch(rt_in, rt)
    load_vgx = fetch(vg.at[tokens(y)], vgx.at[k, y])
    share = d // 4
    load_err = [fetch(err.at[pl.ds(i * share, share)], err_v.at[pl.ds(i * share, share)]) for i in range(4)]
    load_act = fetch(act, actr.at[0])
    load_vg = [fetch(vg.at[tokens(yy)], vg_v.at[i]) for i, yy in enumerate((y, down, up, across))]
    load_w = [
        fetch(w.at[pl.ds(pl.multiple_of((k * nz + zz) * BLK, BLK), BLK)], wbuf.at[zz, y]) for zz in range(nz)
    ]

    barrier = pltpu.get_barrier_semaphore()
    everyone = (
        [device(z, xx, cc, y) for xx, cc in group]
        + [device(zz, x, c, y) for _, zz in z_peers]
        + [device(z, x, c, yy) for _, yy in y_peers]
    )
    for peer in everyone:
        pl.semaphore_signal(barrier, inc=1, device_id=peer, device_id_type=MESH)
    pl.semaphore_wait(barrier, len(everyone))

    recv_rt = [send(rt_in, rtf.at[y], device(z, x, c, yy)) for _, yy in y_peers]
    recv_vg = [send(vg.at[tokens(yy)], vgx.at[k, y], device(z, x, c, yy)) for _, yy in y_peers]
    recv_w = [
        send(w.at[pl.ds(pl.multiple_of((k * nz + z) * BLK, BLK), BLK)], wbuf.at[z, y], device(z, x, c, yy))
        for _, yy in y_peers
    ]
    half = CHUNKS // 2
    part = d // CHUNKS

    def cols(i):
        return pl.ds(i * part, part)

    from_down, from_up, from_across = {}, {}, {}
    for i in range(CHUNKS):
        j = (i + half) % CHUNKS
        from_down[i] = send(act.at[:, cols(i)], actr.at[1, :, cols(i)], device(z, x, c, up))
        from_up[j] = send(act.at[:, cols(j)], actr.at[2, :, cols(j)], device(z, x, c, down))

    def forward(i):
        from_down[i].wait_recv()
        from_across[i] = send(actr.at[1, :, cols(i)], actr.at[3, :, cols(i)], device(z, x, c, up))
        j = i + half
        from_up[j].wait_recv()
        from_across[j] = send(actr.at[2, :, cols(j)], actr.at[3, :, cols(j)], device(z, x, c, down))

    load_rt.wait()
    rtf[y] = rt[...]
    rt3 = rows3(rt[...])

    def columns(p):
        return pl.ds(pl.multiple_of(p * wide, wide), wide)

    def store_left(value, cc, j0):
        for j in range(wb):
            lacc[cc, j0 + j] = value[:, j * BLK : (j + 1) * BLK]

    def load_left(ref, cc, j0):
        return jnp.concatenate([ref[cc, j0 + j] for j in range(wb)], axis=1)

    per_piece = per // wb

    for load in load_err:
        load.wait()

    def err_left(p, carry):
        hi, lo = split2(err_v[columns(p), :])
        store_left(fold3(mm(rt3, lo, NT)) + fold3(mm(rt3, hi, NT)), lax.div(p, per_piece), lax.rem(p, per_piece) * wb)
        return carry

    lax.fori_loop(0, pieces, err_left, 0)

    wait_all(recv_rt)
    load_vgx.wait()
    wait_all(recv_vg)
    recv_vgx = [send(vgx.at[k], vgx.at[k], device(z, xx, cc, y)) for xx, cc in group]
    ut = jnp.zeros((r, tok), F32)
    for yy in range(ny):
        ut = ut + fold3(mm(rows3(rtf[yy]), vgx[k, yy], NT))
    ut3 = rows3(ut)
    load_act.wait()

    def act_left(cc):
        def step(i, carry):
            value = fold3(mm(ut3, actr[0, :, columns(cc * per_piece + i)]))
            store_left(load_left(lacc, cc, i * wb) + value, cc, i * wb)
            return carry

        lax.fori_loop(0, per_piece, step, 0)

    recv_c = []
    for dc in range(1, nc):
        cc = shifted(c, dc, nc)
        act_left(cc)
        recv_c.append(send(lacc.at[cc], rc, device(z, x, cc, y)))
    act_left(c)

    for copy in load_w:
        copy.wait()
    recv_wz = []
    for copy, (dy, _) in zip(recv_w, y_peers):
        copy.wait_recv()
        source = shifted(y, ny - dy, ny)
        for _, zz in z_peers:
            recv_wz.append(send(wbuf.at[z, source], wbuf.at[z, source], device(zz, x, c, y)))

    wait_all(recv_c)
    lacc[c] += rc[...]
    recv = [
        send(lacc.at[c, pl.ds(xx * nz, nz)], rx.at[dx - 1], device(z, xx, c, y)) for dx, xx in x_peers
    ]
    wait_all(recv)
    own_x = pl.ds(x * nz, nz)
    total = lacc[c, own_x]
    for dx in range(nx - 1):
        total = total + rx[dx]
    lacc[c, own_x] = total
    mine = x * nz + z
    recv = [send(lacc.at[c, x * nz + zz], rz.at[dz - 1], device(zz, x, c, y)) for dz, zz in z_peers]
    wait_all(recv)
    total = lacc[c, mine]
    for dz in range(nz - 1):
        total = total + rz[dz]
    lacc[c, mine] = total

    def strip(yy):
        return pl.ds(pl.multiple_of(yy * rq, rq), rq)

    recv = [send(lacc.at[c, mine, strip(yy)], ry.at[dy - 1], device(z, x, c, yy)) for dy, yy in y_peers]
    forward(0)
    wait_all(recv)
    total = lacc[c, mine, strip(y)]
    for dy in range(ny - 1):
        total = total + ry[dy]
    lf[c, mine, strip(y)] = total

    own = lf.at[c, mine, strip(y)]
    recv = [send(own, own, device(z, x, c, yy)) for _, yy in y_peers]
    forward(1)
    wait_all(recv)
    own = lf.at[c, mine]
    recv = [send(own, own, device(zz, x, c, y)) for _, zz in z_peers]
    wait_all(recv)
    own = lf.at[c, own_x]
    recv = [send(own, own, device(z, xx, c, y)) for _, xx in x_peers]

    wait_all(recv_wz)
    wait_all(recv_vgx)
    xc = nc * nx
    many = min(4, xc)

    def input_grad(i, carry):
        zz, g = lax.div(i, xc // many), lax.rem(i, xc // many)
        total = None
        for yy in range(ny):
            cotangent = vgx[pl.ds(g * many, many), yy].reshape(many * tok, BLK)
            piece = mm(cotangent, wbuf[zz, yy], NT).astype(BF16).astype(F32)
            total = piece if total is None else total + piece
        outs[zz, pl.ds(g * many, many)] = total.astype(BF16).reshape(many, tok, BLK)
        return carry

    lax.fori_loop(0, nz * xc // many, input_grad, 0)

    def place(zz):
        return gi.at[:, pl.ds(pl.multiple_of((k * nz + zz) * BLK, BLK), BLK)]

    sent_out = [
        send(outs.at[zz, cc * nx + xx], place(zz), device(z, xx, cc, y)) for xx, cc in group for zz in range(nz)
    ]
    kept_out = [fetch(outs.at[zz, k], place(zz)) for zz in range(nz)]

    wait_all(recv)
    own = lf.at[c]
    recv = [send(own, own, device(z, x, shifted(c, dc, nc), y)) for dc in range(1, nc)]
    forward(2)
    wait_all(recv)

    def left_piece(p):
        return load_left(lf, lax.div(p, per_piece), lax.rem(p, per_piece) * wb)

    def first_gram(p, total):
        block = rows3(left_piece(p))
        return total + mm(block, block, NT)

    nothing = jnp.zeros((3 * r, 3 * r), F32)
    gram = self_products(lax.fori_loop(0, pieces, first_gram, nothing), r)
    weights, norms = gram_schmidt(gram)
    forward(3)

    def apply_first(p, total):
        block = times(weights, left_piece(p))
        q1[p] = block
        block = rows3(block)
        return total + mm(block, block, NT)

    off = self_products(lax.fori_loop(0, pieces, apply_first, nothing), r) - norms
    row_id = lax.broadcasted_iota(jnp.int32, (r, r), 0)
    col_id = lax.broadcasted_iota(jnp.int32, (r, r), 1)
    again = jnp.where(col_id < row_id, off, jnp.where(col_id == row_id, 0.5 * off, 0.0))

    def apply_second(p, total):
        block = q1[p]
        block = block - times(again, block)
        for j in range(wb):
            q_out[p * wb + j] = block[:, j * BLK : (j + 1) * BLK]
        block = rows3(block)
        q3[p] = block
        return total + mm(block, actr[0, :, columns(p)], NT)

    pt = fold3(lax.fori_loop(0, pieces, apply_second, jnp.zeros((3 * r, tok), F32)))
    ptf[0] = pt
    recv = [send(ptf.at[0], ptf.at[dy], device(z, x, c, yy)) for dy, yy in y_peers]

    def err_right(p, total):
        hi, lo = split2(err_v[columns(p), :])
        return total + (mm(q3[p], lo) + mm(q3[p], hi))

    right = fold3(lax.fori_loop(0, pieces, err_right, jnp.zeros((3 * r, err_v.shape[1]), F32)))
    for load in load_vg:
        load.wait()
    wait_all(recv)
    for dy, slot in enumerate((0, 1, 3, 2)):
        right = right + fold3(mm(rows3(ptf[dy]), vg_v[slot]))
    rs0[...] = right
    recv = [send(rs0, rr_c.at[dc - 1], device(z, x, shifted(c, dc, nc), y)) for dc in range(1, nc)]

    for i in range(CHUNKS):
        if i >= half:
            from_down[i].wait_recv()
        else:
            from_up[i].wait_recv()
    near = vg_v[1:3].reshape(2 * tok, BLK)

    def merge_near(i, carry):
        at = pl.ds(pl.multiple_of(i * BLK, BLK), BLK)
        block = actr[1:3, :, at].reshape(2 * tok, BLK)
        merged[at, :] = err_v[at, :] + mm(block, near, TN)
        return carry

    def some_near(p, of):
        lax.fori_loop(p * nb // of, (p + 1) * nb // of, merge_near, 0)

    some_near(0, 4)
    wait_all(recv)
    for dc in range(nc - 1):
        right = right + rr_c[dc]
    rs1[0] = right
    recv = [send(rs1.at[0], rr_x.at[dx - 1], device(z, xx, c, y)) for dx, xx in x_peers]
    some_near(1, 4)
    wait_all(recv)
    for dx in range(nx - 1):
        right = right + rr_x[dx]
    rs1[1] = right
    recv = [send(rs1.at[1], rr_z.at[dz - 1], device(zz, x, c, y)) for dz, zz in z_peers]
    some_near(2, 4)
    some_near(3, 4)
    wait_all(recv)
    for dz in range(nz - 1):
        right = right + rr_z[dz]
    r_out[...] = right / float(nz * nx * nc)

    far = jnp.concatenate([vg_v[0], vg_v[3]], axis=0)

    def merge_far(i, carry):
        at = pl.ds(pl.multiple_of(i * BLK, BLK), BLK)
        block = jnp.concatenate([actr[0, :, at], actr[3, :, at]], axis=0)
        merged[at, :] += mm(block, far, TN)
        return carry

    for i in range(half):
        for j in (i, i + half):
            from_across[j].wait_recv()
            lax.fori_loop(j * part // BLK, (j + 1) * part // BLK, merge_far, 0)

    wait_all(sent_out)
    for copy in kept_out:
        copy.wait()
    for copy in sent:
        copy.wait_send()


def error_kernel(merged, q, right, gi_in, out, left_out, right_out, gi_out):
    gi_out[...] = gi_in[...]
    right_out[...] = right[...]
    scale = math.sqrt(float(D))
    hi, lo = split2(right[...])
    right3 = jnp.concatenate([hi, hi, lo], axis=0)
    for j in range(q.shape[0]):
        cols = slice(j * BLK, (j + 1) * BLK)
        left_out[:, cols] = q[j] * scale
        hi, lo = split2(q[j])
        approx = mm(jnp.concatenate([hi, lo, hi], axis=0), right3, TN)
        out[cols, :] = merged[cols, :] - approx


def build(geom):
    nz, nx, nc, ny = geom

    def body(act, vg, w, err, right_prev):
        tok, d = act.shape
        kv = vg.shape[1]
        r = right_prev.shape[1]
        nb = nc * nx * nz
        per = nx * nz
        wide = min(WIDE, per * BLK)
        assert d == nb * BLK and kv == BLK and per * BLK % wide == 0
        xc = nx * nc
        sends = 6 * (ny - 1) + 3 * CHUNKS + (xc - 1) * (nz + 1) + (ny - 1) * (nz - 1) + 3 * (nc + nx + nz - 3)
        inputs = [
            pltpu.with_memory_space_constraint(a, pltpu.HBM) for a in (act, vg, w, err[0], right_prev.T)
        ]
        hbm = pl.BlockSpec(memory_space=pltpu.HBM)
        vmem = pl.BlockSpec(memory_space=pltpu.VMEM)
        merged, q, right, grad_input = pl.pallas_call(
            functools.partial(comm_kernel, geom),
            out_shape=(
                pltpu.VMEM((d, kv), F32),
                pltpu.VMEM((nb, r, BLK), F32),
                pltpu.VMEM((r, kv), F32),
                pltpu.VMEM((tok, d), BF16),
            ),
            in_specs=[hbm] * 5,
            out_specs=(vmem, vmem, vmem, vmem),
            scratch_shapes=[
                pltpu.VMEM((r, kv), F32),
                pltpu.VMEM((ny, tok, d), BF16),
                pltpu.VMEM((ny, tok, kv), BF16),
                pltpu.VMEM((d, kv), F32),
                pltpu.VMEM((ny, r, kv), F32),
                pltpu.VMEM((xc, ny, tok, kv), BF16),
                pltpu.VMEM((nz, ny, BLK, kv), BF16),
                pltpu.VMEM((nz, xc, tok, BLK), BF16),
                pltpu.VMEM((nc, per, r, BLK), F32),
                pltpu.VMEM((nc, per, r, BLK), F32),
                pltpu.VMEM((per, r, BLK), F32),
                pltpu.VMEM((max(nx - 1, 1), nz, r, BLK), F32),
                pltpu.VMEM((max(nz - 1, 1), r, BLK), F32),
                pltpu.VMEM((ny - 1, r // ny, BLK), F32),
                pltpu.VMEM((d // wide, r, wide), F32),
                pltpu.VMEM((d // wide, 3 * r, wide), BF16),
                pltpu.VMEM((ny, r, tok), F32),
                pltpu.VMEM((r, kv), F32),
                pltpu.VMEM((2, r, kv), F32),
                pltpu.VMEM((max(nc - 1, 1), r, kv), F32),
                pltpu.VMEM((max(nx - 1, 1), r, kv), F32),
                pltpu.VMEM((max(nz - 1, 1), r, kv), F32),
                pltpu.SemaphoreType.DMA((1 + 1 + 4 + 1 + ny + 2 * nz,)),
                pltpu.SemaphoreType.DMA((sends,)),
                pltpu.SemaphoreType.DMA((sends,)),
            ],
            compiler_params=pltpu.CompilerParams(
                collective_id=0, has_side_effects=True, vmem_limit_bytes=44 * MIB
            ),
        )(*inputs)

        blocks = min(4, nb)
        width = blocks * BLK
        error_next, left, right, grad_input = pl.pallas_call(
            error_kernel,
            grid=(d // width,),
            out_shape=(
                jax.ShapeDtypeStruct((d, kv), F32),
                jax.ShapeDtypeStruct((r, d), F32),
                jax.ShapeDtypeStruct((r, kv), F32),
                jax.ShapeDtypeStruct((tok, d), BF16),
            ),
            in_specs=[
                pl.BlockSpec((width, kv), lambda i: (i, 0)),
                pl.BlockSpec((blocks, r, BLK), lambda i: (i, 0, 0)),
                pl.BlockSpec((r, kv), lambda i: (0, 0)),
                pl.BlockSpec((tok, width), lambda i: (0, i)),
            ],
            out_specs=(
                pl.BlockSpec((width, kv), lambda i: (i, 0)),
                pl.BlockSpec((r, width), lambda i: (0, i)),
                pl.BlockSpec((r, kv), lambda i: (0, 0)),
                pl.BlockSpec((tok, width), lambda i: (0, i)),
            ),
            compiler_params=pltpu.CompilerParams(vmem_limit_bytes=20 * MIB),
        )(merged, q, right, grad_input)
        return (grad_input, error_next[None], left.T, right.T)

    return body


def solution(mesh):
    return jax.shard_map(
        build((4, 4, 2, 4)),
        mesh=mesh,
        in_specs=(
            P(("dp", "tp"), None),
            P("dp", "tp"),
            P(None, "tp"),
            P("dp", None, "tp"),
            P("tp", None),
        ),
        out_specs=(P(("dp", "tp"), None), P("dp", None, "tp"), P(), P("tp", None)),
        check_vma=False,
    )
```

time: 161 us -> 127 us (0.79); the launches traced: 159 us -> 127 us
  Pallas kernels: 144 us -> 127 us
  between operations: 14.1 us -> 0.64 us
    pallas_call x1, Pallas kernels: 18 us -> 6.09 us  [body(): pl.pallas_call(error_kernel, grid=(d // width,), out_shape=(jax.ShapeDtyp...]
    pallas_call x1, Pallas kernels: 126 us -> 120 us  [body(): pl.pallas_call(functools.partial(comm_kernel, geom), out_shape=(pltpu.VME...]
  transfers between devices with their start and end apart: 1 -> 0, of which waited for: 0 -> 0; matrix products, arithmetic and copies ran while one was open for 0% -> 0% of each run, Pallas kernels for 79% -> 0%
where the time goes in v3:
time: 127 us
  Pallas kernels  127 us (100%)
    pallas_call x1, Pallas kernels, body(): pl.pallas_call(functools.partial(comm_kernel, geom), out_shape=(pltpu.VME...  120 us
    pallas_call x1, Pallas kernels, body(): pl.pallas_call(error_kernel, grid=(d // width,), out_shape=(jax.ShapeDtyp...  6.09 us

profile of v3, /device:TPU:1, one launch (start us, length us, event | category | flops | bytes accessed | tf_op | source)
XLA Modules:
  0.0 127.2 jit_solution(561611633752140059)
XLA Ops:
  0.6 120.4 %shard_map.84 = (f32[8192,256]{1,0:T(8,128)S(1)}, f32[32,32,256]{2,1,0:T(8,128)S(1)}, f32[32,256]{1,0:T(8,128)S(1)}, bf16[128,8192]{1,0:T(8,128)(2,1)S(1)}) custom-call(bf16[128,8192]{1,0:T(8,128)(2,1)} %act.1, bf16[512,256]{1,0:T(8,128)(2,1)} %vg.1, bf16[8192,256]{1,0:T(8,128)(2,1)} %w.1, f32[8192,256]{1,0:T(8,128)} %bitcast.5, f32[32,256]{1,0:T(8,128)} %bitcast.6), custom_call_target="tpu_custom_call" | custom-call | tf_op jit(solution)/shard_map/pallas_call | solution.py:456
  121.1 6.1 %shard_map.85 = (f32[8192,256]{1,0:T(8,128)}, f32[32,8192]{1,0:T(8,128)}, f32[32,256]{1,0:T(8,128)}, bf16[128,8192]{1,0:T(8,128)(2,1)}) custom-call(f32[8192,256]{1,0:T(8,128)S(1)} %get-tuple-element.12.merged, f32[32,32,256]{2,1,0:T(8,128)S(1)} %get-tuple-element.13.q, f32[32,256]{1,0:T(8,128)S(1)} %get-tuple-element.14.right, ...), custom_call_target="tpu_custom_call" | custom-call | tf_op jit(solution)/shard_map/pallas_call | solution.py:500

commit v4 on v3

v4 whole, which is shorter than its diff:
```python
import functools
import math

import jax
import jax.numpy as jnp
from jax import lax
from jax.experimental import pallas as pl
from jax.experimental.pallas import tpu as pltpu
from jax.sharding import PartitionSpec as P

MESH = pl.DeviceIdType.MESH
F32 = jnp.float32
BF16 = jnp.bfloat16
BLK = 256
EPS = 1e-12
MIB = 1024 * 1024
WIDE = 8 * BLK
CHUNKS = 8
NN = (((1,), (0,)), ((), ()))
NT = (((1,), (1,)), ((), ()))
TN = (((0,), (0,)), ((), ()))


def mm(a, b, dims=NN):
    return lax.dot_general(a, b, dims, preferred_element_type=F32)


def split2(a):
    hi = a.astype(BF16)
    lo = (a - hi.astype(F32)).astype(BF16)
    return hi, lo


def split3(a):
    hi = a.astype(BF16)
    rest = a - hi.astype(F32)
    mid = rest.astype(BF16)
    lo = (rest - mid.astype(F32)).astype(BF16)
    return hi, mid, lo


def rows3(a):
    return jnp.concatenate(split3(a), axis=0)


def fold3(a):
    n = a.shape[0] // 3
    return (a[2 * n :] + a[n : 2 * n]) + a[:n]


def self_products(total, r):
    total = fold3(total)
    return (total[:, 2 * r :] + total[:, r : 2 * r]) + total[:, :r]


def times(a, b):
    a_hi, a_mid, a_lo = (v.astype(F32) for v in split3(a))
    b_hi, b_mid, b_lo = split3(b)
    left = jnp.concatenate([a_lo, a_mid, a_hi, a_mid, a_hi, a_hi], axis=1).astype(BF16)
    return mm(left, jnp.concatenate([b_hi, b_mid, b_lo, b_hi, b_mid, b_hi], axis=0))


def eye_like(n):
    return (lax.broadcasted_iota(jnp.int32, (n, n), 0) == lax.broadcasted_iota(jnp.int32, (n, n), 1)).astype(F32)


def gram_schmidt_steps(state, steps):
    left, weights = state
    n = left.shape[0]
    row_id = lax.broadcasted_iota(jnp.int32, (n, 1), 0)
    for j in steps:
        column = jnp.broadcast_to(left[:, j : j + 1], (n, n))
        s = jnp.maximum(column[j : j + 1, :], 0.0)
        inverse = 1.0 / (s + EPS)
        c = (2.0 - s * inverse) * inverse
        f = jnp.where(row_id > j, column * c, 0.0)
        new_weights = weights - f * weights[j : j + 1, :]
        left = left - (f * (2.0 - c * s)) * left[j : j + 1, :]
        weights = new_weights
    return left, weights


def unit_weights(state):
    left, weights = state
    eye = eye_like(left.shape[0])
    s = jnp.maximum(jnp.sum(left * eye, axis=1, keepdims=True), 0.0)
    return weights / jnp.sqrt(s + EPS), eye * (s / (s + EPS))


def comm_kernel(
    geom, act, vg, w, err, rt_in, error_out, left_out, r_out, gi,
    rt, actr, vg_v, err_v, rtf, vgx, wbuf, outs, lacc, lf, rc, rxz, ysum, q1, q3, zout, zin, tz,
    local_sem, send_sem, recv_sem,
):
    nz, nx, nc, ny = geom
    nb = nc * nx * nz
    per = nx * nz
    _, tok, d = actr.shape
    r = rt.shape[0]
    wide = min(WIDE, per * BLK)
    wb = wide // BLK
    pieces = d // wide
    per_piece = per // wb
    dp, y = lax.axis_index("dp"), lax.axis_index("tp")
    c = lax.rem(dp, nc)
    x = lax.rem(lax.div(dp, nc), nx)
    z = lax.div(dp, nc * nx)
    k = c * nx + x
    mine = x * nz + z

    def shifted(i, by, n):
        return lax.rem(i + by, n)

    def device(zz, xx, cc, yy):
        return ((zz * nx + xx) * nc + cc, yy)

    y_peers = [(dy, shifted(y, dy, ny)) for dy in range(1, ny)]
    z_peers = [(dz, shifted(z, dz, nz)) for dz in range(1, nz)]
    x_peers = [(dx, shifted(x, dx, nx)) for dx in range(1, nx)]
    plane = [
        (shifted(x, dx, nx), shifted(z, dz, nz)) for dx in range(nx) for dz in range(nz) if (dx, dz) != (0, 0)
    ]
    group = [
        (shifted(x, dx, nx), shifted(c, dc, nc)) for dc in range(nc) for dx in range(nx) if (dc, dx) != (0, 0)
    ]
    cores = [shifted(c, dc, nc) for dc in range(1, nc)]
    up, down, across = shifted(y, 1, ny), shifted(y, ny - 1, ny), shifted(y, 2, ny)

    sent = []
    counter = [0, 0]

    def send(src, dst, to):
        i = counter[0]
        counter[0] += 1
        copy = pltpu.make_async_remote_copy(
            src_ref=src, dst_ref=dst, send_sem=send_sem.at[i], recv_sem=recv_sem.at[i], device_id=to, device_id_type=MESH
        )
        copy.start()
        sent.append(copy)
        return copy

    def fetch(src, dst):
        i = counter[1]
        counter[1] += 1
        copy = pltpu.make_async_copy(src, dst, local_sem.at[i])
        copy.start()
        return copy

    def wait_all(copies):
        for copy in copies:
            copy.wait_recv()

    def tokens(yy):
        return pl.ds(pl.multiple_of(yy * tok, tok), tok)

    def weight_rows(zz):
        return pl.ds(pl.multiple_of((k * nz + zz) * BLK, BLK), BLK)

    load_rt = fetch(rt_in, rt)
    load_vgx = fetch(vg.at[tokens(y)], vgx.at[k, y])
    share = d // 4
    load_err = [fetch(err.at[pl.ds(i * share, share)], err_v.at[pl.ds(i * share, share)]) for i in range(4)]
    load_act = fetch(act, actr.at[0])
    load_vg = [fetch(vg.at[tokens(yy)], vg_v.at[i]) for i, yy in enumerate((y, down, up, across))]
    load_w = [fetch(w.at[weight_rows(zz)], wbuf.at[zz, y]) for zz in range(nz)]

    barrier = pltpu.get_barrier_semaphore()
    everyone = (
        [device(z, xx, cc, y) for xx, cc in group]
        + [device(zz, shifted(x, dx, nx), c, y) for dx in range(nx) for _, zz in z_peers]
        + [device(z, x, cc, yy) for _, yy in y_peers for cc in [c] + cores]
    )
    for peer in everyone:
        pl.semaphore_signal(barrier, inc=1, device_id=peer, device_id_type=MESH)
    pl.semaphore_wait(barrier, len(everyone))

    recv_rt = [send(rt_in, rtf.at[y], device(z, x, c, yy)) for _, yy in y_peers]
    recv_vg = [send(vg.at[tokens(yy)], vgx.at[k, y], device(z, x, c, yy)) for _, yy in y_peers]
    half = CHUNKS // 2
    part = d // CHUNKS

    def cols(i):
        return pl.ds(i * part, part)

    from_down, from_up, from_across = {}, {}, {}

    def direct(*numbers):
        for i in numbers:
            j = (i + half) % CHUNKS
            from_down[i] = send(act.at[:, cols(i)], actr.at[1, :, cols(i)], device(z, x, c, up))
            from_up[j] = send(act.at[:, cols(j)], actr.at[2, :, cols(j)], device(z, x, c, down))

    def forward(*numbers):
        for i in numbers:
            from_down[i].wait_recv()
            from_across[i] = send(actr.at[1, :, cols(i)], actr.at[3, :, cols(i)], device(z, x, c, up))
            j = i + half
            from_up[j].wait_recv()
            from_across[j] = send(actr.at[2, :, cols(j)], actr.at[3, :, cols(j)], device(z, x, c, down))

    direct(0, 1, 2)

    load_rt.wait()
    rtf[y] = rt[...]
    rt3 = rows3(rt[...])

    def columns(p):
        return pl.ds(pl.multiple_of(p * wide, wide), wide)

    def store_left(value, cc, j0):
        for j in range(wb):
            lacc[cc, j0 + j] = value[:, j * BLK : (j + 1) * BLK]

    def load_left(ref, cc, j0):
        return jnp.concatenate([ref[cc, j0 + j] for j in range(wb)], axis=1)

    for load in load_err:
        load.wait()

    def err_left(p, carry):
        hi, lo = split2(err_v[columns(p), :])
        store_left(fold3(mm(rt3, lo, NT)) + fold3(mm(rt3, hi, NT)), lax.div(p, per_piece), lax.rem(p, per_piece) * wb)
        return carry

    lax.fori_loop(0, pieces, err_left, 0)

    wait_all(recv_rt)
    load_vgx.wait()
    wait_all(recv_vg)
    recv_vgx = [send(vgx.at[k], vgx.at[k], device(z, xx, c, y)) for _, xx in x_peers]
    relayed = [send(vgx.at[k], vgx.at[k], device(z, x, cc, y)) for cc in cores]
    ut = jnp.zeros((r, tok), F32)
    for yy in range(ny):
        ut = ut + fold3(mm(rows3(rtf[yy]), vgx[k, yy], NT))
    ut3 = rows3(ut)
    load_act.wait()

    def act_left(cc):
        def step(i, carry):
            value = fold3(mm(ut3, actr[0, :, columns(cc * per_piece + i)]))
            store_left(load_left(lacc, cc, i * wb) + value, cc, i * wb)
            return carry

        lax.fori_loop(0, per_piece, step, 0)

    recv = []
    for cc in cores:
        act_left(cc)
        recv.append(send(lacc.at[cc], rc, device(z, x, cc, y)))
    act_left(c)

    wait_all(recv)
    lacc[c] += rc[...]
    recv = [
        send(lacc.at[c, xx * nz + zz], rxz.at[i], device(zz, xx, c, y)) for i, (xx, zz) in enumerate(plane)
    ]
    direct(3)
    recv_w = [send(w.at[weight_rows(z)], wbuf.at[z, y], device(z, x, c, yy)) for _, yy in y_peers]
    wait_all(recv)
    total = lacc[c, mine]
    for i in range(len(plane)):
        total = total + rxz[i]
    ysum[y] = total
    own = ysum.at[y]
    recv = [send(own, own, device(z, x, c, yy)) for _, yy in y_peers]
    direct(4)
    wait_all(recv)
    total = ysum[0]
    for yy in range(1, ny):
        total = total + ysum[yy]
    lf[c, mine] = total
    own = lf.at[c, mine]
    recv = [send(own, own, device(zz, xx, c, y)) for xx, zz in plane]
    direct(5)
    wait_all(recv)
    own = lf.at[c]
    recv = [send(own, own, device(z, x, cc, y)) for cc in cores]

    for copy in load_w:
        copy.wait()
    recv_wz = []
    for copy, (dy, _) in zip(recv_w, y_peers):
        copy.wait_recv()
        source = shifted(y, ny - dy, ny)
        for _, zz in z_peers:
            recv_wz.append(send(wbuf.at[z, source], wbuf.at[z, source], device(zz, x, c, y)))
    for copy, (dx, _) in zip(recv_vgx, x_peers):
        copy.wait_recv()
        slot = c * nx + shifted(x, nx - dx, nx)
        relayed += [send(vgx.at[slot], vgx.at[slot], device(z, x, cc, y)) for cc in cores]
    direct(6)
    wait_all(recv)

    def products(p, carry):
        gram, by_act, by_err = carry
        block = rows3(load_left(lf, lax.div(p, per_piece), lax.rem(p, per_piece) * wb))
        hi, lo = split2(err_v[columns(p), :])
        by_act = by_act + mm(block, actr[0, :, columns(p)], NT)
        by_err = by_err + (mm(block, lo) + mm(block, hi))
        return gram + mm(block, block, NT), by_act, by_err

    gram, by_act, by_err = lax.fori_loop(
        0,
        pieces,
        products,
        (jnp.zeros((3 * r, 3 * r), F32), jnp.zeros((3 * r, tok), F32), jnp.zeros((3 * r, err_v.shape[1]), F32)),
    )
    by_act = rows3(fold3(by_act))
    for yy in range(ny):
        zout[yy] = fold3(mm(by_act, vgx[k, yy]))
    zout[y] += fold3(by_err)
    zin[c, y] = zout[y]
    recv = [
        send(zout.at[yy], zin.at[c, y], device(z, x, cc, yy))
        for yy, cc in [(yy, cc) for _, yy in y_peers for cc in [c] + cores] + [(y, cc) for cc in cores]
    ]
    direct(7)
    forward(0)

    state = self_products(gram, r), eye_like(r)
    state = gram_schmidt_steps(state, range(r // 2))
    wait_all(recv)
    total = None
    for cc in range(nc):
        for yy in range(ny):
            total = zin[cc, yy] if total is None else total + zin[cc, yy]
    tz[mine] = total
    own = tz.at[mine]
    recv = [send(own, own, device(zz, xx, c, y)) for xx, zz in plane]
    forward(1)
    state = gram_schmidt_steps(state, range(r // 2, r))
    weights, norms = unit_weights(state)

    def apply_first(p, total):
        block = times(weights, load_left(lf, lax.div(p, per_piece), lax.rem(p, per_piece) * wb))
        q1[p] = block
        block = rows3(block)
        return total + mm(block, block, NT)

    off = self_products(lax.fori_loop(0, pieces, apply_first, jnp.zeros((3 * r, 3 * r), F32)), r) - norms
    row_id = lax.broadcasted_iota(jnp.int32, (r, r), 0)
    col_id = lax.broadcasted_iota(jnp.int32, (r, r), 1)
    again = jnp.where(col_id < row_id, off, jnp.where(col_id == row_id, 0.5 * off, 0.0))
    weights = weights - times(again, weights)
    scale = math.sqrt(float(d))

    def apply_second(p, carry):
        block = q1[p]
        block = block - times(again, block)
        left_out[:, columns(p)] = block * scale
        hi, lo = split2(block)
        q3[p] = jnp.concatenate([hi, lo, hi], axis=0)
        return carry

    lax.fori_loop(0, pieces, apply_second, 0)
    forward(2)

    wait_all(recv_wz)
    wait_all(relayed)
    xc = nc * nx
    many = min(4, xc)

    def input_grad(i, carry):
        zz, g = lax.div(i, xc // many), lax.rem(i, xc // many)
        total = None
        for yy in range(ny):
            cotangent = vgx[pl.ds(g * many, many), yy].reshape(many * tok, BLK)
            piece = mm(cotangent, wbuf[zz, yy], NT).astype(BF16).astype(F32)
            total = piece if total is None else total + piece
        outs[zz, pl.ds(g * many, many)] = total.astype(BF16).reshape(many, tok, BLK)
        return carry

    lax.fori_loop(0, nz * xc // many, input_grad, 0)

    def place(zz):
        return gi.at[:, pl.ds(pl.multiple_of((k * nz + zz) * BLK, BLK), BLK)]

    sent_out = [
        send(outs.at[zz, cc * nx + xx], place(zz), device(z, xx, cc, y)) for xx, cc in group for zz in range(nz)
    ]
    kept_out = [fetch(outs.at[zz, k], place(zz)) for zz in range(nz)]
    forward(3)

    wait_all(recv)
    total = tz[0]
    for i in range(1, per):
        total = total + tz[i]
    right = times(weights, total) / float(nb)
    r_out[...] = right
    hi, lo = split2(right)
    right3 = jnp.concatenate([hi, hi, lo], axis=0)

    for load in load_vg:
        load.wait()
    for i in range(CHUNKS):
        if i >= half:
            from_down[i].wait_recv()
        else:
            from_up[i].wait_recv()
    near = vg_v[0:3].reshape(3 * tok, BLK)
    far = vg_v[3]

    def error_near(i, carry):
        at = pl.ds(pl.multiple_of(i * BLK, BLK), BLK)
        block = actr[0:3, :, at].reshape(3 * tok, BLK)
        inside = pl.ds(pl.multiple_of(lax.rem(i, wb) * BLK, BLK), BLK)
        approx = mm(q3[lax.div(i, wb), :, inside], right3, TN)
        error_out[at, :] = (err_v[at, :] - approx) + mm(block, near, TN)
        return carry

    lax.fori_loop(0, nb, error_near, 0)

    def error_far(i, carry):
        at = pl.ds(pl.multiple_of(i * BLK, BLK), BLK)
        error_out[at, :] += mm(actr[3, :, at], far, TN)
        return carry

    for i in range(half):
        for j in (i, i + half):
            from_across[j].wait_recv()
            lax.fori_loop(j * part // BLK, (j + 1) * part // BLK, error_far, 0)

    wait_all(sent_out)
    for copy in kept_out:
        copy.wait()
    for copy in sent:
        copy.wait_send()


def store_kernel(error_in, left_in, right_in, gi_in, error_out, left_out, right_out, gi_out, sem):
    n = 8
    rows = error_in.shape[0] // n
    pairs = [(error_in.at[pl.ds(i * rows, rows)], error_out.at[pl.ds(i * rows, rows)]) for i in range(n)]
    pairs += [(left_in, left_out), (right_in, right_out), (gi_in, gi_out)]
    copies = [pltpu.make_async_copy(a, b, sem.at[i]) for i, (a, b) in enumerate(pairs)]
    for copy in copies:
        copy.start()
    for copy in copies:
        copy.wait()


def build(geom):
    nz, nx, nc, ny = geom

    def body(act, vg, w, err, right_prev):
        tok, d = act.shape
        kv = vg.shape[1]
        r = right_prev.shape[1]
        nb = nc * nx * nz
        per = nx * nz
        wide = min(WIDE, per * BLK)
        assert d == nb * BLK and kv == BLK and per * BLK % wide == 0
        xc = nx * nc
        sends = (
            4 * (ny - 1) + 3 * CHUNKS + (nx - 1) + nx * (nc - 1) + (xc - 1) * nz + (ny - 1) * (nz - 1)
            + 3 * (per - 1) + 2 * (nc - 1) + (ny * nc - 1)
        )
        inputs = [
            pltpu.with_memory_space_constraint(a, pltpu.HBM) for a in (act, vg, w, err[0], right_prev.T)
        ]
        hbm = pl.BlockSpec(memory_space=pltpu.HBM)
        vmem = pl.BlockSpec(memory_space=pltpu.VMEM)
        anywhere = pl.BlockSpec(memory_space=pl.ANY)
        results = (((d, kv), F32), ((r, d), F32), ((r, kv), F32), ((tok, d), BF16))
        made = pl.pallas_call(
            functools.partial(comm_kernel, geom),
            out_shape=tuple(pltpu.VMEM(*shape) for shape in results),
            in_specs=[hbm] * 5,
            out_specs=(vmem,) * 4,
            scratch_shapes=[
                pltpu.VMEM((r, kv), F32),
                pltpu.VMEM((ny, tok, d), BF16),
                pltpu.VMEM((ny, tok, kv), BF16),
                pltpu.VMEM((d, kv), F32),
                pltpu.VMEM((ny, r, kv), F32),
                pltpu.VMEM((xc, ny, tok, kv), BF16),
                pltpu.VMEM((nz, ny, BLK, kv), BF16),
                pltpu.VMEM((nz, xc, tok, BLK), BF16),
                pltpu.VMEM((nc, per, r, BLK), F32),
                pltpu.VMEM((nc, per, r, BLK), F32),
                pltpu.VMEM((per, r, BLK), F32),
                pltpu.VMEM((per - 1, r, BLK), F32),
                pltpu.VMEM((ny, r, BLK), F32),
                pltpu.VMEM((d // wide, r, wide), F32),
                pltpu.VMEM((d // wide, 3 * r, wide), BF16),
                pltpu.VMEM((ny, r, kv), F32),
                pltpu.VMEM((nc, ny, r, kv), F32),
                pltpu.VMEM((per, r, kv), F32),
                pltpu.SemaphoreType.DMA((1 + 1 + 4 + 1 + ny + 2 * nz,)),
                pltpu.SemaphoreType.DMA((sends,)),
                pltpu.SemaphoreType.DMA((sends,)),
            ],
            compiler_params=pltpu.CompilerParams(
                collective_id=0, has_side_effects=True, vmem_limit_bytes=44 * MIB
            ),
        )(*inputs)

        error_next, left, right, grad_input = pl.pallas_call(
            store_kernel,
            out_shape=tuple(jax.ShapeDtypeStruct(*shape) for shape in results),
            in_specs=[anywhere] * 4,
            out_specs=(anywhere,) * 4,
            scratch_shapes=[pltpu.SemaphoreType.DMA((11,))],
            compiler_params=pltpu.CompilerParams(vmem_limit_bytes=4 * MIB),
        )(*made)
        return (grad_input, error_next[None], left.T, right.T)

    return body


def solution(mesh):
    return jax.shard_map(
        build((4, 4, 2, 4)),
        mesh=mesh,
        in_specs=(
            P(("dp", "tp"), None),
            P("dp", "tp"),
            P(None, "tp"),
            P("dp", None, "tp"),
            P("tp", None),
        ),
        out_specs=(P(("dp", "tp"), None), P("dp", None, "tp"), P(), P("tp", None)),
        check_vma=False,
    )
```

time: 127 us -> 110 us (0.87)
  Pallas kernels: 127 us -> 109 us
    pallas_call x2, Pallas kernels: 127 us -> 109 us  [the longest x1 104 us: body(): pl.pallas_call(functools.partial(comm_kernel, geom), out_shape=tuple((plt...]
where the time goes in v4:
time: 110 us; the launch traced here: 109 us
  Pallas kernels  109 us (99%)
    pallas_call x1, Pallas kernels, body(): pl.pallas_call(functools.partial(comm_kernel, geom), out_shape=tuple((plt...  104 us
    pallas_call x1, Pallas kernels, body(): pl.pallas_call(store_kernel, out_shape=tuple((jax.ShapeDtypeStruct(*shape...  4.39 us

profile of v4, /device:TPU:1, one launch (start us, length us, event | category | flops | bytes accessed | tf_op | source)
XLA Modules:
  0.0 109.4 jit_solution(11394196611353266095)
XLA Ops:
  0.6 104.4 %shard_map.84 = (f32[8192,256]{1,0:T(8,128)S(1)}, f32[32,8192]{1,0:T(8,128)S(1)}, f32[32,256]{1,0:T(8,128)S(1)}, bf16[128,8192]{1,0:T(8,128)(2,1)S(1)}) custom-call(bf16[128,8192]{1,0:T(8,128)(2,1)} %act.1, bf16[512,256]{1,0:T(8,128)(2,1)} %vg.1, bf16[8192,256]{1,0:T(8,128)(2,1)} %w.1, f32[8192,256]{1,0:T(8,128)} %bitcast.5, f32[32,256]{1,0:T(8,128)} %bitcast.6), custom_call_target="tpu_custom_call" | custom-call | tf_op jit(solution)/shard_map/pallas_call | solution.py:465
  105.1 4.4 %shard_map.85 = (f32[8192,256]{1,0:T(8,128)}, f32[32,8192]{1,0:T(8,128)}, f32[32,256]{1,0:T(8,128)}, bf16[128,8192]{1,0:T(8,128)(2,1)}) custom-call(f32[8192,256]{1,0:T(8,128)S(1)} %get-tuple-element.12.error_in, f32[32,8192]{1,0:T(8,128)S(1)} %get-tuple-element.13.left_in, f32[32,256]{1,0:T(8,128)S(1)} %get-tuple-element.14.right_in, ...), custom_call_target="tpu_custom_call" | custom-call | tf_op jit(solution)/shard_map/pallas_call | solution.py:498

commit v5 on v4

--- a/solution.py
+++ b/solution.py
@@ -48,6 +48,15 @@
     return (a[2 * n :] + a[n : 2 * n]) + a[:n]
 
 
+def rows2(a):
+    return jnp.concatenate(split2(a), axis=0)
+
+
+def fold2(a):
+    n = a.shape[0] // 2
+    return a[n:] + a[:n]
+
+
 def self_products(total, r):
     total = fold3(total)
     return (total[:, 2 * r :] + total[:, r : 2 * r]) + total[:, :r]
@@ -64,19 +73,31 @@
     return (lax.broadcasted_iota(jnp.int32, (n, n), 0) == lax.broadcasted_iota(jnp.int32, (n, n), 1)).astype(F32)
 
 
-def gram_schmidt_steps(state, steps):
-    left, weights = state
-    n = left.shape[0]
+def gram_schmidt(gram):
+    n = gram.shape[0]
+    left, weights = gram, eye_like(n)
     row_id = lax.broadcasted_iota(jnp.int32, (n, 1), 0)
-    for j in steps:
-        column = jnp.broadcast_to(left[:, j : j + 1], (n, n))
-        s = jnp.maximum(column[j : j + 1, :], 0.0)
-        inverse = 1.0 / (s + EPS)
-        c = (2.0 - s * inverse) * inverse
-        f = jnp.where(row_id > j, column * c, 0.0)
-        new_weights = weights - f * weights[j : j + 1, :]
-        left = left - (f * (2.0 - c * s)) * left[j : j + 1, :]
-        weights = new_weights
+    m = 4
+    for j in range(0, n, m):
+        columns = [jnp.broadcast_to(left[:, i : i + 1], (n, n)) for i in range(j, j + m)]
+        rows = [left[i : i + 1, :] for i in range(j, j + m)]
+        given = [weights[i : i + 1, :] for i in range(j, j + m)]
+        off_left, off_weights = jnp.zeros((n, n), F32), jnp.zeros((n, n), F32)
+        for i in range(m):
+            at = j + i
+            s = jnp.maximum(columns[i][at : at + 1, :], 0.0)
+            inverse = 1.0 / (s + EPS)
+            c = (2.0 - s * inverse) * inverse
+            f = jnp.where(row_id > at, columns[i] * c, 0.0)
+            h = f * (2.0 - c * s)
+            for later in range(i + 1, m):
+                to = j + later
+                columns[later] = columns[later] - h * columns[later][at : at + 1, :]
+                rows[later] = rows[later] - h[to : to + 1, :] * rows[i]
+                given[later] = given[later] - f[to : to + 1, :] * given[i]
+            off_left = off_left + h * rows[i]
+            off_weights = off_weights + f * given[i]
+        left, weights = left - off_left, weights - off_weights
     return left, weights
 
 
@@ -176,6 +197,7 @@
 
     recv_rt = [send(rt_in, rtf.at[y], device(z, x, c, yy)) for _, yy in y_peers]
     recv_vg = [send(vg.at[tokens(yy)], vgx.at[k, y], device(z, x, c, yy)) for _, yy in y_peers]
+    recv_w = [send(w.at[weight_rows(z)], wbuf.at[z, y], device(z, x, c, yy)) for _, yy in y_peers]
     half = CHUNKS // 2
     part = d // CHUNKS
 
@@ -202,7 +224,7 @@
 
     load_rt.wait()
     rtf[y] = rt[...]
-    rt3 = rows3(rt[...])
+    rt2 = rows2(rt[...])
 
     def columns(p):
         return pl.ds(pl.multiple_of(p * wide, wide), wide)
@@ -219,7 +241,7 @@
 
     def err_left(p, carry):
         hi, lo = split2(err_v[columns(p), :])
-        store_left(fold3(mm(rt3, lo, NT)) + fold3(mm(rt3, hi, NT)), lax.div(p, per_piece), lax.rem(p, per_piece) * wb)
+        store_left(fold2(mm(rt2, lo, NT) + mm(rt2, hi, NT)), lax.div(p, per_piece), lax.rem(p, per_piece) * wb)
         return carry
 
     lax.fori_loop(0, pieces, err_left, 0)
@@ -255,27 +277,6 @@
         send(lacc.at[c, xx * nz + zz], rxz.at[i], device(zz, xx, c, y)) for i, (xx, zz) in enumerate(plane)
     ]
     direct(3)
-    recv_w = [send(w.at[weight_rows(z)], wbuf.at[z, y], device(z, x, c, yy)) for _, yy in y_peers]
-    wait_all(recv)
-    total = lacc[c, mine]
-    for i in range(len(plane)):
-        total = total + rxz[i]
-    ysum[y] = total
-    own = ysum.at[y]
-    recv = [send(own, own, device(z, x, c, yy)) for _, yy in y_peers]
-    direct(4)
-    wait_all(recv)
-    total = ysum[0]
-    for yy in range(1, ny):
-        total = total + ysum[yy]
-    lf[c, mine] = total
-    own = lf.at[c, mine]
-    recv = [send(own, own, device(zz, xx, c, y)) for xx, zz in plane]
-    direct(5)
-    wait_all(recv)
-    own = lf.at[c]
-    recv = [send(own, own, device(z, x, cc, y)) for cc in cores]
-
     for copy in load_w:
         copy.wait()
     recv_wz = []
@@ -284,6 +285,26 @@
         source = shifted(y, ny - dy, ny)
         for _, zz in z_peers:
             recv_wz.append(send(wbuf.at[z, source], wbuf.at[z, source], device(zz, x, c, y)))
+    wait_all(recv)
+    total = lacc[c, mine]
+    for i in range(len(plane)):
+        total = total + rxz[i]
+    ysum[y] = total
+    own = ysum.at[y]
+    recv = [send(own, own, device(z, x, c, yy)) for _, yy in y_peers]
+    direct(4)
+    wait_all(recv)
+    total = ysum[0]
+    for yy in range(1, ny):
+        total = total + ysum[yy]
+    lf[c, mine] = total
+    own = lf.at[c, mine]
+    recv = [send(own, own, device(zz, xx, c, y)) for xx, zz in plane]
+    direct(5)
+    wait_all(recv)
+    own = lf.at[c]
+    recv = [send(own, own, device(z, x, cc, y)) for cc in cores]
+
     for copy, (dx, _) in zip(recv_vgx, x_peers):
         copy.wait_recv()
         slot = c * nx + shifted(x, nx - dx, nx)
@@ -295,20 +316,21 @@
         gram, by_act, by_err = carry
         block = rows3(load_left(lf, lax.div(p, per_piece), lax.rem(p, per_piece) * wb))
         hi, lo = split2(err_v[columns(p), :])
-        by_act = by_act + mm(block, actr[0, :, columns(p)], NT)
-        by_err = by_err + (mm(block, lo) + mm(block, hi))
+        top = block[: 2 * r]
+        by_act = by_act + mm(top, actr[0, :, columns(p)], NT)
+        by_err = by_err + (mm(top, lo) + mm(top, hi))
         return gram + mm(block, block, NT), by_act, by_err
 
     gram, by_act, by_err = lax.fori_loop(
         0,
         pieces,
         products,
-        (jnp.zeros((3 * r, 3 * r), F32), jnp.zeros((3 * r, tok), F32), jnp.zeros((3 * r, err_v.shape[1]), F32)),
+        (jnp.zeros((3 * r, 3 * r), F32), jnp.zeros((2 * r, tok), F32), jnp.zeros((2 * r, err_v.shape[1]), F32)),
     )
-    by_act = rows3(fold3(by_act))
+    by_act = rows3(fold2(by_act))
     for yy in range(ny):
         zout[yy] = fold3(mm(by_act, vgx[k, yy]))
-    zout[y] += fold3(by_err)
+    zout[y] += fold2(by_err)
     zin[c, y] = zout[y]
     recv = [
         send(zout.at[yy], zin.at[c, y], device(z, x, cc, yy))
@@ -317,8 +339,30 @@
     direct(7)
     forward(0)
 
-    state = self_products(gram, r), eye_like(r)
-    state = gram_schmidt_steps(state, range(r // 2))
+    wait_all(recv_wz)
+    wait_all(relayed)
+    xc = nc * nx
+    many = min(4, xc)
+
+    def place(zz):
+        return gi.at[:, pl.ds(pl.multiple_of((k * nz + zz) * BLK, BLK), BLK)]
+
+    sent_out, kept_out = [], []
+    for zz in range(nz):
+
+        def input_grad(g, carry, zz=zz):
+            total = None
+            for yy in range(ny):
+                cotangent = vgx[pl.ds(g * many, many), yy].reshape(many * tok, BLK)
+                piece = mm(cotangent, wbuf[zz, yy], NT).astype(BF16).astype(F32)
+                total = piece if total is None else total + piece
+            outs[zz, pl.ds(g * many, many)] = total.astype(BF16).reshape(many, tok, BLK)
+            return carry
+
+        lax.fori_loop(0, xc // many, input_grad, 0)
+        sent_out += [send(outs.at[zz, cc * nx + xx], place(zz), device(z, xx, cc, y)) for xx, cc in group]
+        kept_out.append(fetch(outs.at[zz, k], place(zz)))
+
     wait_all(recv)
     total = None
     for cc in range(nc):
@@ -328,8 +372,7 @@
     own = tz.at[mine]
     recv = [send(own, own, device(zz, xx, c, y)) for xx, zz in plane]
     forward(1)
-    state = gram_schmidt_steps(state, range(r // 2, r))
-    weights, norms = unit_weights(state)
+    weights, norms = unit_weights(gram_schmidt(self_products(gram, r)))
 
     def apply_first(p, total):
         block = times(weights, load_left(lf, lax.div(p, per_piece), lax.rem(p, per_piece) * wb))
@@ -355,30 +398,6 @@
     lax.fori_loop(0, pieces, apply_second, 0)
     forward(2)
 
-    wait_all(recv_wz)
-    wait_all(relayed)
-    xc = nc * nx
-    many = min(4, xc)
-
-    def input_grad(i, carry):
-        zz, g = lax.div(i, xc // many), lax.rem(i, xc // many)
-        total = None
-        for yy in range(ny):
-            cotangent = vgx[pl.ds(g * many, many), yy].reshape(many * tok, BLK)
-            piece = mm(cotangent, wbuf[zz, yy], NT).astype(BF16).astype(F32)
-            total = piece if total is None else total + piece
-        outs[zz, pl.ds(g * many, many)] = total.astype(BF16).reshape(many, tok, BLK)
-        return carry
-
-    lax.fori_loop(0, nz * xc // many, input_grad, 0)
-
-    def place(zz):
-        return gi.at[:, pl.ds(pl.multiple_of((k * nz + zz) * BLK, BLK), BLK)]
-
-    sent_out = [
-        send(outs.at[zz, cc * nx + xx], place(zz), device(z, xx, cc, y)) for xx, cc in group for zz in range(nz)
-    ]
-    kept_out = [fetch(outs.at[zz, k], place(zz)) for zz in range(nz)]
     forward(3)
 
     wait_all(recv)
@@ -388,7 +407,8 @@
     right = times(weights, total) / float(nb)
     r_out[...] = right
     hi, lo = split2(right)
-    right3 = jnp.concatenate([hi, hi, lo], axis=0)
+    hi, lo = hi.astype(F32), lo.astype(F32)
+    low_rank = jnp.concatenate([hi, hi, lo], axis=0).T.astype(BF16)
 
     for load in load_vg:
         load.wait()
@@ -397,28 +417,19 @@
             from_down[i].wait_recv()
         else:
             from_up[i].wait_recv()
-    near = vg_v[0:3].reshape(3 * tok, BLK)
-    far = vg_v[3]
-
-    def error_near(i, carry):
+    cotangent = vg_v[...].reshape(ny * tok, BLK).astype(F32).T.astype(BF16)
+
+    def new_error(i, carry):
         at = pl.ds(pl.multiple_of(i * BLK, BLK), BLK)
-        block = actr[0:3, :, at].reshape(3 * tok, BLK)
         inside = pl.ds(pl.multiple_of(lax.rem(i, wb) * BLK, BLK), BLK)
-        approx = mm(q3[lax.div(i, wb), :, inside], right3, TN)
-        error_out[at, :] = (err_v[at, :] - approx) + mm(block, near, TN)
-        return carry
-
-    lax.fori_loop(0, nb, error_near, 0)
-
-    def error_far(i, carry):
-        at = pl.ds(pl.multiple_of(i * BLK, BLK), BLK)
-        error_out[at, :] += mm(actr[3, :, at], far, TN)
+        block = mm(cotangent, actr[:, :, at].reshape(ny * tok, BLK)) - mm(low_rank, q3[lax.div(i, wb), :, inside])
+        error_out[at, :] = err_v[at, :] + block.T
         return carry
 
     for i in range(half):
         for j in (i, i + half):
             from_across[j].wait_recv()
-            lax.fori_loop(j * part // BLK, (j + 1) * part // BLK, error_far, 0)
+            lax.fori_loop(j * part // BLK, (j + 1) * part // BLK, new_error, 0)
 
     wait_all(sent_out)
     for copy in kept_out:

time: 110 us -> 110 us (level)
  no operation moved by 1% of the time
where the time goes in v5:
time: 110 us
  Pallas kernels  109 us (99%)
    pallas_call x1, Pallas kernels, body(): pl.pallas_call(functools.partial(comm_kernel, geom), out_shape=tuple((plt...  105 us
    pallas_call x1, Pallas kernels, body(): pl.pallas_call(store_kernel, out_shape=tuple((jax.ShapeDtypeStruct(*shape...  4.39 us

profile of v5, /device:TPU:1, one launch (start us, length us, event | category | flops | bytes accessed | tf_op | source)
XLA Modules:
  0.0 109.9 jit_solution(10383972059357372337)
XLA Ops:
  0.6 104.9 %shard_map.84 = (f32[8192,256]{1,0:T(8,128)S(1)}, f32[32,8192]{1,0:T(8,128)S(1)}, f32[32,256]{1,0:T(8,128)S(1)}, bf16[128,8192]{1,0:T(8,128)(2,1)S(1)}) custom-call(bf16[128,8192]{1,0:T(8,128)(2,1)} %act.1, bf16[512,256]{1,0:T(8,128)(2,1)} %vg.1, bf16[8192,256]{1,0:T(8,128)(2,1)} %w.1, f32[8192,256]{1,0:T(8,128)} %bitcast.5, f32[32,256]{1,0:T(8,128)} %bitcast.6), custom_call_target="tpu_custom_call" | custom-call | tf_op jit(solution)/shard_map/pallas_call | solution.py:476
  105.5 4.4 %shard_map.85 = (f32[8192,256]{1,0:T(8,128)}, f32[32,8192]{1,0:T(8,128)}, f32[32,256]{1,0:T(8,128)}, bf16[128,8192]{1,0:T(8,128)(2,1)}) custom-call(f32[8192,256]{1,0:T(8,128)S(1)} %get-tuple-element.12.error_in, f32[32,8192]{1,0:T(8,128)S(1)} %get-tuple-element.13.left_in, f32[32,256]{1,0:T(8,128)S(1)} %get-tuple-element.14.right_in, ...), custom_call_target="tpu_custom_call" | custom-call | tf_op jit(solution)/shard_map/pallas_call | solution.py:509

commit v6 on v5

--- a/solution.py
+++ b/solution.py
@@ -110,13 +110,15 @@
 
 def comm_kernel(
     geom, act, vg, w, err, rt_in, error_out, left_out, r_out, gi,
-    rt, actr, vg_v, err_v, rtf, vgx, wbuf, outs, lacc, lf, rc, rxz, ysum, q1, q3, zout, zin, tz,
+    rt, actr, vg_v, err_v, uout, uin, vgx, wbuf, outs, lacc, lf, rc, rxz, ysum, q1, q3, zout, zin, zsum, tz,
     local_sem, send_sem, recv_sem,
 ):
     nz, nx, nc, ny = geom
     nb = nc * nx * nz
     per = nx * nz
-    _, tok, d = actr.shape
+    _, _, tok, part = actr.shape
+    d = part * CHUNKS
+    half = CHUNKS // 2
     r = rt.shape[0]
     wide = min(WIDE, per * BLK)
     wb = wide // BLK
@@ -178,53 +180,59 @@
         return pl.ds(pl.multiple_of((k * nz + zz) * BLK, BLK), BLK)
 
     load_rt = fetch(rt_in, rt)
+    load_vg = [fetch(vg.at[tokens(yy)], vg_v.at[i]) for i, yy in enumerate((y, up, across, down))]
     load_vgx = fetch(vg.at[tokens(y)], vgx.at[k, y])
+    load_act = [fetch(act.at[:, pl.ds(i * part, part)], actr.at[0, i]) for i in range(CHUNKS)]
     share = d // 4
     load_err = [fetch(err.at[pl.ds(i * share, share)], err_v.at[pl.ds(i * share, share)]) for i in range(4)]
-    load_act = fetch(act, actr.at[0])
-    load_vg = [fetch(vg.at[tokens(yy)], vg_v.at[i]) for i, yy in enumerate((y, down, up, across))]
     load_w = [fetch(w.at[weight_rows(zz)], wbuf.at[zz, y]) for zz in range(nz)]
 
     barrier = pltpu.get_barrier_semaphore()
     everyone = (
         [device(z, xx, cc, y) for xx, cc in group]
         + [device(zz, shifted(x, dx, nx), c, y) for dx in range(nx) for _, zz in z_peers]
-        + [device(z, x, cc, yy) for _, yy in y_peers for cc in [c] + cores]
+        + [device(z, x, c, yy) for _, yy in y_peers]
     )
     for peer in everyone:
         pl.semaphore_signal(barrier, inc=1, device_id=peer, device_id_type=MESH)
     pl.semaphore_wait(barrier, len(everyone))
 
-    recv_rt = [send(rt_in, rtf.at[y], device(z, x, c, yy)) for _, yy in y_peers]
-    recv_vg = [send(vg.at[tokens(yy)], vgx.at[k, y], device(z, x, c, yy)) for _, yy in y_peers]
-    recv_w = [send(w.at[weight_rows(z)], wbuf.at[z, y], device(z, x, c, yy)) for _, yy in y_peers]
-    half = CHUNKS // 2
-    part = d // CHUNKS
-
-    def cols(i):
-        return pl.ds(i * part, part)
+    load_rt.wait()
+    rt3 = rows3(rt[...])
+    for load in load_vg:
+        load.wait()
+    for dy in range(ny):
+        uout[dy] = fold3(mm(rt3, vg_v[dy], NT))
+    recv_u = [send(uout.at[dy], uin.at[dy - 1], device(z, x, c, yy)) for dy, yy in y_peers]
 
     from_down, from_up, from_across = {}, {}, {}
 
     def direct(*numbers):
         for i in numbers:
             j = (i + half) % CHUNKS
-            from_down[i] = send(act.at[:, cols(i)], actr.at[1, :, cols(i)], device(z, x, c, up))
-            from_up[j] = send(act.at[:, cols(j)], actr.at[2, :, cols(j)], device(z, x, c, down))
+            for piece in (i, j):
+                if piece in load_act:
+                    load_act.pop(piece).wait()
+            from_down[i] = send(actr.at[0, i], actr.at[3, i], device(z, x, c, up))
+            from_up[j] = send(actr.at[0, j], actr.at[1, j], device(z, x, c, down))
 
     def forward(*numbers):
         for i in numbers:
             from_down[i].wait_recv()
-            from_across[i] = send(actr.at[1, :, cols(i)], actr.at[3, :, cols(i)], device(z, x, c, up))
+            from_across[i] = send(actr.at[3, i], actr.at[2, i], device(z, x, c, up))
             j = i + half
             from_up[j].wait_recv()
-            from_across[j] = send(actr.at[2, :, cols(j)], actr.at[3, :, cols(j)], device(z, x, c, down))
-
-    direct(0, 1, 2)
-
-    load_rt.wait()
-    rtf[y] = rt[...]
-    rt2 = rows2(rt[...])
+            from_across[j] = send(actr.at[1, j], actr.at[2, j], device(z, x, c, down))
+
+    load_act = dict(enumerate(load_act))
+    direct(0)
+    recv_vg = [send(vg.at[tokens(yy)], vgx.at[k, y], device(z, x, c, yy)) for _, yy in y_peers]
+    own_w = w.at[weight_rows(z)]
+    w_from_down = send(own_w, wbuf.at[z, y], device(z, x, c, up))
+    w_from_up = send(own_w, wbuf.at[z, y], device(z, x, c, down))
+    direct(1, 2)
+
+    rt2 = rt3[: 2 * r]
 
     def columns(p):
         return pl.ds(pl.multiple_of(p * wide, wide), wide)
@@ -246,20 +254,26 @@
 
     lax.fori_loop(0, pieces, err_left, 0)
 
-    wait_all(recv_rt)
-    load_vgx.wait()
-    wait_all(recv_vg)
-    recv_vgx = [send(vgx.at[k], vgx.at[k], device(z, xx, c, y)) for _, xx in x_peers]
-    relayed = [send(vgx.at[k], vgx.at[k], device(z, x, cc, y)) for cc in cores]
-    ut = jnp.zeros((r, tok), F32)
-    for yy in range(ny):
-        ut = ut + fold3(mm(rows3(rtf[yy]), vgx[k, yy], NT))
+    wait_all(recv_u)
+    ut = uout[0]
+    for dy in range(ny - 1):
+        ut = ut + uin[dy]
     ut3 = rows3(ut)
-    load_act.wait()
+    for load in load_act.values():
+        load.wait()
+    load_act = {}
+
+    def own_act(p):
+        n = wide // part
+        if n >= 1:
+            return jnp.concatenate([actr[0, p * n + i] for i in range(n)], axis=1)
+        n = part // wide
+        inside = pl.ds(pl.multiple_of(lax.rem(p, n) * wide, wide), wide)
+        return actr[0, lax.div(p, n), :, inside]
 
     def act_left(cc):
         def step(i, carry):
-            value = fold3(mm(ut3, actr[0, :, columns(cc * per_piece + i)]))
+            value = fold3(mm(ut3, own_act(cc * per_piece + i)))
             store_left(load_left(lacc, cc, i * wb) + value, cc, i * wb)
             return carry
 
@@ -277,14 +291,26 @@
         send(lacc.at[c, xx * nz + zz], rxz.at[i], device(zz, xx, c, y)) for i, (xx, zz) in enumerate(plane)
     ]
     direct(3)
+
+    load_vgx.wait()
+    wait_all(recv_vg)
+    recv_vgx = [send(vgx.at[k], vgx.at[k], device(z, xx, c, y)) for _, xx in x_peers]
+    relayed = [send(vgx.at[k], vgx.at[k], device(z, x, cc, y)) for cc in cores]
     for copy in load_w:
         copy.wait()
+    first, second = pl.ds(0, BLK // 2), pl.ds(BLK // 2, BLK // 2)
+    w_from_down.wait_recv()
+    w_halves = [send(wbuf.at[z, down, first], wbuf.at[z, down, first], device(z, x, c, up))]
+    w_from_up.wait_recv()
+    w_halves.append(send(wbuf.at[z, up, second], wbuf.at[z, up, second], device(z, x, c, down)))
     recv_wz = []
-    for copy, (dy, _) in zip(recv_w, y_peers):
-        copy.wait_recv()
-        source = shifted(y, ny - dy, ny)
+
+    def weights_on(source):
         for _, zz in z_peers:
             recv_wz.append(send(wbuf.at[z, source], wbuf.at[z, source], device(zz, x, c, y)))
+
+    weights_on(down)
+    weights_on(up)
     wait_all(recv)
     total = lacc[c, mine]
     for i in range(len(plane)):
@@ -293,6 +319,8 @@
     own = ysum.at[y]
     recv = [send(own, own, device(z, x, c, yy)) for _, yy in y_peers]
     direct(4)
+    wait_all(w_halves)
+    weights_on(across)
     wait_all(recv)
     total = ysum[0]
     for yy in range(1, ny):
@@ -317,7 +345,7 @@
         block = rows3(load_left(lf, lax.div(p, per_piece), lax.rem(p, per_piece) * wb))
         hi, lo = split2(err_v[columns(p), :])
         top = block[: 2 * r]
-        by_act = by_act + mm(top, actr[0, :, columns(p)], NT)
+        by_act = by_act + mm(top, own_act(p), NT)
         by_err = by_err + (mm(top, lo) + mm(top, hi))
         return gram + mm(block, block, NT), by_act, by_err
 
@@ -331,11 +359,7 @@
     for yy in range(ny):
         zout[yy] = fold3(mm(by_act, vgx[k, yy]))
     zout[y] += fold2(by_err)
-    zin[c, y] = zout[y]
-    recv = [
-        send(zout.at[yy], zin.at[c, y], device(z, x, cc, yy))
-        for yy, cc in [(yy, cc) for _, yy in y_peers for cc in [c] + cores] + [(y, cc) for cc in cores]
-    ]
+    recv = [send(zout.at[yy], zin.at[dy - 1], device(z, x, c, yy)) for dy, yy in y_peers]
     direct(7)
     forward(0)
 
@@ -364,14 +388,18 @@
         kept_out.append(fetch(outs.at[zz, k], place(zz)))
 
     wait_all(recv)
-    total = None
-    for cc in range(nc):
-        for yy in range(ny):
-            total = zin[cc, yy] if total is None else total + zin[cc, yy]
+    total = zout[y]
+    for dy in range(ny - 1):
+        total = total + zin[dy]
+    zsum[0] = total
+    recv = [send(zsum.at[0], zsum.at[dc], device(z, x, cc, y)) for dc, cc in enumerate(cores, 1)]
+    forward(1)
+    wait_all(recv)
+    for dc in range(1, nc):
+        total = total + zsum[dc]
     tz[mine] = total
     own = tz.at[mine]
     recv = [send(own, own, device(zz, xx, c, y)) for xx, zz in plane]
-    forward(1)
     weights, norms = unit_weights(gram_schmidt(self_products(gram, r)))
 
     def apply_first(p, total):
@@ -410,8 +438,6 @@
     hi, lo = hi.astype(F32), lo.astype(F32)
     low_rank = jnp.concatenate([hi, hi, lo], axis=0).T.astype(BF16)
 
-    for load in load_vg:
-        load.wait()
     for i in range(CHUNKS):
         if i >= half:
             from_down[i].wait_recv()
@@ -422,7 +448,10 @@
     def new_error(i, carry):
         at = pl.ds(pl.multiple_of(i * BLK, BLK), BLK)
         inside = pl.ds(pl.multiple_of(lax.rem(i, wb) * BLK, BLK), BLK)
-        block = mm(cotangent, actr[:, :, at].reshape(ny * tok, BLK)) - mm(low_rank, q3[lax.div(i, wb), :, inside])
+        n = part // BLK
+        piece = pl.ds(pl.multiple_of(lax.rem(i, n) * BLK, BLK), BLK)
+        block = actr[:, lax.div(i, n), :, piece].reshape(ny * tok, BLK)
+        block = mm(cotangent, block) - mm(low_rank, q3[lax.div(i, wb), :, inside])
         error_out[at, :] = err_v[at, :] + block.T
         return carry
 
@@ -463,8 +492,8 @@
         assert d == nb * BLK and kv == BLK and per * BLK % wide == 0
         xc = nx * nc
         sends = (
-            4 * (ny - 1) + 3 * CHUNKS + (nx - 1) + nx * (nc - 1) + (xc - 1) * nz + (ny - 1) * (nz - 1)
-            + 3 * (per - 1) + 2 * (nc - 1) + (ny * nc - 1)
+            4 * (ny - 1) + 4 + 3 * CHUNKS + (nx - 1) + nx * (nc - 1) + (xc - 1) * nz + (ny - 1) * (nz - 1)
+            + 3 * (per - 1) + 3 * (nc - 1)
         )
         inputs = [
             pltpu.with_memory_space_constraint(a, pltpu.HBM) for a in (act, vg, w, err[0], right_prev.T)
@@ -480,10 +509,11 @@
             out_specs=(vmem,) * 4,
             scratch_shapes=[
                 pltpu.VMEM((r, kv), F32),
-                pltpu.VMEM((ny, tok, d), BF16),
+                pltpu.VMEM((ny, CHUNKS, tok, d // CHUNKS), BF16),
                 pltpu.VMEM((ny, tok, kv), BF16),
                 pltpu.VMEM((d, kv), F32),
-                pltpu.VMEM((ny, r, kv), F32),
+                pltpu.VMEM((ny, r, tok), F32),
+                pltpu.VMEM((ny - 1, r, tok), F32),
                 pltpu.VMEM((xc, ny, tok, kv), BF16),
                 pltpu.VMEM((nz, ny, BLK, kv), BF16),
                 pltpu.VMEM((nz, xc, tok, BLK), BF16),
@@ -495,9 +525,10 @@
                 pltpu.VMEM((d // wide, r, wide), F32),
                 pltpu.VMEM((d // wide, 3 * r, wide), BF16),
                 pltpu.VMEM((ny, r, kv), F32),
-                pltpu.VMEM((nc, ny, r, kv), F32),
+                pltpu.VMEM((ny - 1, r, kv), F32),
+                pltpu.VMEM((nc, r, kv), F32),
                 pltpu.VMEM((per, r, kv), F32),
-                pltpu.SemaphoreType.DMA((1 + 1 + 4 + 1 + ny + 2 * nz,)),
+                pltpu.SemaphoreType.DMA((1 + 1 + 4 + CHUNKS + ny + 2 * nz,)),
                 pltpu.SemaphoreType.DMA((sends,)),
                 pltpu.SemaphoreType.DMA((sends,)),
             ],

time: 110 us -> 110 us (level)
  no operation moved by 1% of the time
where the time goes in v6:
time: 110 us
  Pallas kernels  109 us (99%)
    pallas_call x1, Pallas kernels, body(): pl.pallas_call(functools.partial(comm_kernel, geom), out_shape=tuple((plt...  105 us
    pallas_call x1, Pallas kernels, body(): pl.pallas_call(store_kernel, out_shape=tuple((jax.ShapeDtypeStruct(*shape...  4.39 us

profile of v6, /device:TPU:1, one launch (start us, length us, event | category | flops | bytes accessed | tf_op | source)
XLA Modules:
  0.0 110.0 jit_solution(6291664791672403542)
XLA Ops:
  0.6 105.0 %shard_map.84 = (f32[8192,256]{1,0:T(8,128)S(1)}, f32[32,8192]{1,0:T(8,128)S(1)}, f32[32,256]{1,0:T(8,128)S(1)}, bf16[128,8192]{1,0:T(8,128)(2,1)S(1)}) custom-call(bf16[128,8192]{1,0:T(8,128)(2,1)} %act.1, bf16[512,256]{1,0:T(8,128)(2,1)} %vg.1, bf16[8192,256]{1,0:T(8,128)(2,1)} %w.1, f32[8192,256]{1,0:T(8,128)} %bitcast.5, f32[32,256]{1,0:T(8,128)} %bitcast.6), custom_call_target="tpu_custom_call" | custom-call | tf_op jit(solution)/shard_map/pallas_call | solution.py:505
  105.6 4.4 %shard_map.85 = (f32[8192,256]{1,0:T(8,128)}, f32[32,8192]{1,0:T(8,128)}, f32[32,256]{1,0:T(8,128)}, bf16[128,8192]{1,0:T(8,128)(2,1)}) custom-call(f32[8192,256]{1,0:T(8,128)S(1)} %get-tuple-element.12.error_in, f32[32,8192]{1,0:T(8,128)S(1)} %get-tuple-element.13.left_in, f32[32,256]{1,0:T(8,128)S(1)} %get-tuple-element.14.right_in, ...), custom_call_target="tpu_custom_call" | custom-call | tf_op jit(solution)/shard_map/pallas_call | solution.py:540

commit v7 on v6

--- a/solution.py
+++ b/solution.py
@@ -109,8 +109,8 @@
 
 
 def comm_kernel(
-    geom, act, vg, w, err, rt_in, error_out, left_out, r_out, gi,
-    rt, actr, vg_v, err_v, uout, uin, vgx, wbuf, outs, lacc, lf, rc, rxz, ysum, q1, q3, zout, zin, zsum, tz,
+    geom, act, vg, w, err, rt_in, merged, left_out, r_out, gi,
+    rt, actr, vg_v, err_v, uout, uin, vgx, wbuf, outs, lacc, lf, rc, rxz, ysum, q1, zout, zin, zsum, tz,
     local_sem, send_sem, recv_sem,
 ):
     nz, nx, nc, ny = geom
@@ -149,7 +149,7 @@
     cores = [shifted(c, dc, nc) for dc in range(1, nc)]
     up, down, across = shifted(y, 1, ny), shifted(y, ny - 1, ny), shifted(y, 2, ny)
 
-    sent = []
+    sent, settled = [], []
     counter = [0, 0]
 
     def send(src, dst, to):
@@ -173,6 +173,11 @@
         for copy in copies:
             copy.wait_recv()
 
+    def settle(copies):
+        for copy in copies:
+            copy.wait_send()
+        settled.extend(id(copy) for copy in copies)
+
     def tokens(yy):
         return pl.ds(pl.multiple_of(yy * tok, tok), tok)
 
@@ -225,8 +230,8 @@
             from_across[j] = send(actr.at[1, j], actr.at[2, j], device(z, x, c, down))
 
     load_act = dict(enumerate(load_act))
+    recv_vg = [send(vg.at[tokens(yy)], vgx.at[k, y], device(z, x, c, yy)) for _, yy in y_peers]
     direct(0)
-    recv_vg = [send(vg.at[tokens(yy)], vgx.at[k, y], device(z, x, c, yy)) for _, yy in y_peers]
     own_w = w.at[weight_rows(z)]
     w_from_down = send(own_w, wbuf.at[z, y], device(z, x, c, up))
     w_from_up = send(own_w, wbuf.at[z, y], device(z, x, c, down))
@@ -285,17 +290,27 @@
         recv.append(send(lacc.at[cc], rc, device(z, x, cc, y)))
     act_left(c)
 
+    recv_core = recv
+    direct(3)
+    load_vgx.wait()
+    wait_all(recv_vg)
+    recv_vgx = [send(vgx.at[k], vgx.at[k], device(z, xx, c, y)) for _, xx in x_peers]
+    relayed = [send(vgx.at[k], vgx.at[k], device(z, x, cc, y)) for cc in cores]
     wait_all(recv)
     lacc[c] += rc[...]
     recv = [
         send(lacc.at[c, xx * nz + zz], rxz.at[i], device(zz, xx, c, y)) for i, (xx, zz) in enumerate(plane)
     ]
-    direct(3)
-
-    load_vgx.wait()
-    wait_all(recv_vg)
-    recv_vgx = [send(vgx.at[k], vgx.at[k], device(z, xx, c, y)) for _, xx in x_peers]
-    relayed = [send(vgx.at[k], vgx.at[k], device(z, x, cc, y)) for cc in cores]
+    settle(recv_u + recv_core)
+    recv_rs = recv
+    wait_all(recv)
+    total = lacc[c, mine]
+    for i in range(len(plane)):
+        total = total + rxz[i]
+    ysum[y] = total
+    own = ysum.at[y]
+    recv = [send(own, own, device(z, x, c, yy)) for _, yy in y_peers]
+    direct(4, 5)
     for copy in load_w:
         copy.wait()
     first, second = pl.ds(0, BLK // 2), pl.ds(BLK // 2, BLK // 2)
@@ -309,35 +324,32 @@
         for _, zz in z_peers:
             recv_wz.append(send(wbuf.at[z, source], wbuf.at[z, source], device(zz, x, c, y)))
 
-    weights_on(down)
-    weights_on(up)
-    wait_all(recv)
-    total = lacc[c, mine]
-    for i in range(len(plane)):
-        total = total + rxz[i]
-    ysum[y] = total
-    own = ysum.at[y]
-    recv = [send(own, own, device(z, x, c, yy)) for _, yy in y_peers]
-    direct(4)
-    wait_all(w_halves)
-    weights_on(across)
+    settle(recv_rs)
     wait_all(recv)
     total = ysum[0]
     for yy in range(1, ny):
         total = total + ysum[yy]
     lf[c, mine] = total
     own = lf.at[c, mine]
+    recv_y = recv
     recv = [send(own, own, device(zz, xx, c, y)) for xx, zz in plane]
-    direct(5)
-    wait_all(recv)
+    weights_on(down)
+    weights_on(up)
+    direct(6, 7)
+    settle(recv_y)
+    wait_all(recv)
+    recv_ag = recv
     own = lf.at[c]
     recv = [send(own, own, device(z, x, cc, y)) for cc in cores]
+    wait_all(w_halves)
+    weights_on(across)
+    settle(recv_ag)
 
     for copy, (dx, _) in zip(recv_vgx, x_peers):
         copy.wait_recv()
         slot = c * nx + shifted(x, nx - dx, nx)
         relayed += [send(vgx.at[slot], vgx.at[slot], device(z, x, cc, y)) for cc in cores]
-    direct(6)
+    forward(0, 1)
     wait_all(recv)
 
     def products(p, carry):
@@ -360,32 +372,28 @@
         zout[yy] = fold3(mm(by_act, vgx[k, yy]))
     zout[y] += fold2(by_err)
     recv = [send(zout.at[yy], zin.at[dy - 1], device(z, x, c, yy)) for dy, yy in y_peers]
-    direct(7)
-    forward(0)
+    forward(2, 3)
 
     wait_all(recv_wz)
     wait_all(relayed)
     xc = nc * nx
     many = min(4, xc)
 
-    def place(zz):
-        return gi.at[:, pl.ds(pl.multiple_of((k * nz + zz) * BLK, BLK), BLK)]
-
-    sent_out, kept_out = [], []
-    for zz in range(nz):
-
-        def input_grad(g, carry, zz=zz):
-            total = None
-            for yy in range(ny):
-                cotangent = vgx[pl.ds(g * many, many), yy].reshape(many * tok, BLK)
-                piece = mm(cotangent, wbuf[zz, yy], NT).astype(BF16).astype(F32)
-                total = piece if total is None else total + piece
-            outs[zz, pl.ds(g * many, many)] = total.astype(BF16).reshape(many, tok, BLK)
-            return carry
-
-        lax.fori_loop(0, xc // many, input_grad, 0)
-        sent_out += [send(outs.at[zz, cc * nx + xx], place(zz), device(z, xx, cc, y)) for xx, cc in group]
-        kept_out.append(fetch(outs.at[zz, k], place(zz)))
+    def input_grad(i, carry):
+        zz, g = lax.div(i, xc // many), lax.rem(i, xc // many)
+        total = None
+        for yy in range(ny):
+            cotangent = vgx[pl.ds(g * many, many), yy].reshape(many * tok, BLK)
+            piece = mm(cotangent, wbuf[zz, yy], NT).astype(BF16).astype(F32)
+            total = piece if total is None else total + piece
+        at = pl.ds(pl.multiple_of(zz * BLK, BLK), BLK)
+        outs[pl.ds(g * many, many), :, at] = total.astype(BF16).reshape(many, tok, BLK)
+        return carry
+
+    lax.fori_loop(0, nz * xc // many, input_grad, 0)
+    place = gi.at[:, pl.ds(pl.multiple_of(k * nz * BLK, BLK), nz * BLK)]
+    sent_out = [send(outs.at[cc * nx + xx], place, device(z, xx, cc, y)) for xx, cc in group]
+    kept_out = [fetch(outs.at[k], place)]
 
     wait_all(recv)
     total = zout[y]
@@ -393,7 +401,6 @@
         total = total + zin[dy]
     zsum[0] = total
     recv = [send(zsum.at[0], zsum.at[dc], device(z, x, cc, y)) for dc, cc in enumerate(cores, 1)]
-    forward(1)
     wait_all(recv)
     for dc in range(1, nc):
         total = total + zsum[dc]
@@ -419,24 +426,10 @@
         block = q1[p]
         block = block - times(again, block)
         left_out[:, columns(p)] = block * scale
-        hi, lo = split2(block)
-        q3[p] = jnp.concatenate([hi, lo, hi], axis=0)
         return carry
 
     lax.fori_loop(0, pieces, apply_second, 0)
-    forward(2)
-
-    forward(3)
-
-    wait_all(recv)
-    total = tz[0]
-    for i in range(1, per):
-        total = total + tz[i]
-    right = times(weights, total) / float(nb)
-    r_out[...] = right
-    hi, lo = split2(right)
-    hi, lo = hi.astype(F32), lo.astype(F32)
-    low_rank = jnp.concatenate([hi, hi, lo], axis=0).T.astype(BF16)
+
 
     for i in range(CHUNKS):
         if i >= half:
@@ -445,36 +438,49 @@
             from_up[i].wait_recv()
     cotangent = vg_v[...].reshape(ny * tok, BLK).astype(F32).T.astype(BF16)
 
-    def new_error(i, carry):
+    def merge(i, carry):
         at = pl.ds(pl.multiple_of(i * BLK, BLK), BLK)
-        inside = pl.ds(pl.multiple_of(lax.rem(i, wb) * BLK, BLK), BLK)
         n = part // BLK
         piece = pl.ds(pl.multiple_of(lax.rem(i, n) * BLK, BLK), BLK)
-        block = actr[:, lax.div(i, n), :, piece].reshape(ny * tok, BLK)
-        block = mm(cotangent, block) - mm(low_rank, q3[lax.div(i, wb), :, inside])
-        error_out[at, :] = err_v[at, :] + block.T
+        block = mm(cotangent, actr[:, lax.div(i, n), :, piece].reshape(ny * tok, BLK))
+        merged[at, :] = err_v[at, :] + block.T
         return carry
 
     for i in range(half):
         for j in (i, i + half):
             from_across[j].wait_recv()
-            lax.fori_loop(j * part // BLK, (j + 1) * part // BLK, new_error, 0)
+            lax.fori_loop(j * part // BLK, (j + 1) * part // BLK, merge, 0)
+
+    wait_all(recv)
+    total = tz[0]
+    for i in range(1, per):
+        total = total + tz[i]
+    r_out[...] = times(weights, total) / float(nb)
 
     wait_all(sent_out)
     for copy in kept_out:
         copy.wait()
-    for copy in sent:
-        copy.wait_send()
-
-
-def store_kernel(error_in, left_in, right_in, gi_in, error_out, left_out, right_out, gi_out, sem):
-    n = 8
-    rows = error_in.shape[0] // n
-    pairs = [(error_in.at[pl.ds(i * rows, rows)], error_out.at[pl.ds(i * rows, rows)]) for i in range(n)]
-    pairs += [(left_in, left_out), (right_in, right_out), (gi_in, gi_out)]
-    copies = [pltpu.make_async_copy(a, b, sem.at[i]) for i, (a, b) in enumerate(pairs)]
+    settle([copy for copy in sent if id(copy) not in settled])
+
+
+def error_kernel(merged, left, right, gi, error_out, left_out, right_out, gi_out, error, sem):
+    d = merged.shape[0]
+    pieces = error.shape[0]
+    rows = d // pieces
+    copies = [
+        pltpu.make_async_copy(a, b, sem.at[pieces + i])
+        for i, (a, b) in enumerate([(gi, gi_out), (left, left_out), (right, right_out)])
+    ]
     for copy in copies:
         copy.start()
+    hi, lo = split2(right[...] / math.sqrt(float(d)))
+    right3 = jnp.concatenate([hi, hi, lo], axis=0)
+    for i in range(pieces):
+        at = pl.ds(i * rows, rows)
+        hi, lo = split2(left[:, at])
+        error[i] = merged[at, :] - mm(jnp.concatenate([hi, lo, hi], axis=0), right3, TN)
+        copies.append(pltpu.make_async_copy(error.at[i], error_out.at[at], sem.at[i]))
+        copies[-1].start()
     for copy in copies:
         copy.wait()
 
@@ -492,7 +498,7 @@
         assert d == nb * BLK and kv == BLK and per * BLK % wide == 0
         xc = nx * nc
         sends = (
-            4 * (ny - 1) + 4 + 3 * CHUNKS + (nx - 1) + nx * (nc - 1) + (xc - 1) * nz + (ny - 1) * (nz - 1)
+            4 * (ny - 1) + 4 + 3 * CHUNKS + (nx - 1) + nx * (nc - 1) + (xc - 1) + (ny - 1) * (nz - 1)
             + 3 * (per - 1) + 3 * (nc - 1)
         )
         inputs = [
@@ -516,19 +522,18 @@
                 pltpu.VMEM((ny - 1, r, tok), F32),
                 pltpu.VMEM((xc, ny, tok, kv), BF16),
                 pltpu.VMEM((nz, ny, BLK, kv), BF16),
-                pltpu.VMEM((nz, xc, tok, BLK), BF16),
+                pltpu.VMEM((xc, tok, nz * BLK), BF16),
                 pltpu.VMEM((nc, per, r, BLK), F32),
                 pltpu.VMEM((nc, per, r, BLK), F32),
                 pltpu.VMEM((per, r, BLK), F32),
                 pltpu.VMEM((per - 1, r, BLK), F32),
                 pltpu.VMEM((ny, r, BLK), F32),
                 pltpu.VMEM((d // wide, r, wide), F32),
-                pltpu.VMEM((d // wide, 3 * r, wide), BF16),
                 pltpu.VMEM((ny, r, kv), F32),
                 pltpu.VMEM((ny - 1, r, kv), F32),
                 pltpu.VMEM((nc, r, kv), F32),
                 pltpu.VMEM((per, r, kv), F32),
-                pltpu.SemaphoreType.DMA((1 + 1 + 4 + CHUNKS + ny + 2 * nz,)),
+                pltpu.SemaphoreType.DMA((1 + 1 + 4 + CHUNKS + ny + nz + 1,)),
                 pltpu.SemaphoreType.DMA((sends,)),
                 pltpu.SemaphoreType.DMA((sends,)),
             ],
@@ -537,13 +542,14 @@
             ),
         )(*inputs)
 
+        pieces = 16
         error_next, left, right, grad_input = pl.pallas_call(
-            store_kernel,
+            error_kernel,
             out_shape=tuple(jax.ShapeDtypeStruct(*shape) for shape in results),
-            in_specs=[anywhere] * 4,
+            in_specs=[vmem] * 4,
             out_specs=(anywhere,) * 4,
-            scratch_shapes=[pltpu.SemaphoreType.DMA((11,))],
-            compiler_params=pltpu.CompilerParams(vmem_limit_bytes=4 * MIB),
+            scratch_shapes=[pltpu.VMEM((pieces, d // pieces, kv), F32), pltpu.SemaphoreType.DMA((pieces + 3,))],
+            compiler_params=pltpu.CompilerParams(vmem_limit_bytes=24 * MIB),
         )(*made)
         return (grad_input, error_next[None], left.T, right.T)
 

time: 110 us -> 106 us (0.964)
  Pallas kernels: 109 us -> 105 us
    pallas_call x1, Pallas kernels: 105 us -> 100 us  [body(): pl.pallas_call(functools.partial(comm_kernel, geom), out_shape=tuple((plt...]
where the time goes in v7:
time: 106 us; the launch traced here: 105 us
  Pallas kernels  105 us (99%)
    pallas_call x1, Pallas kernels, body(): pl.pallas_call(functools.partial(comm_kernel, geom), out_shape=tuple((plt...  100 us
    pallas_call x1, Pallas kernels, body(): pl.pallas_call(error_kernel, out_shape=tuple((jax.ShapeDtypeStruct(*shape...  4.4 us

profile of v7, /device:TPU:1, one launch (start us, length us, event | category | flops | bytes accessed | tf_op | source)
XLA Modules:
  0.0 105.2 jit_solution(12176938945918865156)
XLA Ops:
  0.6 100.2 %shard_map.84 = (f32[8192,256]{1,0:T(8,128)S(1)}, f32[32,8192]{1,0:T(8,128)S(1)}, f32[32,256]{1,0:T(8,128)S(1)}, bf16[128,8192]{1,0:T(8,128)(2,1)S(1)}) custom-call(bf16[128,8192]{1,0:T(8,128)(2,1)} %act.1, bf16[512,256]{1,0:T(8,128)(2,1)} %vg.1, bf16[8192,256]{1,0:T(8,128)(2,1)} %w.1, f32[8192,256]{1,0:T(8,128)} %bitcast.5, f32[32,256]{1,0:T(8,128)} %bitcast.6), custom_call_target="tpu_custom_call" | custom-call | tf_op jit(solution)/shard_map/pallas_call | solution.py:511
  100.8 4.4 %shard_map.85 = (f32[8192,256]{1,0:T(8,128)}, f32[32,8192]{1,0:T(8,128)}, f32[32,256]{1,0:T(8,128)}, bf16[128,8192]{1,0:T(8,128)(2,1)}) custom-call(f32[8192,256]{1,0:T(8,128)S(1)} %get-tuple-element.12.merged, f32[32,8192]{1,0:T(8,128)S(1)} %get-tuple-element.13.left, f32[32,256]{1,0:T(8,128)S(1)} %get-tuple-element.14.right, ...), custom_call_target="tpu_custom_call" | custom-call | tf_op jit(solution)/shard_map/pallas_call | solution.py:546

commit v8 on v7

--- a/solution.py
+++ b/solution.py
@@ -110,7 +110,7 @@
 
 def comm_kernel(
     geom, act, vg, w, err, rt_in, merged, left_out, r_out, gi,
-    rt, actr, vg_v, err_v, uout, uin, vgx, wbuf, outs, lacc, lf, rc, rxz, ysum, q1, zout, zin, zsum, tz,
+    rt, actr, vg_v, err_v, uout, uin, vgx, wbuf, outs, lacc, lf, rc, rxz, ysum, q1, aout, ain, zsum, tz,
     local_sem, send_sem, recv_sem,
 ):
     nz, nx, nc, ny = geom
@@ -202,14 +202,6 @@
         pl.semaphore_signal(barrier, inc=1, device_id=peer, device_id_type=MESH)
     pl.semaphore_wait(barrier, len(everyone))
 
-    load_rt.wait()
-    rt3 = rows3(rt[...])
-    for load in load_vg:
-        load.wait()
-    for dy in range(ny):
-        uout[dy] = fold3(mm(rt3, vg_v[dy], NT))
-    recv_u = [send(uout.at[dy], uin.at[dy - 1], device(z, x, c, yy)) for dy, yy in y_peers]
-
     from_down, from_up, from_across = {}, {}, {}
 
     def direct(*numbers):
@@ -230,12 +222,21 @@
             from_across[j] = send(actr.at[1, j], actr.at[2, j], device(z, x, c, down))
 
     load_act = dict(enumerate(load_act))
+    direct(0)
+
+    load_rt.wait()
+    rt3 = rows3(rt[...])
+    for load in load_vg:
+        load.wait()
+    for dy in range(ny):
+        uout[dy] = fold3(mm(rt3, vg_v[dy], NT))
+    recv_u = [send(uout.at[dy], uin.at[dy - 1], device(z, x, c, yy)) for dy, yy in y_peers]
+
     recv_vg = [send(vg.at[tokens(yy)], vgx.at[k, y], device(z, x, c, yy)) for _, yy in y_peers]
-    direct(0)
     own_w = w.at[weight_rows(z)]
     w_from_down = send(own_w, wbuf.at[z, y], device(z, x, c, up))
     w_from_up = send(own_w, wbuf.at[z, y], device(z, x, c, down))
-    direct(1, 2)
+    direct(1)
 
     rt2 = rt3[: 2 * r]
 
@@ -291,7 +292,7 @@
     act_left(c)
 
     recv_core = recv
-    direct(3)
+    direct(2)
     load_vgx.wait()
     wait_all(recv_vg)
     recv_vgx = [send(vgx.at[k], vgx.at[k], device(z, xx, c, y)) for _, xx in x_peers]
@@ -310,7 +311,7 @@
     ysum[y] = total
     own = ysum.at[y]
     recv = [send(own, own, device(z, x, c, yy)) for _, yy in y_peers]
-    direct(4, 5)
+    direct(3, 4)
     for copy in load_w:
         copy.wait()
     first, second = pl.ds(0, BLK // 2), pl.ds(BLK // 2, BLK // 2)
@@ -335,7 +336,7 @@
     recv = [send(own, own, device(zz, xx, c, y)) for xx, zz in plane]
     weights_on(down)
     weights_on(up)
-    direct(6, 7)
+    direct(5)
     settle(recv_y)
     wait_all(recv)
     recv_ag = recv
@@ -349,30 +350,36 @@
         copy.wait_recv()
         slot = c * nx + shifted(x, nx - dx, nx)
         relayed += [send(vgx.at[slot], vgx.at[slot], device(z, x, cc, y)) for cc in cores]
-    forward(0, 1)
-    wait_all(recv)
+    direct(6)
+    wait_all(recv)
+
+    def left_piece(p):
+        return rows3(load_left(lf, lax.div(p, per_piece), lax.rem(p, per_piece) * wb))
 
     def products(p, carry):
-        gram, by_act, by_err = carry
-        block = rows3(load_left(lf, lax.div(p, per_piece), lax.rem(p, per_piece) * wb))
+        gram, by_act = carry
+        block = left_piece(p)
+        return gram + mm(block, block, NT), by_act + mm(block[: 2 * r], own_act(p), NT)
+
+    gram, by_act = lax.fori_loop(
+        0, pieces, products, (jnp.zeros((3 * r, 3 * r), F32), jnp.zeros((2 * r, tok), F32))
+    )
+    aout[...] = fold2(by_act)
+    recv_a = [send(aout, ain.at[dy - 1], device(z, x, c, yy)) for dy, yy in y_peers]
+    direct(7)
+    forward(0, 1, 2, 3)
+
+    def error_product(p, total):
         hi, lo = split2(err_v[columns(p), :])
-        top = block[: 2 * r]
-        by_act = by_act + mm(top, own_act(p), NT)
-        by_err = by_err + (mm(top, lo) + mm(top, hi))
-        return gram + mm(block, block, NT), by_act, by_err
-
-    gram, by_act, by_err = lax.fori_loop(
-        0,
-        pieces,
-        products,
-        (jnp.zeros((3 * r, 3 * r), F32), jnp.zeros((2 * r, tok), F32), jnp.zeros((2 * r, err_v.shape[1]), F32)),
-    )
-    by_act = rows3(fold2(by_act))
-    for yy in range(ny):
-        zout[yy] = fold3(mm(by_act, vgx[k, yy]))
-    zout[y] += fold2(by_err)
-    recv = [send(zout.at[yy], zin.at[dy - 1], device(z, x, c, yy)) for dy, yy in y_peers]
-    forward(2, 3)
+        block = left_piece(p)[: 2 * r]
+        return total + (mm(block, lo) + mm(block, hi))
+
+    total = fold2(lax.fori_loop(0, pieces, error_product, jnp.zeros((2 * r, err_v.shape[1]), F32)))
+    wait_all(recv_a)
+    for slot in range(ny):
+        total = total + fold3(mm(rows3(aout[...] if slot == 0 else ain[ny - slot - 1]), vg_v[slot]))
+    zsum[0] = total
+    recv = [send(zsum.at[0], zsum.at[dc], device(z, x, cc, y)) for dc, cc in enumerate(cores, 1)]
 
     wait_all(recv_wz)
     wait_all(relayed)
@@ -395,12 +402,6 @@
     sent_out = [send(outs.at[cc * nx + xx], place, device(z, xx, cc, y)) for xx, cc in group]
     kept_out = [fetch(outs.at[k], place)]
 
-    wait_all(recv)
-    total = zout[y]
-    for dy in range(ny - 1):
-        total = total + zin[dy]
-    zsum[0] = total
-    recv = [send(zsum.at[0], zsum.at[dc], device(z, x, cc, y)) for dc, cc in enumerate(cores, 1)]
     wait_all(recv)
     for dc in range(1, nc):
         total = total + zsum[dc]
@@ -529,8 +530,8 @@
                 pltpu.VMEM((per - 1, r, BLK), F32),
                 pltpu.VMEM((ny, r, BLK), F32),
                 pltpu.VMEM((d // wide, r, wide), F32),
-                pltpu.VMEM((ny, r, kv), F32),
-                pltpu.VMEM((ny - 1, r, kv), F32),
+                pltpu.VMEM((r, tok), F32),
+                pltpu.VMEM((ny - 1, r, tok), F32),
                 pltpu.VMEM((nc, r, kv), F32),
                 pltpu.VMEM((per, r, kv), F32),
                 pltpu.SemaphoreType.DMA((1 + 1 + 4 + CHUNKS + ny + nz + 1,)),

time: 106 us -> 108 us (1.019)
  Pallas kernels: 105 us -> 107 us
    pallas_call x1, Pallas kernels: 100 us -> 103 us  [body(): pl.pallas_call(functools.partial(comm_kernel, geom), out_shape=tuple((plt...]
where the time goes in v8:
time: 108 us
  Pallas kernels  107 us (99%)
    pallas_call x1, Pallas kernels, body(): pl.pallas_call(functools.partial(comm_kernel, geom), out_shape=tuple((plt...  103 us
    pallas_call x1, Pallas kernels, body(): pl.pallas_call(error_kernel, out_shape=tuple((jax.ShapeDtypeStruct(*shape...  4.4 us

profile of v8, /device:TPU:1, one launch (start us, length us, event | category | flops | bytes accessed | tf_op | source)
XLA Modules:
  0.0 107.5 jit_solution(10091879248232015055)
XLA Ops:
  0.6 102.5 %shard_map.84 = (f32[8192,256]{1,0:T(8,128)S(1)}, f32[32,8192]{1,0:T(8,128)S(1)}, f32[32,256]{1,0:T(8,128)S(1)}, bf16[128,8192]{1,0:T(8,128)(2,1)S(1)}) custom-call(bf16[128,8192]{1,0:T(8,128)(2,1)} %act.1, bf16[512,256]{1,0:T(8,128)(2,1)} %vg.1, bf16[8192,256]{1,0:T(8,128)(2,1)} %w.1, f32[8192,256]{1,0:T(8,128)} %bitcast.5, f32[32,256]{1,0:T(8,128)} %bitcast.6), custom_call_target="tpu_custom_call" | custom-call | tf_op jit(solution)/shard_map/pallas_call | solution.py:512
  103.1 4.4 %shard_map.85 = (f32[8192,256]{1,0:T(8,128)}, f32[32,8192]{1,0:T(8,128)}, f32[32,256]{1,0:T(8,128)}, bf16[128,8192]{1,0:T(8,128)(2,1)}) custom-call(f32[8192,256]{1,0:T(8,128)S(1)} %get-tuple-element.12.merged, f32[32,8192]{1,0:T(8,128)S(1)} %get-tuple-element.13.left, f32[32,256]{1,0:T(8,128)S(1)} %get-tuple-element.14.right, ...), custom_call_target="tpu_custom_call" | custom-call | tf_op jit(solution)/shard_map/pallas_call | solution.py:547

commit v9 on v8

--- a/solution.py
+++ b/solution.py
@@ -128,7 +128,6 @@
     c = lax.rem(dp, nc)
     x = lax.rem(lax.div(dp, nc), nx)
     z = lax.div(dp, nc * nx)
-    k = c * nx + x
     mine = x * nz + z
 
     def shifted(i, by, n):
@@ -138,13 +137,8 @@
         return ((zz * nx + xx) * nc + cc, yy)
 
     y_peers = [(dy, shifted(y, dy, ny)) for dy in range(1, ny)]
-    z_peers = [(dz, shifted(z, dz, nz)) for dz in range(1, nz)]
-    x_peers = [(dx, shifted(x, dx, nx)) for dx in range(1, nx)]
     plane = [
         (shifted(x, dx, nx), shifted(z, dz, nz)) for dx in range(nx) for dz in range(nz) if (dx, dz) != (0, 0)
-    ]
-    group = [
-        (shifted(x, dx, nx), shifted(c, dc, nc)) for dc in range(nc) for dx in range(nx) if (dc, dx) != (0, 0)
     ]
     cores = [shifted(c, dc, nc) for dc in range(1, nc)]
     up, down, across = shifted(y, 1, ny), shifted(y, ny - 1, ny), shifted(y, 2, ny)
@@ -181,21 +175,18 @@
     def tokens(yy):
         return pl.ds(pl.multiple_of(yy * tok, tok), tok)
 
-    def weight_rows(zz):
-        return pl.ds(pl.multiple_of((k * nz + zz) * BLK, BLK), BLK)
-
     load_rt = fetch(rt_in, rt)
     load_vg = [fetch(vg.at[tokens(yy)], vg_v.at[i]) for i, yy in enumerate((y, up, across, down))]
-    load_vgx = fetch(vg.at[tokens(y)], vgx.at[k, y])
+    load_vgx = fetch(vg.at[tokens(y)], vgx.at[0, 0])
     load_act = [fetch(act.at[:, pl.ds(i * part, part)], actr.at[0, i]) for i in range(CHUNKS)]
     share = d // 4
     load_err = [fetch(err.at[pl.ds(i * share, share)], err_v.at[pl.ds(i * share, share)]) for i in range(4)]
-    load_w = [fetch(w.at[weight_rows(zz)], wbuf.at[zz, y]) for zz in range(nz)]
+    load_w = fetch(w.at[c], wbuf.at[:, :, :, 0])
 
     barrier = pltpu.get_barrier_semaphore()
     everyone = (
-        [device(z, xx, cc, y) for xx, cc in group]
-        + [device(zz, shifted(x, dx, nx), c, y) for dx in range(nx) for _, zz in z_peers]
+        [device(z, x, cc, y) for cc in cores]
+        + [device(zz, xx, c, y) for xx, zz in plane]
         + [device(z, x, c, yy) for _, yy in y_peers]
     )
     for peer in everyone:
@@ -232,11 +223,69 @@
         uout[dy] = fold3(mm(rt3, vg_v[dy], NT))
     recv_u = [send(uout.at[dy], uin.at[dy - 1], device(z, x, c, yy)) for dy, yy in y_peers]
 
-    recv_vg = [send(vg.at[tokens(yy)], vgx.at[k, y], device(z, x, c, yy)) for _, yy in y_peers]
-    own_w = w.at[weight_rows(z)]
-    w_from_down = send(own_w, wbuf.at[z, y], device(z, x, c, up))
-    w_from_up = send(own_w, wbuf.at[z, y], device(z, x, c, down))
+    recv_vg = [send(vg.at[tokens(yy)], vgx.at[0, ny - dy], device(z, x, c, yy)) for dy, yy in y_peers]
+    own_w = w.at[c, x, z]
+    w_from_down = send(own_w, wbuf.at[x, z, :, 3], device(z, x, c, up))
+    w_from_up = send(own_w, wbuf.at[x, z, :, 1], device(z, x, c, down))
     direct(1)
+
+    def place(h, a, b):
+        return (a, b) if h == 0 else (b, a)
+
+    def piece(h, first, second):
+        zz, xx = place(h, first, second)
+        return wbuf.at[xx, zz, h, 1:ny]
+
+    def neighbour(h, stage, way):
+        n = (nz if h == 0 else nx) if stage == 0 else (nx if h == 0 else nz)
+        first, second = place(h, z, x)
+        if stage == 0:
+            first = shifted(first, way % n, n)
+        else:
+            second = shifted(second, way % n, n)
+        zz, xx = place(h, first, second)
+        return device(zz, xx, c, y)
+
+    half_here = [(place(h, z, x), place(h, nz, nx)) for h in range(2)]
+    stage_one, stage_one_across, stage_two, stage_two_across = {}, {}, {}, {}
+
+    def weights_first():
+        for h in range(2):
+            (first, second), _ = half_here[h]
+            own = piece(h, first, second)
+            for way in (1, -1):
+                stage_one[h, way] = send(own, own, neighbour(h, 0, way))
+
+    def weights_across():
+        for h in range(2):
+            (first, second), (n, _) = half_here[h]
+            way = 1 - 2 * h
+            stage_one[h, way].wait_recv()
+            came = piece(h, shifted(first, -way % n, n), second)
+            stage_one_across[h] = send(came, came, neighbour(h, 0, way))
+
+    def weights_second(i):
+        for h in range(2):
+            (first, second), (n, _) = half_here[h]
+            if i in (1, 2):
+                way = 3 - 2 * i
+                if way != 1 - 2 * h:
+                    stage_one[h, way].wait_recv()
+                first = shifted(first, -way % n, n)
+            elif i == 3:
+                stage_one_across[h].wait_recv()
+                first = shifted(first, 2, n)
+            for way in (1, -1):
+                stage_two[h, i, way] = send(piece(h, first, second), piece(h, first, second), neighbour(h, 1, way))
+
+    def weights_second_across(i):
+        for h in range(2):
+            (first, second), (n, m) = half_here[h]
+            first = shifted(first, (0, n - 1, 1, 2)[i], n)
+            way = (1, -1, 1, -1)[i]
+            stage_two[h, i, way].wait_recv()
+            came = piece(h, first, shifted(second, -way % m, m))
+            stage_two_across[h, i] = send(came, came, neighbour(h, 1, way))
 
     rt2 = rt3[: 2 * r]
 
@@ -295,13 +344,17 @@
     direct(2)
     load_vgx.wait()
     wait_all(recv_vg)
-    recv_vgx = [send(vgx.at[k], vgx.at[k], device(z, xx, c, y)) for _, xx in x_peers]
-    relayed = [send(vgx.at[k], vgx.at[k], device(z, x, cc, y)) for cc in cores]
+    recv_vgx = [send(vgx.at[0], vgx.at[dc], device(z, x, cc, y)) for dc, cc in enumerate(cores, 1)]
     wait_all(recv)
     lacc[c] += rc[...]
     recv = [
         send(lacc.at[c, xx * nz + zz], rxz.at[i], device(zz, xx, c, y)) for i, (xx, zz) in enumerate(plane)
     ]
+    load_w.wait()
+    w_from_down.wait_recv()
+    w_halves = [send(wbuf.at[x, z, 0, 3], wbuf.at[x, z, 0, 2], device(z, x, c, up))]
+    w_from_up.wait_recv()
+    w_halves.append(send(wbuf.at[x, z, 1, 1], wbuf.at[x, z, 1, 2], device(z, x, c, down)))
     settle(recv_u + recv_core)
     recv_rs = recv
     wait_all(recv)
@@ -312,19 +365,9 @@
     own = ysum.at[y]
     recv = [send(own, own, device(z, x, c, yy)) for _, yy in y_peers]
     direct(3, 4)
-    for copy in load_w:
-        copy.wait()
-    first, second = pl.ds(0, BLK // 2), pl.ds(BLK // 2, BLK // 2)
-    w_from_down.wait_recv()
-    w_halves = [send(wbuf.at[z, down, first], wbuf.at[z, down, first], device(z, x, c, up))]
-    w_from_up.wait_recv()
-    w_halves.append(send(wbuf.at[z, up, second], wbuf.at[z, up, second], device(z, x, c, down)))
-    recv_wz = []
-
-    def weights_on(source):
-        for _, zz in z_peers:
-            recv_wz.append(send(wbuf.at[z, source], wbuf.at[z, source], device(zz, x, c, y)))
-
+    wait_all(w_halves)
+    weights_first()
+    weights_second(0)
     settle(recv_rs)
     wait_all(recv)
     total = ysum[0]
@@ -334,22 +377,19 @@
     own = lf.at[c, mine]
     recv_y = recv
     recv = [send(own, own, device(zz, xx, c, y)) for xx, zz in plane]
-    weights_on(down)
-    weights_on(up)
     direct(5)
+    weights_across()
+    weights_second(1)
+    weights_second(2)
     settle(recv_y)
     wait_all(recv)
     recv_ag = recv
     own = lf.at[c]
     recv = [send(own, own, device(z, x, cc, y)) for cc in cores]
-    wait_all(w_halves)
-    weights_on(across)
+    weights_second(3)
+    weights_second_across(0)
     settle(recv_ag)
 
-    for copy, (dx, _) in zip(recv_vgx, x_peers):
-        copy.wait_recv()
-        slot = c * nx + shifted(x, nx - dx, nx)
-        relayed += [send(vgx.at[slot], vgx.at[slot], device(z, x, cc, y)) for cc in cores]
     direct(6)
     wait_all(recv)
 
@@ -368,6 +408,8 @@
     recv_a = [send(aout, ain.at[dy - 1], device(z, x, c, yy)) for dy, yy in y_peers]
     direct(7)
     forward(0, 1, 2, 3)
+    weights_second_across(1)
+    weights_second_across(2)
 
     def error_product(p, total):
         hi, lo = split2(err_v[columns(p), :])
@@ -381,26 +423,7 @@
     zsum[0] = total
     recv = [send(zsum.at[0], zsum.at[dc], device(z, x, cc, y)) for dc, cc in enumerate(cores, 1)]
 
-    wait_all(recv_wz)
-    wait_all(relayed)
-    xc = nc * nx
-    many = min(4, xc)
-
-    def input_grad(i, carry):
-        zz, g = lax.div(i, xc // many), lax.rem(i, xc // many)
-        total = None
-        for yy in range(ny):
-            cotangent = vgx[pl.ds(g * many, many), yy].reshape(many * tok, BLK)
-            piece = mm(cotangent, wbuf[zz, yy], NT).astype(BF16).astype(F32)
-            total = piece if total is None else total + piece
-        at = pl.ds(pl.multiple_of(zz * BLK, BLK), BLK)
-        outs[pl.ds(g * many, many), :, at] = total.astype(BF16).reshape(many, tok, BLK)
-        return carry
-
-    lax.fori_loop(0, nz * xc // many, input_grad, 0)
-    place = gi.at[:, pl.ds(pl.multiple_of(k * nz * BLK, BLK), nz * BLK)]
-    sent_out = [send(outs.at[cc * nx + xx], place, device(z, xx, cc, y)) for xx, cc in group]
-    kept_out = [fetch(outs.at[k], place)]
+    weights_second_across(3)
 
     wait_all(recv)
     for dc in range(1, nc):
@@ -432,6 +455,28 @@
     lax.fori_loop(0, pieces, apply_second, 0)
 
 
+    for i in range(4):
+        for h in range(2):
+            stage_two[h, i, (-1, 1, -1, 1)[i]].wait_recv()
+            stage_two_across[h, i].wait_recv()
+    wait_all(recv_vgx)
+
+    def input_grad(i, carry):
+        total = None
+        for slot in range(ny):
+            weight = wbuf[lax.div(i, nz), lax.rem(i, nz), :, slot].reshape(BLK, BLK)
+            part_sum = mm(vgx[:, slot].reshape(nc * tok, BLK), weight, NT).astype(BF16).astype(F32)
+            total = part_sum if total is None else total + part_sum
+        total = total.astype(BF16).reshape(nc, tok, BLK)
+        gi[:, pl.ds(pl.multiple_of((c * per + i) * BLK, BLK), BLK)] = total[0]
+        for dc in range(1, nc):
+            outs[dc - 1, :, pl.ds(pl.multiple_of(i * BLK, BLK), BLK)] = total[dc]
+        return carry
+
+    lax.fori_loop(0, per, input_grad, 0)
+    share_of = gi.at[:, pl.ds(pl.multiple_of(c * per * BLK, BLK), per * BLK)]
+    sent_out = [send(outs.at[nc - 1 - dc], share_of, device(z, x, cc, y)) for dc, cc in enumerate(cores, 1)]
+
     for i in range(CHUNKS):
         if i >= half:
             from_down[i].wait_recv()
@@ -459,9 +504,8 @@
     r_out[...] = times(weights, total) / float(nb)
 
     wait_all(sent_out)
-    for copy in kept_out:
-        copy.wait()
     settle([copy for copy in sent if id(copy) not in settled])
+    assert counter == [send_sem.shape[0], local_sem.shape[0]], counter
 
 
 def error_kernel(merged, left, right, gi, error_out, left_out, right_out, gi_out, error, sem):
@@ -497,13 +541,10 @@
         per = nx * nz
         wide = min(WIDE, per * BLK)
         assert d == nb * BLK and kv == BLK and per * BLK % wide == 0
-        xc = nx * nc
-        sends = (
-            4 * (ny - 1) + 4 + 3 * CHUNKS + (nx - 1) + nx * (nc - 1) + (xc - 1) + (ny - 1) * (nz - 1)
-            + 3 * (per - 1) + 3 * (nc - 1)
-        )
+        sends = 4 * (ny - 1) + 4 + 3 * CHUNKS + 30 + 3 * (per - 1) + 5 * (nc - 1)
+        pieces = w.reshape(nc, nx, nz, 2, BLK // 2, kv)
         inputs = [
-            pltpu.with_memory_space_constraint(a, pltpu.HBM) for a in (act, vg, w, err[0], right_prev.T)
+            pltpu.with_memory_space_constraint(a, pltpu.HBM) for a in (act, vg, pieces, err[0], right_prev.T)
         ]
         hbm = pl.BlockSpec(memory_space=pltpu.HBM)
         vmem = pl.BlockSpec(memory_space=pltpu.VMEM)
@@ -521,9 +562,9 @@
                 pltpu.VMEM((d, kv), F32),
                 pltpu.VMEM((ny, r, tok), F32),
                 pltpu.VMEM((ny - 1, r, tok), F32),
-                pltpu.VMEM((xc, ny, tok, kv), BF16),
-                pltpu.VMEM((nz, ny, BLK, kv), BF16),
-                pltpu.VMEM((xc, tok, nz * BLK), BF16),
+                pltpu.VMEM((nc, ny, tok, kv), BF16),
+                pltpu.VMEM((nx, nz, 2, ny, BLK // 2, kv), BF16),
+                pltpu.VMEM((max(nc - 1, 1), tok, per * BLK), BF16),
                 pltpu.VMEM((nc, per, r, BLK), F32),
                 pltpu.VMEM((nc, per, r, BLK), F32),
                 pltpu.VMEM((per, r, BLK), F32),
@@ -534,7 +575,7 @@
                 pltpu.VMEM((ny - 1, r, tok), F32),
                 pltpu.VMEM((nc, r, kv), F32),
                 pltpu.VMEM((per, r, kv), F32),
-                pltpu.SemaphoreType.DMA((1 + 1 + 4 + CHUNKS + ny + nz + 1,)),
+                pltpu.SemaphoreType.DMA((1 + 1 + 4 + CHUNKS + ny + 1,)),
                 pltpu.SemaphoreType.DMA((sends,)),
                 pltpu.SemaphoreType.DMA((sends,)),
             ],

time: 108 us -> 101 us (0.935)
  Pallas kernels: 107 us -> 98.8 us
    pallas_call x1, Pallas kernels: 103 us -> 94.4 us  [body(): pl.pallas_call(functools.partial(comm_kernel, geom), out_shape=tuple((plt...]
where the time goes in v9:
time: 101 us; the launch traced here: 99.5 us
  Pallas kernels  98.8 us (98%)
    pallas_call x1, Pallas kernels, body(): pl.pallas_call(functools.partial(comm_kernel, geom), out_shape=tuple((plt...  94.4 us
    pallas_call x1, Pallas kernels, body(): pl.pallas_call(error_kernel, out_shape=tuple((jax.ShapeDtypeStruct(*shape...  4.4 us

profile of v9, /device:TPU:1, one launch (start us, length us, event | category | flops | bytes accessed | tf_op | source)
XLA Modules:
  0.0 99.5 jit_solution(7433701162599584493)
XLA Ops:
  0.6 94.4 %shard_map.84 = (f32[8192,256]{1,0:T(8,128)S(1)}, f32[32,8192]{1,0:T(8,128)S(1)}, f32[32,256]{1,0:T(8,128)S(1)}, bf16[128,8192]{1,0:T(8,128)(2,1)S(1)}) custom-call(bf16[128,8192]{1,0:T(8,128)(2,1)} %act.1, bf16[512,256]{1,0:T(8,128)(2,1)} %vg.1, bf16[2,4,4,2,128,256]{5,4,3,2,1,0:T(8,128)(2,1)} %bitcast.7, f32[8192,256]{1,0:T(8,128)} %bitcast.6, ...), custom_call_target="tpu_custom_call" | custom-call | tf_op jit(solution)/shard_map/pallas_call | solution.py:553
  95.1 4.4 %shard_map.85 = (f32[8192,256]{1,0:T(8,128)}, f32[32,8192]{1,0:T(8,128)}, f32[32,256]{1,0:T(8,128)}, bf16[128,8192]{1,0:T(8,128)(2,1)}) custom-call(f32[8192,256]{1,0:T(8,128)S(1)} %get-tuple-element.12.merged, f32[32,8192]{1,0:T(8,128)S(1)} %get-tuple-element.13.left, f32[32,256]{1,0:T(8,128)S(1)} %get-tuple-element.14.right, ...), custom_call_target="tpu_custom_call" | custom-call | tf_op jit(solution)/shard_map/pallas_call | solution.py:588

commit v10 on v9

--- a/solution.py
+++ b/solution.py
@@ -98,7 +98,7 @@
             off_left = off_left + h * rows[i]
             off_weights = off_weights + f * given[i]
         left, weights = left - off_left, weights - off_weights
-    return left, weights
+        yield left, weights
 
 
 def unit_weights(state):
@@ -227,7 +227,7 @@
     own_w = w.at[c, x, z]
     w_from_down = send(own_w, wbuf.at[x, z, :, 3], device(z, x, c, up))
     w_from_up = send(own_w, wbuf.at[x, z, :, 1], device(z, x, c, down))
-    direct(1)
+    direct(1, 2, 3)
 
     def place(h, a, b):
         return (a, b) if h == 0 else (b, a)
@@ -341,7 +341,7 @@
     act_left(c)
 
     recv_core = recv
-    direct(2)
+    direct(4, 5)
     load_vgx.wait()
     wait_all(recv_vg)
     recv_vgx = [send(vgx.at[0], vgx.at[dc], device(z, x, cc, y)) for dc, cc in enumerate(cores, 1)]
@@ -364,7 +364,8 @@
     ysum[y] = total
     own = ysum.at[y]
     recv = [send(own, own, device(z, x, c, yy)) for _, yy in y_peers]
-    direct(3, 4)
+    direct(6, 7)
+    forward(0)
     wait_all(w_halves)
     weights_first()
     weights_second(0)
@@ -377,7 +378,7 @@
     own = lf.at[c, mine]
     recv_y = recv
     recv = [send(own, own, device(zz, xx, c, y)) for xx, zz in plane]
-    direct(5)
+    forward(1)
     weights_across()
     weights_second(1)
     weights_second(2)
@@ -390,7 +391,8 @@
     weights_second_across(0)
     settle(recv_ag)
 
-    direct(6)
+    forward(2, 3)
+    settle(recv_vg + recv_vgx + [w_from_down, w_from_up] + w_halves + list(stage_one.values()))
     wait_all(recv)
 
     def left_piece(p):
@@ -406,17 +408,19 @@
     )
     aout[...] = fold2(by_act)
     recv_a = [send(aout, ain.at[dy - 1], device(z, x, c, yy)) for dy, yy in y_peers]
-    direct(7)
-    forward(0, 1, 2, 3)
     weights_second_across(1)
     weights_second_across(2)
 
-    def error_product(p, total):
-        hi, lo = split2(err_v[columns(p), :])
-        block = left_piece(p)[: 2 * r]
-        return total + (mm(block, lo) + mm(block, hi))
-
-    total = fold2(lax.fori_loop(0, pieces, error_product, jnp.zeros((2 * r, err_v.shape[1]), F32)))
+    total = jnp.zeros((2 * r, err_v.shape[1]), F32)
+    count = nb // (r // 4)
+    for i, state in enumerate(gram_schmidt(self_products(gram, r))):
+        block = jnp.concatenate([lf[(i * count + j) // per, (i * count + j) % per] for j in range(count)], axis=1)
+        hi, lo = split2(err_v[i * count * BLK : (i + 1) * count * BLK, :])
+        block = rows2(block)
+        total = total + (mm(block, lo) + mm(block, hi))
+    total = fold2(total)
+    weights, norms = unit_weights(state)
+
     wait_all(recv_a)
     for slot in range(ny):
         total = total + fold3(mm(rows3(aout[...] if slot == 0 else ain[ny - slot - 1]), vg_v[slot]))
@@ -425,23 +429,21 @@
 
     weights_second_across(3)
 
+    def apply_first(p, gram):
+        block = times(weights, load_left(lf, lax.div(p, per_piece), lax.rem(p, per_piece) * wb))
+        q1[p] = block
+        block = rows3(block)
+        return gram + mm(block, block, NT)
+
+    off = self_products(lax.fori_loop(0, pieces, apply_first, jnp.zeros((3 * r, 3 * r), F32)), r) - norms
+    row_id = lax.broadcasted_iota(jnp.int32, (r, r), 0)
+    col_id = lax.broadcasted_iota(jnp.int32, (r, r), 1)
     wait_all(recv)
     for dc in range(1, nc):
         total = total + zsum[dc]
     tz[mine] = total
     own = tz.at[mine]
     recv = [send(own, own, device(zz, xx, c, y)) for xx, zz in plane]
-    weights, norms = unit_weights(gram_schmidt(self_products(gram, r)))
-
-    def apply_first(p, total):
-        block = times(weights, load_left(lf, lax.div(p, per_piece), lax.rem(p, per_piece) * wb))
-        q1[p] = block
-        block = rows3(block)
-        return total + mm(block, block, NT)
-
-    off = self_products(lax.fori_loop(0, pieces, apply_first, jnp.zeros((3 * r, 3 * r), F32)), r) - norms
-    row_id = lax.broadcasted_iota(jnp.int32, (r, r), 0)
-    col_id = lax.broadcasted_iota(jnp.int32, (r, r), 1)
     again = jnp.where(col_id < row_id, off, jnp.where(col_id == row_id, 0.5 * off, 0.0))
     weights = weights - times(again, weights)
     scale = math.sqrt(float(d))

time: 101 us -> 119 us (1.18)
  the two profiles are of different devices: /device:TPU:1 before, /device:TPU:6 now
where the time goes in v10:
time: 119 us
  Pallas kernels  118 us (99%)
    pallas_call x1, Pallas kernels, body(): pl.pallas_call(functools.partial(comm_kernel, geom), out_shape=tuple((plt...  114 us
    pallas_call x1, Pallas kernels, body(): pl.pallas_call(error_kernel, out_shape=tuple((jax.ShapeDtypeStruct(*shape...  4.4 us

profile of v10, /device:TPU:6, one launch (start us, length us, event | category | flops | bytes accessed | tf_op | source)
XLA Modules:
  0.0 119.1 jit_solution(16216121111294819846)
XLA Ops:
  0.6 114.0 %shard_map.84 = (f32[8192,256]{1,0:T(8,128)S(1)}, f32[32,8192]{1,0:T(8,128)S(1)}, f32[32,256]{1,0:T(8,128)S(1)}, bf16[128,8192]{1,0:T(8,128)(2,1)S(1)}) custom-call(bf16[128,8192]{1,0:T(8,128)(2,1)} %act.1, bf16[512,256]{1,0:T(8,128)(2,1)} %vg.1, bf16[2,4,4,2,128,256]{5,4,3,2,1,0:T(8,128)(2,1)} %bitcast.7, f32[8192,256]{1,0:T(8,128)} %bitcast.6, ...), custom_call_target="tpu_custom_call" | custom-call | tf_op jit(solution)/shard_map/pallas_call | solution.py:555
  114.7 4.4 %shard_map.85 = (f32[8192,256]{1,0:T(8,128)}, f32[32,8192]{1,0:T(8,128)}, f32[32,256]{1,0:T(8,128)}, bf16[128,8192]{1,0:T(8,128)(2,1)}) custom-call(f32[8192,256]{1,0:T(8,128)S(1)} %get-tuple-element.12.merged, f32[32,8192]{1,0:T(8,128)S(1)} %get-tuple-element.13.left, f32[32,256]{1,0:T(8,128)S(1)} %get-tuple-element.14.right, ...), custom_call_target="tpu_custom_call" | custom-call | tf_op jit(solution)/shard_map/pallas_call | solution.py:590

commit v11 on v10

--- a/solution.py
+++ b/solution.py
@@ -15,7 +15,7 @@
 EPS = 1e-12
 MIB = 1024 * 1024
 WIDE = 8 * BLK
-CHUNKS = 8
+CHUNKS = 16
 NN = (((1,), (0,)), ((), ()))
 NT = (((1,), (1,)), ((), ()))
 TN = (((0,), (0,)), ((), ()))
@@ -110,7 +110,7 @@
 
 def comm_kernel(
     geom, act, vg, w, err, rt_in, merged, left_out, r_out, gi,
-    rt, actr, vg_v, err_v, uout, uin, vgx, wbuf, outs, lacc, lf, rc, rxz, ysum, q1, aout, ain, zsum, tz,
+    rt, actr, vg_v, err_v, uout, uin, vstage, vgx, wbuf, outs, lacc, lf, rc, rxz, ysum, q1, aout, ain, zsum, tz,
     local_sem, send_sem, recv_sem,
 ):
     nz, nx, nc, ny = geom
@@ -213,7 +213,6 @@
             from_across[j] = send(actr.at[1, j], actr.at[2, j], device(z, x, c, down))
 
     load_act = dict(enumerate(load_act))
-    direct(0)
 
     load_rt.wait()
     rt3 = rows3(rt[...])
@@ -223,11 +222,19 @@
         uout[dy] = fold3(mm(rt3, vg_v[dy], NT))
     recv_u = [send(uout.at[dy], uin.at[dy - 1], device(z, x, c, yy)) for dy, yy in y_peers]
 
-    recv_vg = [send(vg.at[tokens(yy)], vgx.at[0, ny - dy], device(z, x, c, yy)) for dy, yy in y_peers]
+    recv_vg = [send(vg.at[tokens(up)], vgx.at[0, 3], device(z, x, c, up))]
+    recv_vg.append(send(vg.at[tokens(down)], vgx.at[0, 1], device(z, x, c, down)))
+    few = tok // 2
+    ways = (up, down)
+    vg_passing = [
+        send(vg.at[pl.ds(pl.multiple_of(across * tok + h * few, few), few)], vstage.at[h], device(z, x, c, ways[h]))
+        for h in range(2)
+    ]
+    direct(0)
     own_w = w.at[c, x, z]
     w_from_down = send(own_w, wbuf.at[x, z, :, 3], device(z, x, c, up))
     w_from_up = send(own_w, wbuf.at[x, z, :, 1], device(z, x, c, down))
-    direct(1, 2, 3)
+    direct(1, 2)
 
     def place(h, a, b):
         return (a, b) if h == 0 else (b, a)
@@ -341,10 +348,11 @@
     act_left(c)
 
     recv_core = recv
-    direct(4, 5)
+    direct(3)
     load_vgx.wait()
-    wait_all(recv_vg)
-    recv_vgx = [send(vgx.at[0], vgx.at[dc], device(z, x, cc, y)) for dc, cc in enumerate(cores, 1)]
+    for h in range(2):
+        vg_passing[h].wait_recv()
+        recv_vg.append(send(vstage.at[h], vgx.at[0, 2, h * few : (h + 1) * few], device(z, x, c, ways[h])))
     wait_all(recv)
     lacc[c] += rc[...]
     recv = [
@@ -364,8 +372,7 @@
     ysum[y] = total
     own = ysum.at[y]
     recv = [send(own, own, device(z, x, c, yy)) for _, yy in y_peers]
-    direct(6, 7)
-    forward(0)
+    direct(4, 5, 6, 7)
     wait_all(w_halves)
     weights_first()
     weights_second(0)
@@ -378,7 +385,7 @@
     own = lf.at[c, mine]
     recv_y = recv
     recv = [send(own, own, device(zz, xx, c, y)) for xx, zz in plane]
-    forward(1)
+    direct(8)
     weights_across()
     weights_second(1)
     weights_second(2)
@@ -391,8 +398,10 @@
     weights_second_across(0)
     settle(recv_ag)
 
-    forward(2, 3)
-    settle(recv_vg + recv_vgx + [w_from_down, w_from_up] + w_halves + list(stage_one.values()))
+    direct(9)
+    wait_all(recv_vg)
+    recv_vgx = [send(vgx.at[0], vgx.at[dc], device(z, x, cc, y)) for dc, cc in enumerate(cores, 1)]
+    settle(vg_passing + recv_vg + [w_from_down, w_from_up] + w_halves + list(stage_one.values()))
     wait_all(recv)
 
     def left_piece(p):
@@ -408,6 +417,8 @@
     )
     aout[...] = fold2(by_act)
     recv_a = [send(aout, ain.at[dy - 1], device(z, x, c, yy)) for dy, yy in y_peers]
+    direct(*range(10, CHUNKS))
+    forward(*range(half))
     weights_second_across(1)
     weights_second_across(2)
 
@@ -486,24 +497,26 @@
             from_up[i].wait_recv()
     cotangent = vg_v[...].reshape(ny * tok, BLK).astype(F32).T.astype(BF16)
 
-    def merge(i, carry):
-        at = pl.ds(pl.multiple_of(i * BLK, BLK), BLK)
-        n = part // BLK
-        piece = pl.ds(pl.multiple_of(lax.rem(i, n) * BLK, BLK), BLK)
-        block = mm(cotangent, actr[:, lax.div(i, n), :, piece].reshape(ny * tok, BLK))
-        merged[at, :] = err_v[at, :] + block.T
-        return carry
-
-    for i in range(half):
-        for j in (i, i + half):
-            from_across[j].wait_recv()
-            lax.fori_loop(j * part // BLK, (j + 1) * part // BLK, merge, 0)
+    def merge(j):
+        from_across[j].wait_recv()
+        at = pl.ds(j * part, part)
+        merged[at, :] = err_v[at, :] + mm(cotangent, actr[:, j].reshape(ny * tok, part)).T
+
+    for i in range(half - 2):
+        merge(i)
+        merge(i + half)
 
     wait_all(recv)
     total = tz[0]
     for i in range(1, per):
         total = total + tz[i]
     r_out[...] = times(weights, total) / float(nb)
+    last = [id(from_across[i + h]) for i in range(half - 2, half) for h in (0, half)]
+    settle([copy for copy in sent if id(copy) not in settled + last])
+
+    for i in range(half - 2, half):
+        merge(i)
+        merge(i + half)
 
     wait_all(sent_out)
     settle([copy for copy in sent if id(copy) not in settled])
@@ -543,7 +556,7 @@
         per = nx * nz
         wide = min(WIDE, per * BLK)
         assert d == nb * BLK and kv == BLK and per * BLK % wide == 0
-        sends = 4 * (ny - 1) + 4 + 3 * CHUNKS + 30 + 3 * (per - 1) + 5 * (nc - 1)
+        sends = 3 * (ny - 1) + 6 + 4 + 3 * CHUNKS + 30 + 3 * (per - 1) + 5 * (nc - 1)
         pieces = w.reshape(nc, nx, nz, 2, BLK // 2, kv)
         inputs = [
             pltpu.with_memory_space_constraint(a, pltpu.HBM) for a in (act, vg, pieces, err[0], right_prev.T)
@@ -564,6 +577,7 @@
                 pltpu.VMEM((d, kv), F32),
                 pltpu.VMEM((ny, r, tok), F32),
                 pltpu.VMEM((ny - 1, r, tok), F32),
+                pltpu.VMEM((2, tok // 2, kv), BF16),
                 pltpu.VMEM((nc, ny, tok, kv), BF16),
                 pltpu.VMEM((nx, nz, 2, ny, BLK // 2, kv), BF16),
                 pltpu.VMEM((max(nc - 1, 1), tok, per * BLK), BF16),

time: 119 us -> 104 us (0.87)
  the two profiles are of different devices: /device:TPU:6 before, /device:TPU:1 now
where the time goes in v11:
time: 104 us
  Pallas kernels  103 us (99%)
    pallas_call x1, Pallas kernels, body(): pl.pallas_call(functools.partial(comm_kernel, geom), out_shape=tuple((plt...  98.3 us
    pallas_call x1, Pallas kernels, body(): pl.pallas_call(error_kernel, out_shape=tuple((jax.ShapeDtypeStruct(*shape...  4.4 us

profile of v11, /device:TPU:1, one launch (start us, length us, event | category | flops | bytes accessed | tf_op | source)
XLA Modules:
  0.0 103.5 jit_solution(8503688786428144853)
XLA Ops:
  0.6 98.3 %shard_map.84 = (f32[8192,256]{1,0:T(8,128)S(1)}, f32[32,8192]{1,0:T(8,128)S(1)}, f32[32,256]{1,0:T(8,128)S(1)}, bf16[128,8192]{1,0:T(8,128)(2,1)S(1)}) custom-call(bf16[128,8192]{1,0:T(8,128)(2,1)} %act.1, bf16[512,256]{1,0:T(8,128)(2,1)} %vg.1, bf16[2,4,4,2,128,256]{5,4,3,2,1,0:T(8,128)(2,1)} %bitcast.7, f32[8192,256]{1,0:T(8,128)} %bitcast.6, ...), custom_call_target="tpu_custom_call" | custom-call | tf_op jit(solution)/shard_map/pallas_call | solution.py:568
  99.0 4.4 %shard_map.85 = (f32[8192,256]{1,0:T(8,128)}, f32[32,8192]{1,0:T(8,128)}, f32[32,256]{1,0:T(8,128)}, bf16[128,8192]{1,0:T(8,128)(2,1)}) custom-call(f32[8192,256]{1,0:T(8,128)S(1)} %get-tuple-element.12.merged, f32[32,8192]{1,0:T(8,128)S(1)} %get-tuple-element.13.left, f32[32,256]{1,0:T(8,128)S(1)} %get-tuple-element.14.right, ...), custom_call_target="tpu_custom_call" | custom-call | tf_op jit(solution)/shard_map/pallas_call | solution.py:604

commit v12 on v11

--- a/solution.py
+++ b/solution.py
@@ -372,7 +372,7 @@
     ysum[y] = total
     own = ysum.at[y]
     recv = [send(own, own, device(z, x, c, yy)) for _, yy in y_peers]
-    direct(4, 5, 6, 7)
+    direct(*range(4, 12))
     wait_all(w_halves)
     weights_first()
     weights_second(0)
@@ -385,7 +385,6 @@
     own = lf.at[c, mine]
     recv_y = recv
     recv = [send(own, own, device(zz, xx, c, y)) for xx, zz in plane]
-    direct(8)
     weights_across()
     weights_second(1)
     weights_second(2)
@@ -398,7 +397,6 @@
     weights_second_across(0)
     settle(recv_ag)
 
-    direct(9)
     wait_all(recv_vg)
     recv_vgx = [send(vgx.at[0], vgx.at[dc], device(z, x, cc, y)) for dc, cc in enumerate(cores, 1)]
     settle(vg_passing + recv_vg + [w_from_down, w_from_up] + w_halves + list(stage_one.values()))
@@ -417,7 +415,7 @@
     )
     aout[...] = fold2(by_act)
     recv_a = [send(aout, ain.at[dy - 1], device(z, x, c, yy)) for dy, yy in y_peers]
-    direct(*range(10, CHUNKS))
+    direct(*range(12, CHUNKS))
     forward(*range(half))
     weights_second_across(1)
     weights_second_across(2)
@@ -432,41 +430,34 @@
     total = fold2(total)
     weights, norms = unit_weights(state)
 
+    def apply_first(p, gram):
+        block = times(weights, load_left(lf, lax.div(p, per_piece), lax.rem(p, per_piece) * wb))
+        q1[p] = block
+        block = rows3(block)
+        return gram + mm(block, block, NT)
+
+    off = self_products(lax.fori_loop(0, pieces, apply_first, jnp.zeros((3 * r, 3 * r), F32)), r) - norms
+    row_id = lax.broadcasted_iota(jnp.int32, (r, r), 0)
+    col_id = lax.broadcasted_iota(jnp.int32, (r, r), 1)
+    again = jnp.where(col_id < row_id, off, jnp.where(col_id == row_id, 0.5 * off, 0.0))
+    weights = weights - times(again, weights)
+    scale = math.sqrt(float(d))
+
+    def apply_second(p, carry):
+        block = q1[p]
+        block = block - times(again, block)
+        left_out[:, columns(p)] = block * scale
+        return carry
+
+    lax.fori_loop(0, pieces, apply_second, 0)
+
+
     wait_all(recv_a)
     for slot in range(ny):
         total = total + fold3(mm(rows3(aout[...] if slot == 0 else ain[ny - slot - 1]), vg_v[slot]))
     zsum[0] = total
     recv = [send(zsum.at[0], zsum.at[dc], device(z, x, cc, y)) for dc, cc in enumerate(cores, 1)]
-
     weights_second_across(3)
-
-    def apply_first(p, gram):
-        block = times(weights, load_left(lf, lax.div(p, per_piece), lax.rem(p, per_piece) * wb))
-        q1[p] = block
-        block = rows3(block)
-        return gram + mm(block, block, NT)
-
-    off = self_products(lax.fori_loop(0, pieces, apply_first, jnp.zeros((3 * r, 3 * r), F32)), r) - norms
-    row_id = lax.broadcasted_iota(jnp.int32, (r, r), 0)
-    col_id = lax.broadcasted_iota(jnp.int32, (r, r), 1)
-    wait_all(recv)
-    for dc in range(1, nc):
-        total = total + zsum[dc]
-    tz[mine] = total
-    own = tz.at[mine]
-    recv = [send(own, own, device(zz, xx, c, y)) for xx, zz in plane]
-    again = jnp.where(col_id < row_id, off, jnp.where(col_id == row_id, 0.5 * off, 0.0))
-    weights = weights - times(again, weights)
-    scale = math.sqrt(float(d))
-
-    def apply_second(p, carry):
-        block = q1[p]
-        block = block - times(again, block)
-        left_out[:, columns(p)] = block * scale
-        return carry
-
-    lax.fori_loop(0, pieces, apply_second, 0)
-
 
     for i in range(4):
         for h in range(2):
@@ -489,6 +480,13 @@
     lax.fori_loop(0, per, input_grad, 0)
     share_of = gi.at[:, pl.ds(pl.multiple_of(c * per * BLK, BLK), per * BLK)]
     sent_out = [send(outs.at[nc - 1 - dc], share_of, device(z, x, cc, y)) for dc, cc in enumerate(cores, 1)]
+
+    wait_all(recv)
+    for dc in range(1, nc):
+        total = total + zsum[dc]
+    tz[mine] = total
+    own = tz.at[mine]
+    recv = [send(own, own, device(zz, xx, c, y)) for xx, zz in plane]
 
     for i in range(CHUNKS):
         if i >= half:

time: 104 us -> 97 us (0.933)
  Pallas kernels: 103 us -> 95.7 us
    pallas_call x1, Pallas kernels: 98.3 us -> 91.3 us  [body(): pl.pallas_call(functools.partial(comm_kernel, geom), out_shape=tuple((plt...]
where the time goes in v12:
time: 97 us; the launch traced here: 96.5 us
  Pallas kernels  95.7 us (99%)
    pallas_call x1, Pallas kernels, body(): pl.pallas_call(functools.partial(comm_kernel, geom), out_shape=tuple((plt...  91.3 us
    pallas_call x1, Pallas kernels, body(): pl.pallas_call(error_kernel, out_shape=tuple((jax.ShapeDtypeStruct(*shape...  4.4 us

profile of v12, /device:TPU:1, one launch (start us, length us, event | category | flops | bytes accessed | tf_op | source)
XLA Modules:
  0.0 96.5 jit_solution(3897308740091458911)
XLA Ops:
  0.6 91.3 %shard_map.84 = (f32[8192,256]{1,0:T(8,128)S(1)}, f32[32,8192]{1,0:T(8,128)S(1)}, f32[32,256]{1,0:T(8,128)S(1)}, bf16[128,8192]{1,0:T(8,128)(2,1)S(1)}) custom-call(bf16[128,8192]{1,0:T(8,128)(2,1)} %act.1, bf16[512,256]{1,0:T(8,128)(2,1)} %vg.1, bf16[2,4,4,2,128,256]{5,4,3,2,1,0:T(8,128)(2,1)} %bitcast.7, f32[8192,256]{1,0:T(8,128)} %bitcast.6, ...), custom_call_target="tpu_custom_call" | custom-call | tf_op jit(solution)/shard_map/pallas_call | solution.py:566
  91.9 4.4 %shard_map.85 = (f32[8192,256]{1,0:T(8,128)}, f32[32,8192]{1,0:T(8,128)}, f32[32,256]{1,0:T(8,128)}, bf16[128,8192]{1,0:T(8,128)(2,1)}) custom-call(f32[8192,256]{1,0:T(8,128)S(1)} %get-tuple-element.12.merged, f32[32,8192]{1,0:T(8,128)S(1)} %get-tuple-element.13.left, f32[32,256]{1,0:T(8,128)S(1)} %get-tuple-element.14.right, ...), custom_call_target="tpu_custom_call" | custom-call | tf_op jit(solution)/shard_map/pallas_call | solution.py:602

commit v13 on v12

--- a/solution.py
+++ b/solution.py
@@ -175,14 +175,6 @@
     def tokens(yy):
         return pl.ds(pl.multiple_of(yy * tok, tok), tok)
 
-    load_rt = fetch(rt_in, rt)
-    load_vg = [fetch(vg.at[tokens(yy)], vg_v.at[i]) for i, yy in enumerate((y, up, across, down))]
-    load_vgx = fetch(vg.at[tokens(y)], vgx.at[0, 0])
-    load_act = [fetch(act.at[:, pl.ds(i * part, part)], actr.at[0, i]) for i in range(CHUNKS)]
-    share = d // 4
-    load_err = [fetch(err.at[pl.ds(i * share, share)], err_v.at[pl.ds(i * share, share)]) for i in range(4)]
-    load_w = fetch(w.at[c], wbuf.at[:, :, :, 0])
-
     barrier = pltpu.get_barrier_semaphore()
     everyone = (
         [device(z, x, cc, y) for cc in cores]
@@ -191,18 +183,23 @@
     )
     for peer in everyone:
         pl.semaphore_signal(barrier, inc=1, device_id=peer, device_id_type=MESH)
+
+    load_rt = fetch(rt_in, rt)
+    load_vg = [fetch(vg.at[tokens(yy)], vg_v.at[i]) for i, yy in enumerate((y, up, across, down))]
+    share = d // 4
+    load_err = [fetch(err.at[pl.ds(i * share, share)], err_v.at[pl.ds(i * share, share)]) for i in range(4)]
     pl.semaphore_wait(barrier, len(everyone))
 
     from_down, from_up, from_across = {}, {}, {}
+
+    def cols(i):
+        return pl.ds(i * part, part)
 
     def direct(*numbers):
         for i in numbers:
             j = (i + half) % CHUNKS
-            for piece in (i, j):
-                if piece in load_act:
-                    load_act.pop(piece).wait()
-            from_down[i] = send(actr.at[0, i], actr.at[3, i], device(z, x, c, up))
-            from_up[j] = send(actr.at[0, j], actr.at[1, j], device(z, x, c, down))
+            from_down[i] = send(act.at[:, cols(i)], actr.at[3, i], device(z, x, c, up))
+            from_up[j] = send(act.at[:, cols(j)], actr.at[1, j], device(z, x, c, down))
 
     def forward(*numbers):
         for i in numbers:
@@ -212,15 +209,6 @@
             from_up[j].wait_recv()
             from_across[j] = send(actr.at[1, j], actr.at[2, j], device(z, x, c, down))
 
-    load_act = dict(enumerate(load_act))
-
-    load_rt.wait()
-    rt3 = rows3(rt[...])
-    for load in load_vg:
-        load.wait()
-    for dy in range(ny):
-        uout[dy] = fold3(mm(rt3, vg_v[dy], NT))
-    recv_u = [send(uout.at[dy], uin.at[dy - 1], device(z, x, c, yy)) for dy, yy in y_peers]
 
     recv_vg = [send(vg.at[tokens(up)], vgx.at[0, 3], device(z, x, c, up))]
     recv_vg.append(send(vg.at[tokens(down)], vgx.at[0, 1], device(z, x, c, down)))
@@ -231,6 +219,20 @@
         for h in range(2)
     ]
     direct(0)
+    load_act = {
+        i: fetch(act.at[:, cols(i)], actr.at[0, i]) for j in range(half) for i in (j, j + half)
+    }
+    load_vgx = fetch(vg.at[tokens(y)], vgx.at[0, 0])
+    load_w = fetch(w.at[c], wbuf.at[:, :, :, 0])
+
+    load_rt.wait()
+    rt3 = rows3(rt[...])
+    for load in load_vg:
+        load.wait()
+    for dy in range(ny):
+        uout[dy] = fold3(mm(rt3, vg_v[dy], NT))
+    recv_u = [send(uout.at[dy], uin.at[dy - 1], device(z, x, c, yy)) for dy, yy in y_peers]
+
     own_w = w.at[c, x, z]
     w_from_down = send(own_w, wbuf.at[x, z, :, 3], device(z, x, c, up))
     w_from_up = send(own_w, wbuf.at[x, z, :, 1], device(z, x, c, down))
@@ -323,7 +325,6 @@
     ut3 = rows3(ut)
     for load in load_act.values():
         load.wait()
-    load_act = {}
 
     def own_act(p):
         n = wide // part
@@ -363,6 +364,7 @@
     w_halves = [send(wbuf.at[x, z, 0, 3], wbuf.at[x, z, 0, 2], device(z, x, c, up))]
     w_from_up.wait_recv()
     w_halves.append(send(wbuf.at[x, z, 1, 1], wbuf.at[x, z, 1, 2], device(z, x, c, down)))
+    direct(4)
     settle(recv_u + recv_core)
     recv_rs = recv
     wait_all(recv)
@@ -372,7 +374,7 @@
     ysum[y] = total
     own = ysum.at[y]
     recv = [send(own, own, device(z, x, c, yy)) for _, yy in y_peers]
-    direct(*range(4, 12))
+    direct(*range(5, 12))
     wait_all(w_halves)
     weights_first()
     weights_second(0)

time: 97 us -> 96.8 us (level)
  no operation moved by 1% of the time
where the time goes in v13:
time: 96.8 us; the launch traced here: 96.1 us
  Pallas kernels  95.3 us (98%)
    pallas_call x1, Pallas kernels, body(): pl.pallas_call(functools.partial(comm_kernel, geom), out_shape=tuple((plt...  90.9 us
    pallas_call x1, Pallas kernels, body(): pl.pallas_call(error_kernel, out_shape=tuple((jax.ShapeDtypeStruct(*shape...  4.4 us

profile of v13, /device:TPU:1, one launch (start us, length us, event | category | flops | bytes accessed | tf_op | source)
XLA Modules:
  0.0 96.1 jit_solution(16529016706070615058)
XLA Ops:
  0.6 90.9 %shard_map.84 = (f32[8192,256]{1,0:T(8,128)S(1)}, f32[32,8192]{1,0:T(8,128)S(1)}, f32[32,256]{1,0:T(8,128)S(1)}, bf16[128,8192]{1,0:T(8,128)(2,1)S(1)}) custom-call(bf16[128,8192]{1,0:T(8,128)(2,1)} %act.1, bf16[512,256]{1,0:T(8,128)(2,1)} %vg.1, bf16[2,4,4,2,128,256]{5,4,3,2,1,0:T(8,128)(2,1)} %bitcast.7, f32[8192,256]{1,0:T(8,128)} %bitcast.6, ...), custom_call_target="tpu_custom_call" | custom-call | tf_op jit(solution)/shard_map/pallas_call | solution.py:568
  91.5 4.4 %shard_map.85 = (f32[8192,256]{1,0:T(8,128)}, f32[32,8192]{1,0:T(8,128)}, f32[32,256]{1,0:T(8,128)}, bf16[128,8192]{1,0:T(8,128)(2,1)}) custom-call(f32[8192,256]{1,0:T(8,128)S(1)} %get-tuple-element.12.merged, f32[32,8192]{1,0:T(8,128)S(1)} %get-tuple-element.13.left, f32[32,256]{1,0:T(8,128)S(1)} %get-tuple-element.14.right, ...), custom_call_target="tpu_custom_call" | custom-call | tf_op jit(solution)/shard_map/pallas_call | solution.py:604

commit v14 on v13

--- a/solution.py
+++ b/solution.py
@@ -146,15 +146,34 @@
     sent, settled = [], []
     counter = [0, 0]
 
-    def send(src, dst, to):
+    def describe(src, dst, to):
         i = counter[0]
         counter[0] += 1
         copy = pltpu.make_async_remote_copy(
             src_ref=src, dst_ref=dst, send_sem=send_sem.at[i], recv_sem=recv_sem.at[i], device_id=to, device_id_type=MESH
         )
-        copy.start()
         sent.append(copy)
         return copy
+
+    def send(src, dst, to):
+        copy = describe(src, dst, to)
+        copy.start()
+        return copy
+
+    def send_both(one, other):
+        one, other = describe(*one), describe(*other)
+
+        @pl.when(c == 0)
+        def _():
+            one.start()
+            other.start()
+
+        @pl.when(c != 0)
+        def _():
+            other.start()
+            one.start()
+
+        return one, other
 
     def fetch(src, dst):
         i = counter[1]
@@ -198,16 +217,20 @@
     def direct(*numbers):
         for i in numbers:
             j = (i + half) % CHUNKS
-            from_down[i] = send(act.at[:, cols(i)], actr.at[3, i], device(z, x, c, up))
-            from_up[j] = send(act.at[:, cols(j)], actr.at[1, j], device(z, x, c, down))
+            from_down[i], from_up[j] = send_both(
+                (act.at[:, cols(i)], actr.at[3, i], device(z, x, c, up)),
+                (act.at[:, cols(j)], actr.at[1, j], device(z, x, c, down)),
+            )
 
     def forward(*numbers):
         for i in numbers:
+            j = i + half
             from_down[i].wait_recv()
-            from_across[i] = send(actr.at[3, i], actr.at[2, i], device(z, x, c, up))
-            j = i + half
             from_up[j].wait_recv()
-            from_across[j] = send(actr.at[1, j], actr.at[2, j], device(z, x, c, down))
+            from_across[i], from_across[j] = send_both(
+                (actr.at[3, i], actr.at[2, i], device(z, x, c, up)),
+                (actr.at[1, j], actr.at[2, j], device(z, x, c, down)),
+            )
 
 
     recv_vg = [send(vg.at[tokens(up)], vgx.at[0, 3], device(z, x, c, up))]
@@ -234,8 +257,9 @@
     recv_u = [send(uout.at[dy], uin.at[dy - 1], device(z, x, c, yy)) for dy, yy in y_peers]
 
     own_w = w.at[c, x, z]
-    w_from_down = send(own_w, wbuf.at[x, z, :, 3], device(z, x, c, up))
-    w_from_up = send(own_w, wbuf.at[x, z, :, 1], device(z, x, c, down))
+    w_from_down, w_from_up = send_both(
+        (own_w, wbuf.at[x, z, :, 3], device(z, x, c, up)), (own_w, wbuf.at[x, z, :, 1], device(z, x, c, down))
+    )
     direct(1, 2)
 
     def place(h, a, b):
@@ -262,8 +286,9 @@
         for h in range(2):
             (first, second), _ = half_here[h]
             own = piece(h, first, second)
-            for way in (1, -1):
-                stage_one[h, way] = send(own, own, neighbour(h, 0, way))
+            stage_one[h, 1], stage_one[h, -1] = send_both(
+                (own, own, neighbour(h, 0, 1)), (own, own, neighbour(h, 0, -1))
+            )
 
     def weights_across():
         for h in range(2):
@@ -284,8 +309,10 @@
             elif i == 3:
                 stage_one_across[h].wait_recv()
                 first = shifted(first, 2, n)
-            for way in (1, -1):
-                stage_two[h, i, way] = send(piece(h, first, second), piece(h, first, second), neighbour(h, 1, way))
+            here = piece(h, first, second)
+            stage_two[h, i, 1], stage_two[h, i, -1] = send_both(
+                (here, here, neighbour(h, 1, 1)), (here, here, neighbour(h, 1, -1))
+            )
 
     def weights_second_across(i):
         for h in range(2):

time: 96.8 us -> 96.8 us (level)
  no operation moved by 1% of the time
where the time goes in v14:
time: 96.8 us; the launch traced here: 96.2 us
  Pallas kernels  95.4 us (99%)
    pallas_call x1, Pallas kernels, body(): pl.pallas_call(functools.partial(comm_kernel, geom), out_shape=tuple((plt...  91 us
    pallas_call x1, Pallas kernels, body(): pl.pallas_call(error_kernel, out_shape=tuple((jax.ShapeDtypeStruct(*shape...  4.4 us

profile of v14, /device:TPU:1, one launch (start us, length us, event | category | flops | bytes accessed | tf_op | source)
XLA Modules:
  0.0 96.2 jit_solution(3969578025556546650)
XLA Ops:
  0.6 91.0 %shard_map.84 = (f32[8192,256]{1,0:T(8,128)S(1)}, f32[32,8192]{1,0:T(8,128)S(1)}, f32[32,256]{1,0:T(8,128)S(1)}, bf16[128,8192]{1,0:T(8,128)(2,1)S(1)}) custom-call(bf16[128,8192]{1,0:T(8,128)(2,1)} %act.1, bf16[512,256]{1,0:T(8,128)(2,1)} %vg.1, bf16[2,4,4,2,128,256]{5,4,3,2,1,0:T(8,128)(2,1)} %bitcast.7, f32[8192,256]{1,0:T(8,128)} %bitcast.6, ...), custom_call_target="tpu_custom_call" | custom-call | tf_op jit(solution)/shard_map/pallas_call | solution.py:595
  91.6 4.4 %shard_map.85 = (f32[8192,256]{1,0:T(8,128)}, f32[32,8192]{1,0:T(8,128)}, f32[32,256]{1,0:T(8,128)}, bf16[128,8192]{1,0:T(8,128)(2,1)}) custom-call(f32[8192,256]{1,0:T(8,128)S(1)} %get-tuple-element.12.merged, f32[32,8192]{1,0:T(8,128)S(1)} %get-tuple-element.13.left, f32[32,256]{1,0:T(8,128)S(1)} %get-tuple-element.14.right, ...), custom_call_target="tpu_custom_call" | custom-call | tf_op jit(solution)/shard_map/pallas_call | solution.py:631

commit v15 on v14

--- a/solution.py
+++ b/solution.py
@@ -443,6 +443,7 @@
         0, pieces, products, (jnp.zeros((3 * r, 3 * r), F32), jnp.zeros((2 * r, tok), F32))
     )
     aout[...] = fold2(by_act)
+    early = list(sent)
     recv_a = [send(aout, ain.at[dy - 1], device(z, x, c, yy)) for dy, yy in y_peers]
     direct(*range(12, CHUNKS))
     forward(*range(half))
@@ -472,21 +473,28 @@
     weights = weights - times(again, weights)
     scale = math.sqrt(float(d))
 
-    def apply_second(p, carry):
-        block = q1[p]
-        block = block - times(again, block)
-        left_out[:, columns(p)] = block * scale
-        return carry
-
-    lax.fori_loop(0, pieces, apply_second, 0)
-
-
     wait_all(recv_a)
     for slot in range(ny):
         total = total + fold3(mm(rows3(aout[...] if slot == 0 else ain[ny - slot - 1]), vg_v[slot]))
     zsum[0] = total
     recv = [send(zsum.at[0], zsum.at[dc], device(z, x, cc, y)) for dc, cc in enumerate(cores, 1)]
     weights_second_across(3)
+
+    def apply_second(p, carry):
+        block = q1[p]
+        block = block - times(again, block)
+        left_out[:, columns(p)] = block * scale
+        return carry
+
+    lax.fori_loop(0, pieces, apply_second, 0)
+    settle([copy for copy in early if id(copy) not in settled])
+    wait_all(recv)
+    for dc in range(1, nc):
+        total = total + zsum[dc]
+    tz[mine] = total
+    own = tz.at[mine]
+    recv = [send(own, own, device(zz, xx, c, y)) for xx, zz in plane]
+
 
     for i in range(4):
         for h in range(2):
@@ -509,13 +517,6 @@
     lax.fori_loop(0, per, input_grad, 0)
     share_of = gi.at[:, pl.ds(pl.multiple_of(c * per * BLK, BLK), per * BLK)]
     sent_out = [send(outs.at[nc - 1 - dc], share_of, device(z, x, cc, y)) for dc, cc in enumerate(cores, 1)]
-
-    wait_all(recv)
-    for dc in range(1, nc):
-        total = total + zsum[dc]
-    tz[mine] = total
-    own = tz.at[mine]
-    recv = [send(own, own, device(zz, xx, c, y)) for xx, zz in plane]
 
     for i in range(CHUNKS):
         if i >= half:

time: 96.8 us -> 96.8 us (level)
  no operation moved by 1% of the time
where the time goes in v15:
time: 96.8 us; the launch traced here: 96.2 us
  Pallas kernels  95.4 us (99%)
    pallas_call x1, Pallas kernels, body(): pl.pallas_call(functools.partial(comm_kernel, geom), out_shape=tuple((plt...  91 us
    pallas_call x1, Pallas kernels, body(): pl.pallas_call(error_kernel, out_shape=tuple((jax.ShapeDtypeStruct(*shape...  4.4 us

profile of v15, /device:TPU:1, one launch (start us, length us, event | category | flops | bytes accessed | tf_op | source)
XLA Modules:
  0.0 96.2 jit_solution(3012859741546728005)
XLA Ops:
  0.6 91.0 %shard_map.84 = (f32[8192,256]{1,0:T(8,128)S(1)}, f32[32,8192]{1,0:T(8,128)S(1)}, f32[32,256]{1,0:T(8,128)S(1)}, bf16[128,8192]{1,0:T(8,128)(2,1)S(1)}) custom-call(bf16[128,8192]{1,0:T(8,128)(2,1)} %act.1, bf16[512,256]{1,0:T(8,128)(2,1)} %vg.1, bf16[2,4,4,2,128,256]{5,4,3,2,1,0:T(8,128)(2,1)} %bitcast.7, f32[8192,256]{1,0:T(8,128)} %bitcast.6, ...), custom_call_target="tpu_custom_call" | custom-call | tf_op jit(solution)/shard_map/pallas_call | solution.py:596
  91.6 4.4 %shard_map.85 = (f32[8192,256]{1,0:T(8,128)}, f32[32,8192]{1,0:T(8,128)}, f32[32,256]{1,0:T(8,128)}, bf16[128,8192]{1,0:T(8,128)(2,1)}) custom-call(f32[8192,256]{1,0:T(8,128)S(1)} %get-tuple-element.12.merged, f32[32,8192]{1,0:T(8,128)S(1)} %get-tuple-element.13.left, f32[32,256]{1,0:T(8,128)S(1)} %get-tuple-element.14.right, ...), custom_call_target="tpu_custom_call" | custom-call | tf_op jit(solution)/shard_map/pallas_call | solution.py:632

commit v16 on v15

--- a/solution.py
+++ b/solution.py
@@ -196,42 +196,55 @@
 
     barrier = pltpu.get_barrier_semaphore()
     everyone = (
-        [device(z, x, cc, y) for cc in cores]
+        [device(z, x, c, yy) for _, yy in y_peers]
+        + [device(z, x, cc, y) for cc in cores]
         + [device(zz, xx, c, y) for xx, zz in plane]
-        + [device(z, x, c, yy) for _, yy in y_peers]
     )
     for peer in everyone:
         pl.semaphore_signal(barrier, inc=1, device_id=peer, device_id_type=MESH)
 
+    def cols(i):
+        return pl.ds(i * part, part)
+
     load_rt = fetch(rt_in, rt)
     load_vg = [fetch(vg.at[tokens(yy)], vg_v.at[i]) for i, yy in enumerate((y, up, across, down))]
     share = d // 4
+    load_act = {i: fetch(act.at[:, cols(i)], actr.at[0, i]) for j in range(half) for i in (j, j + half)}
     load_err = [fetch(err.at[pl.ds(i * share, share)], err_v.at[pl.ds(i * share, share)]) for i in range(4)]
     pl.semaphore_wait(barrier, len(everyone))
 
     from_down, from_up, from_across = {}, {}, {}
 
-    def cols(i):
-        return pl.ds(i * part, part)
-
-    def direct(*numbers):
-        for i in numbers:
+    def direct(*units):
+        for u in units:
+            i = 2 * u
             j = (i + half) % CHUNKS
+            for n in (i, i + 1, j, j + 1):
+                if n in load_act:
+                    load_act.pop(n).wait()
             from_down[i], from_up[j] = send_both(
-                (act.at[:, cols(i)], actr.at[3, i], device(z, x, c, up)),
-                (act.at[:, cols(j)], actr.at[1, j], device(z, x, c, down)),
+                (actr.at[0, i : i + 2], actr.at[3, i : i + 2], device(z, x, c, up)),
+                (actr.at[0, j : j + 2], actr.at[1, j : j + 2], device(z, x, c, down)),
             )
 
-    def forward(*numbers):
-        for i in numbers:
+    arrived = set()
+
+    def arrive(copies, i):
+        if (id(copies), i) not in arrived:
+            arrived.add((id(copies), i))
+            copies[i].wait_recv()
+
+    passed_on = [(0, 2), (2, 2), (4, 2), (6, 1), (7, 1)]
+
+    def forward():
+        for i, n in passed_on:
             j = i + half
-            from_down[i].wait_recv()
-            from_up[j].wait_recv()
+            arrive(from_down, i // 2 * 2)
+            arrive(from_up, j // 2 * 2)
             from_across[i], from_across[j] = send_both(
-                (actr.at[3, i], actr.at[2, i], device(z, x, c, up)),
-                (actr.at[1, j], actr.at[2, j], device(z, x, c, down)),
+                (actr.at[3, i : i + n], actr.at[2, i : i + n], device(z, x, c, up)),
+                (actr.at[1, j : j + n], actr.at[2, j : j + n], device(z, x, c, down)),
             )
-
 
     recv_vg = [send(vg.at[tokens(up)], vgx.at[0, 3], device(z, x, c, up))]
     recv_vg.append(send(vg.at[tokens(down)], vgx.at[0, 1], device(z, x, c, down)))
@@ -242,9 +255,6 @@
         for h in range(2)
     ]
     direct(0)
-    load_act = {
-        i: fetch(act.at[:, cols(i)], actr.at[0, i]) for j in range(half) for i in (j, j + half)
-    }
     load_vgx = fetch(vg.at[tokens(y)], vgx.at[0, 0])
     load_w = fetch(w.at[c], wbuf.at[:, :, :, 0])
 
@@ -260,7 +270,7 @@
     w_from_down, w_from_up = send_both(
         (own_w, wbuf.at[x, z, :, 3], device(z, x, c, up)), (own_w, wbuf.at[x, z, :, 1], device(z, x, c, down))
     )
-    direct(1, 2)
+    direct(1)
 
     def place(h, a, b):
         return (a, b) if h == 0 else (b, a)
@@ -352,6 +362,7 @@
     ut3 = rows3(ut)
     for load in load_act.values():
         load.wait()
+    load_act.clear()
 
     def own_act(p):
         n = wide // part
@@ -376,7 +387,6 @@
     act_left(c)
 
     recv_core = recv
-    direct(3)
     load_vgx.wait()
     for h in range(2):
         vg_passing[h].wait_recv()
@@ -391,7 +401,6 @@
     w_halves = [send(wbuf.at[x, z, 0, 3], wbuf.at[x, z, 0, 2], device(z, x, c, up))]
     w_from_up.wait_recv()
     w_halves.append(send(wbuf.at[x, z, 1, 1], wbuf.at[x, z, 1, 2], device(z, x, c, down)))
-    direct(4)
     settle(recv_u + recv_core)
     recv_rs = recv
     wait_all(recv)
@@ -401,7 +410,7 @@
     ysum[y] = total
     own = ysum.at[y]
     recv = [send(own, own, device(z, x, c, yy)) for _, yy in y_peers]
-    direct(*range(5, 12))
+    direct(2, 3, 4, 5)
     wait_all(w_halves)
     weights_first()
     weights_second(0)
@@ -445,8 +454,8 @@
     aout[...] = fold2(by_act)
     early = list(sent)
     recv_a = [send(aout, ain.at[dy - 1], device(z, x, c, yy)) for dy, yy in y_peers]
-    direct(*range(12, CHUNKS))
-    forward(*range(half))
+    direct(6, 7)
+    forward()
     weights_second_across(1)
     weights_second_across(2)
 
@@ -518,33 +527,31 @@
     share_of = gi.at[:, pl.ds(pl.multiple_of(c * per * BLK, BLK), per * BLK)]
     sent_out = [send(outs.at[nc - 1 - dc], share_of, device(z, x, cc, y)) for dc, cc in enumerate(cores, 1)]
 
-    for i in range(CHUNKS):
-        if i >= half:
-            from_down[i].wait_recv()
-        else:
-            from_up[i].wait_recv()
+    for i in range(0, CHUNKS, 2):
+        arrive(from_down, i)
+        arrive(from_up, i)
     cotangent = vg_v[...].reshape(ny * tok, BLK).astype(F32).T.astype(BF16)
 
-    def merge(j):
-        from_across[j].wait_recv()
-        at = pl.ds(j * part, part)
-        merged[at, :] = err_v[at, :] + mm(cotangent, actr[:, j].reshape(ny * tok, part)).T
-
-    for i in range(half - 2):
-        merge(i)
-        merge(i + half)
+    def merge(i, n):
+        for j0 in (i, i + half):
+            from_across[j0].wait_recv()
+            for j in range(j0, j0 + n):
+                at = pl.ds(j * part, part)
+                merged[at, :] = err_v[at, :] + mm(cotangent, actr[:, j].reshape(ny * tok, part)).T
+
+    for i, n in passed_on[:-2]:
+        merge(i, n)
 
     wait_all(recv)
     total = tz[0]
     for i in range(1, per):
         total = total + tz[i]
     r_out[...] = times(weights, total) / float(nb)
-    last = [id(from_across[i + h]) for i in range(half - 2, half) for h in (0, half)]
+    last = [id(from_across[i + h]) for i, _ in passed_on[-2:] for h in (0, half)]
     settle([copy for copy in sent if id(copy) not in settled + last])
 
-    for i in range(half - 2, half):
-        merge(i)
-        merge(i + half)
+    for i, n in passed_on[-2:]:
+        merge(i, n)
 
     wait_all(sent_out)
     settle([copy for copy in sent if id(copy) not in settled])
@@ -584,7 +591,7 @@
         per = nx * nz
         wide = min(WIDE, per * BLK)
         assert d == nb * BLK and kv == BLK and per * BLK % wide == 0
-        sends = 3 * (ny - 1) + 6 + 4 + 3 * CHUNKS + 30 + 3 * (per - 1) + 5 * (nc - 1)
+        sends = 3 * (ny - 1) + 6 + 4 + CHUNKS + 10 + 30 + 3 * (per - 1) + 5 * (nc - 1)
         pieces = w.reshape(nc, nx, nz, 2, BLK // 2, kv)
         inputs = [
             pltpu.with_memory_space_constraint(a, pltpu.HBM) for a in (act, vg, pieces, err[0], right_prev.T)

time: 96.8 us -> 99.3 us (1.026)
  Pallas kernels: 95.4 us -> 98.6 us
    pallas_call x1, Pallas kernels: 91 us -> 94.2 us  [body(): pl.pallas_call(functools.partial(comm_kernel, geom), out_shape=tuple((plt...]
where the time goes in v16:
time: 99.3 us; the launch traced here: 99.2 us
  Pallas kernels  98.6 us (99%)
    pallas_call x1, Pallas kernels, body(): pl.pallas_call(functools.partial(comm_kernel, geom), out_shape=tuple((plt...  94.2 us
    pallas_call x1, Pallas kernels, body(): pl.pallas_call(error_kernel, out_shape=tuple((jax.ShapeDtypeStruct(*shape...  4.4 us

profile of v16, /device:TPU:1, one launch (start us, length us, event | category | flops | bytes accessed | tf_op | source)
XLA Modules:
  0.0 99.2 jit_solution(14526647870001472041)
XLA Ops:
  0.6 94.2 %shard_map.84 = (f32[8192,256]{1,0:T(8,128)S(1)}, f32[32,8192]{1,0:T(8,128)S(1)}, f32[32,256]{1,0:T(8,128)S(1)}, bf16[128,8192]{1,0:T(8,128)(2,1)S(1)}) custom-call(bf16[128,8192]{1,0:T(8,128)(2,1)} %act.1, bf16[512,256]{1,0:T(8,128)(2,1)} %vg.1, bf16[2,4,4,2,128,256]{5,4,3,2,1,0:T(8,128)(2,1)} %bitcast.7, f32[8192,256]{1,0:T(8,128)} %bitcast.6, ...), custom_call_target="tpu_custom_call" | custom-call | tf_op jit(solution)/shard_map/pallas_call | solution.py:603
  94.8 4.4 %shard_map.85 = (f32[8192,256]{1,0:T(8,128)}, f32[32,8192]{1,0:T(8,128)}, f32[32,256]{1,0:T(8,128)}, bf16[128,8192]{1,0:T(8,128)(2,1)}) custom-call(f32[8192,256]{1,0:T(8,128)S(1)} %get-tuple-element.12.merged, f32[32,8192]{1,0:T(8,128)S(1)} %get-tuple-element.13.left, f32[32,256]{1,0:T(8,128)S(1)} %get-tuple-element.14.right, ...), custom_call_target="tpu_custom_call" | custom-call | tf_op jit(solution)/shard_map/pallas_call | solution.py:639

commit v17 on v15

--- a/solution.py
+++ b/solution.py
@@ -196,9 +196,9 @@
 
     barrier = pltpu.get_barrier_semaphore()
     everyone = (
-        [device(z, x, cc, y) for cc in cores]
+        [device(z, x, c, yy) for _, yy in y_peers]
+        + [device(z, x, cc, y) for cc in cores]
         + [device(zz, xx, c, y) for xx, zz in plane]
-        + [device(z, x, c, yy) for _, yy in y_peers]
     )
     for peer in everyone:
         pl.semaphore_signal(barrier, inc=1, device_id=peer, device_id_type=MESH)
@@ -391,7 +391,7 @@
     w_halves = [send(wbuf.at[x, z, 0, 3], wbuf.at[x, z, 0, 2], device(z, x, c, up))]
     w_from_up.wait_recv()
     w_halves.append(send(wbuf.at[x, z, 1, 1], wbuf.at[x, z, 1, 2], device(z, x, c, down)))
-    direct(4)
+    direct(4, 5)
     settle(recv_u + recv_core)
     recv_rs = recv
     wait_all(recv)
@@ -401,7 +401,7 @@
     ysum[y] = total
     own = ysum.at[y]
     recv = [send(own, own, device(z, x, c, yy)) for _, yy in y_peers]
-    direct(*range(5, 12))
+    direct(*range(6, 12))
     wait_all(w_halves)
     weights_first()
     weights_second(0)

time: 96.8 us -> 96.7 us (level)
  no operation moved by 1% of the time
where the time goes in v17:
time: 96.7 us; the launch traced here: 96.1 us
  Pallas kernels  95.3 us (99%)
    pallas_call x1, Pallas kernels, body(): pl.pallas_call(functools.partial(comm_kernel, geom), out_shape=tuple((plt...  90.9 us
    pallas_call x1, Pallas kernels, body(): pl.pallas_call(error_kernel, out_shape=tuple((jax.ShapeDtypeStruct(*shape...  4.4 us

profile of v17, /device:TPU:1, one launch (start us, length us, event | category | flops | bytes accessed | tf_op | source)
XLA Modules:
  0.0 96.1 jit_solution(12903175743164206614)
XLA Ops:
  0.6 90.9 %shard_map.84 = (f32[8192,256]{1,0:T(8,128)S(1)}, f32[32,8192]{1,0:T(8,128)S(1)}, f32[32,256]{1,0:T(8,128)S(1)}, bf16[128,8192]{1,0:T(8,128)(2,1)S(1)}) custom-call(bf16[128,8192]{1,0:T(8,128)(2,1)} %act.1, bf16[512,256]{1,0:T(8,128)(2,1)} %vg.1, bf16[2,4,4,2,128,256]{5,4,3,2,1,0:T(8,128)(2,1)} %bitcast.7, f32[8192,256]{1,0:T(8,128)} %bitcast.6, ...), custom_call_target="tpu_custom_call" | custom-call | tf_op jit(solution)/shard_map/pallas_call | solution.py:596
  91.5 4.4 %shard_map.85 = (f32[8192,256]{1,0:T(8,128)}, f32[32,8192]{1,0:T(8,128)}, f32[32,256]{1,0:T(8,128)}, bf16[128,8192]{1,0:T(8,128)(2,1)}) custom-call(f32[8192,256]{1,0:T(8,128)S(1)} %get-tuple-element.12.merged, f32[32,8192]{1,0:T(8,128)S(1)} %get-tuple-element.13.left, f32[32,256]{1,0:T(8,128)S(1)} %get-tuple-element.14.right, ...), custom_call_target="tpu_custom_call" | custom-call | tf_op jit(solution)/shard_map/pallas_call | solution.py:632

commit v18 on v17

--- a/solution.py
+++ b/solution.py
@@ -222,16 +222,19 @@
                 (act.at[:, cols(j)], actr.at[1, j], device(z, x, c, down)),
             )
 
-    def forward(*numbers):
-        for i in numbers:
+    passed_on = [(i, 0, part) for i in range(half - 1)]
+    passed_on += [(half - 1, 0, part // 2), (half - 1, part // 2, part)]
+
+    def forward():
+        for i, lo, hi in passed_on:
             j = i + half
-            from_down[i].wait_recv()
-            from_up[j].wait_recv()
-            from_across[i], from_across[j] = send_both(
-                (actr.at[3, i], actr.at[2, i], device(z, x, c, up)),
-                (actr.at[1, j], actr.at[2, j], device(z, x, c, down)),
+            if lo == 0:
+                from_down[i].wait_recv()
+                from_up[j].wait_recv()
+            from_across[i, lo], from_across[j, lo] = send_both(
+                (actr.at[3, i, :, lo:hi], actr.at[2, i, :, lo:hi], device(z, x, c, up)),
+                (actr.at[1, j, :, lo:hi], actr.at[2, j, :, lo:hi], device(z, x, c, down)),
             )
-
 
     recv_vg = [send(vg.at[tokens(up)], vgx.at[0, 3], device(z, x, c, up))]
     recv_vg.append(send(vg.at[tokens(down)], vgx.at[0, 1], device(z, x, c, down)))
@@ -446,7 +449,7 @@
     early = list(sent)
     recv_a = [send(aout, ain.at[dy - 1], device(z, x, c, yy)) for dy, yy in y_peers]
     direct(*range(12, CHUNKS))
-    forward(*range(half))
+    forward()
     weights_second_across(1)
     weights_second_across(2)
 
@@ -525,26 +528,26 @@
             from_up[i].wait_recv()
     cotangent = vg_v[...].reshape(ny * tok, BLK).astype(F32).T.astype(BF16)
 
-    def merge(j):
-        from_across[j].wait_recv()
-        at = pl.ds(j * part, part)
-        merged[at, :] = err_v[at, :] + mm(cotangent, actr[:, j].reshape(ny * tok, part)).T
-
-    for i in range(half - 2):
-        merge(i)
-        merge(i + half)
+    def merge(i, lo, hi):
+        for j in (i, i + half):
+            from_across[j, lo].wait_recv()
+            at = pl.ds(j * part + lo, hi - lo)
+            block = mm(cotangent, actr[:, j, :, lo:hi].reshape(ny * tok, hi - lo))
+            merged[at, :] = err_v[at, :] + block.T
+
+    for bounds in passed_on[:-3]:
+        merge(*bounds)
 
     wait_all(recv)
     total = tz[0]
     for i in range(1, per):
         total = total + tz[i]
     r_out[...] = times(weights, total) / float(nb)
-    last = [id(from_across[i + h]) for i in range(half - 2, half) for h in (0, half)]
+    last = [id(from_across[i + h, lo]) for i, lo, _ in passed_on[-3:] for h in (0, half)]
     settle([copy for copy in sent if id(copy) not in settled + last])
 
-    for i in range(half - 2, half):
-        merge(i)
-        merge(i + half)
+    for bounds in passed_on[-3:]:
+        merge(*bounds)
 
     wait_all(sent_out)
     settle([copy for copy in sent if id(copy) not in settled])
@@ -555,10 +558,10 @@
     d = merged.shape[0]
     pieces = error.shape[0]
     rows = d // pieces
-    copies = [
-        pltpu.make_async_copy(a, b, sem.at[pieces + i])
-        for i, (a, b) in enumerate([(gi, gi_out), (left, left_out), (right, right_out)])
-    ]
+    pairs = [(gi.at[i : i + 16], gi_out.at[i : i + 16]) for i in range(0, gi.shape[0], 16)]
+    pairs += [(left.at[i : i + 8], left_out.at[i : i + 8]) for i in range(0, left.shape[0], 8)]
+    pairs.append((right, right_out))
+    copies = [pltpu.make_async_copy(a, b, sem.at[pieces + i]) for i, (a, b) in enumerate(pairs)]
     for copy in copies:
         copy.start()
     hi, lo = split2(right[...] / math.sqrt(float(d)))
@@ -584,7 +587,7 @@
         per = nx * nz
         wide = min(WIDE, per * BLK)
         assert d == nb * BLK and kv == BLK and per * BLK % wide == 0
-        sends = 3 * (ny - 1) + 6 + 4 + 3 * CHUNKS + 30 + 3 * (per - 1) + 5 * (nc - 1)
+        sends = 3 * (ny - 1) + 6 + 4 + 3 * CHUNKS + 2 + 30 + 3 * (per - 1) + 5 * (nc - 1)
         pieces = w.reshape(nc, nx, nz, 2, BLK // 2, kv)
         inputs = [
             pltpu.with_memory_space_constraint(a, pltpu.HBM) for a in (act, vg, pieces, err[0], right_prev.T)
@@ -634,7 +637,7 @@
             out_shape=tuple(jax.ShapeDtypeStruct(*shape) for shape in results),
             in_specs=[vmem] * 4,
             out_specs=(anywhere,) * 4,
-            scratch_shapes=[pltpu.VMEM((pieces, d // pieces, kv), F32), pltpu.SemaphoreType.DMA((pieces + 3,))],
+            scratch_shapes=[pltpu.VMEM((pieces, d // pieces, kv), F32), pltpu.SemaphoreType.DMA((pieces + tok // 16 + r // 8 + 1,))],
             compiler_params=pltpu.CompilerParams(vmem_limit_bytes=24 * MIB),
         )(*made)
         return (grad_input, error_next[None], left.T, right.T)

time: 96.7 us -> 96.9 us (level)
  no operation moved by 1% of the time
where the time goes in v18:
time: 96.9 us; the launch traced here: 96 us
  Pallas kernels  95.2 us (98%)
    pallas_call x1, Pallas kernels, body(): pl.pallas_call(functools.partial(comm_kernel, geom), out_shape=tuple((plt...  90.7 us
    pallas_call x1, Pallas kernels, body(): pl.pallas_call(error_kernel, out_shape=tuple((jax.ShapeDtypeStruct(*shape...  4.49 us

profile of v18, /device:TPU:1, one launch (start us, length us, event | category | flops | bytes accessed | tf_op | source)
XLA Modules:
  0.0 96.0 jit_solution(1024133618567031884)
XLA Ops:
  0.6 90.7 %shard_map.84 = (f32[8192,256]{1,0:T(8,128)S(1)}, f32[32,8192]{1,0:T(8,128)S(1)}, f32[32,256]{1,0:T(8,128)S(1)}, bf16[128,8192]{1,0:T(8,128)(2,1)S(1)}) custom-call(bf16[128,8192]{1,0:T(8,128)(2,1)} %act.1, bf16[512,256]{1,0:T(8,128)(2,1)} %vg.1, bf16[2,4,4,2,128,256]{5,4,3,2,1,0:T(8,128)(2,1)} %bitcast.7, f32[8192,256]{1,0:T(8,128)} %bitcast.6, ...), custom_call_target="tpu_custom_call" | custom-call | tf_op jit(solution)/shard_map/pallas_call | solution.py:599
  91.4 4.5 %shard_map.85 = (f32[8192,256]{1,0:T(8,128)}, f32[32,8192]{1,0:T(8,128)}, f32[32,256]{1,0:T(8,128)}, bf16[128,8192]{1,0:T(8,128)(2,1)}) custom-call(f32[8192,256]{1,0:T(8,128)S(1)} %get-tuple-element.12.merged, f32[32,8192]{1,0:T(8,128)S(1)} %get-tuple-element.13.left, f32[32,256]{1,0:T(8,128)S(1)} %get-tuple-element.14.right, ...), custom_call_target="tpu_custom_call" | custom-call | tf_op jit(solution)/shard_map/pallas_call | solution.py:635

commit v19 on v17

--- a/solution.py
+++ b/solution.py
@@ -391,7 +391,7 @@
     w_halves = [send(wbuf.at[x, z, 0, 3], wbuf.at[x, z, 0, 2], device(z, x, c, up))]
     w_from_up.wait_recv()
     w_halves.append(send(wbuf.at[x, z, 1, 1], wbuf.at[x, z, 1, 2], device(z, x, c, down)))
-    direct(4, 5)
+    direct(4, 5, 6)
     settle(recv_u + recv_core)
     recv_rs = recv
     wait_all(recv)
@@ -401,7 +401,7 @@
     ysum[y] = total
     own = ysum.at[y]
     recv = [send(own, own, device(z, x, c, yy)) for _, yy in y_peers]
-    direct(*range(6, 12))
+    direct(*range(7, 12))
     wait_all(w_halves)
     weights_first()
     weights_second(0)

time: 96.7 us -> 98.1 us (1.014)
  Pallas kernels: 95.3 us -> 96.6 us
    pallas_call x1, Pallas kernels: 90.9 us -> 92.2 us  [body(): pl.pallas_call(functools.partial(comm_kernel, geom), out_shape=tuple((plt...]
where the time goes in v19:
time: 98.1 us; the launch traced here: 97.4 us
  Pallas kernels  96.6 us (98%)
    pallas_call x1, Pallas kernels, body(): pl.pallas_call(functools.partial(comm_kernel, geom), out_shape=tuple((plt...  92.2 us
    pallas_call x1, Pallas kernels, body(): pl.pallas_call(error_kernel, out_shape=tuple((jax.ShapeDtypeStruct(*shape...  4.4 us

profile of v19, /device:TPU:1, one launch (start us, length us, event | category | flops | bytes accessed | tf_op | source)
XLA Modules:
  0.0 97.4 jit_solution(2401221833328130311)
XLA Ops:
  0.6 92.2 %shard_map.84 = (f32[8192,256]{1,0:T(8,128)S(1)}, f32[32,8192]{1,0:T(8,128)S(1)}, f32[32,256]{1,0:T(8,128)S(1)}, bf16[128,8192]{1,0:T(8,128)(2,1)S(1)}) custom-call(bf16[128,8192]{1,0:T(8,128)(2,1)} %act.1, bf16[512,256]{1,0:T(8,128)(2,1)} %vg.1, bf16[2,4,4,2,128,256]{5,4,3,2,1,0:T(8,128)(2,1)} %bitcast.7, f32[8192,256]{1,0:T(8,128)} %bitcast.6, ...), custom_call_target="tpu_custom_call" | custom-call | tf_op jit(solution)/shard_map/pallas_call | solution.py:596
  92.9 4.4 %shard_map.85 = (f32[8192,256]{1,0:T(8,128)}, f32[32,8192]{1,0:T(8,128)}, f32[32,256]{1,0:T(8,128)}, bf16[128,8192]{1,0:T(8,128)(2,1)}) custom-call(f32[8192,256]{1,0:T(8,128)S(1)} %get-tuple-element.12.merged, f32[32,8192]{1,0:T(8,128)S(1)} %get-tuple-element.13.left, f32[32,256]{1,0:T(8,128)S(1)} %get-tuple-element.14.right, ...), custom_call_target="tpu_custom_call" | custom-call | tf_op jit(solution)/shard_map/pallas_call | solution.py:632
